TPU v7x, 32 devices: a whole 2x2x4 slice. The times are simulated.
32 devices in a mesh: wide: 8 (over z, y), narrow: 4 (over x, core).
Axes of the slice: x: 2, y: 2, z: 4, core: 2. Of those that a mesh axis runs over, the one named last changes fastest.
Arguments:
- block_input: bfloat16 [4096, 2048], P('wide'), may hold values from -6 to 6
- gain_attn: float32 [2048], replicated, may hold values from 0.5 to 1.5
- w_query: bfloat16 [2048, 2048], P('wide', 'narrow'), may hold values from -0.125 to 0.125
- w_key: bfloat16 [2048, 2048], P('wide', 'narrow'), may hold values from -0.125 to 0.125
- w_value: bfloat16 [2048, 4096], P('wide', 'narrow'), may hold values from -0.125 to 0.125
- w_gate_out: bfloat16 [2048, 4096], P('wide', 'narrow'), may hold values from -0.125 to 0.125
- w_decay: bfloat16 [2048, 16], P('wide', 'narrow'), may hold values from -0.0625 to 0.0625
- w_beta: bfloat16 [2048, 16], P('wide', 'narrow'), may hold values from -0.125 to 0.125
- conv_query: float32 [4, 2048], P(None, 'narrow'), may hold values from -3 to 3
- conv_key: float32 [4, 2048], P(None, 'narrow'), may hold values from -3 to 3
- conv_value: float32 [4, 4096], P(None, 'narrow'), may hold values from -3 to 3
- a_log: float32 [16], P('narrow'), may hold values from -1.5 to 1
- dt_bias: float32 [16], P('narrow'), may hold values from -6 to -1
- out_gain: float32 [256], replicated, may hold values from 0.5 to 1.5
- w_out: bfloat16 [2048, 4096], P('wide', 'narrow'), may hold values from -0.1875 to 0.1875
- gain_mlp: float32 [2048], replicated, may hold values from 0.5 to 1.5
- w_gate: bfloat16 [2048, 5504], P(None, 'wide'), may hold values from -0.125 to 0.125
- w_up: bfloat16 [2048, 5504], P(None, 'wide'), may hold values from -0.125 to 0.125
- w_down: bfloat16 [5504, 2048], P('wide'), may hold values from -0.109375 to 0.109375
- doc_lengths: int32 [9], replicated, may hold values from 1 to 3584, as said below
- cotangent: bfloat16 [4096, 2048], P(('wide', 'narrow')), may hold values from -6 to 6
Outputs:
- output: bfloat16 [4096, 2048], P(('wide', 'narrow'))
- grad_input: float32 [4096, 2048], P(('wide', 'narrow'))
- grad_gain_attn: float32 [2048], replicated
- grad_w_query: float32 [2048, 2048], P('wide', 'narrow')
- grad_w_key: float32 [2048, 2048], P('wide', 'narrow')
- grad_w_value: float32 [2048, 4096], P('wide', 'narrow')
- grad_w_gate_out: float32 [2048, 4096], P('wide', 'narrow')
- grad_w_decay: float32 [2048, 16], P('wide', 'narrow')
- grad_w_beta: float32 [2048, 16], P('wide', 'narrow')
- grad_conv_query: float32 [4, 2048], replicated
- grad_conv_key: float32 [4, 2048], replicated
- grad_conv_value: float32 [4, 4096], replicated
- grad_a_log: float32 [16], replicated
- grad_dt_bias: float32 [16], replicated
- grad_out_gain: float32 [256], replicated
- grad_w_out: float32 [2048, 4096], P('wide', 'narrow')
- grad_gain_mlp: float32 [2048], replicated
- grad_w_gate: float32 [2048, 5504], P('narrow', 'wide')
- grad_w_up: float32 [2048, 5504], P('narrow', 'wide')
- grad_w_down: float32 [5504, 2048], P('wide', 'narrow')
Inputs may be any that keep to these rules, and one draw needn't show every extreme that they name: `doc_lengths`: sequences lie end to end from row 0 in order, each taking its length rounded up to a multiple of 64 rows; these rounded lengths add up to 4096. One sequence, at a place drawn from the seed, starts within the first 512 rows and ends within the last 512 rows.
All inputs are finite; a program needn't handle non-finite values.
Results may differ from a plain program's by a relative error of at most 0.019.
Values may be sent and summed in bfloat16 or wider, within the bound.
A program may use at most 384 MiB of HBM per device.

v0:
```python
import jax
import jax.numpy as jnp
from jax import lax
from jax.sharding import PartitionSpec as P

DK = 128
DV = 256
CONV = 4
BLOCK = 64


EPS = 1e-06
HIGH = lax.Precision.HIGHEST


def from_behind(value, axis, steps):
    count = lax.axis_size(axis)
    initial, last = (max(0, -steps), min(count, count - steps))
    return lax.ppermute(value, axis, [(source, source + steps) for source in range(initial, last)])


def entering(value, axis, join, neutral):
    count, mine = (lax.axis_size(axis), lax.axis_index(axis))
    pieces = jax.tree.map(lambda part: lax.all_gather(part, axis), value)
    total = jax.tree.map(
        lambda part, zero: jnp.full_like(part, 0) + jnp.asarray(zero, part.dtype), value, neutral
    )

    def lap(position, total):
        longer = join(total, jax.tree.map(lambda part: part[position], pieces))
        return jax.tree.map(lambda new, old: jnp.where(position < mine, new, old), longer, total)

    return lax.fori_loop(0, count - 1, lap, total)


def entering_2(value, axis, combine, identity):
    size, position = (lax.axis_size(axis), lax.axis_index(axis))
    everything = jax.tree.map(
        lambda part, kind: lax.all_gather(part.astype(kind), axis),
        value,
        jax.tree.map(lambda a: jnp.bfloat16 if a.dtype == jnp.float32 else a.dtype, value),
    )
    start = jax.tree.map(
        lambda part, zero: jnp.broadcast_to(jnp.asarray(zero, part.dtype), part.shape),
        value,
        identity,
    )

    def lap(k, before):
        at = size - 1 - k
        reached = at > position
        new = combine(
            before, jax.tree.map(lambda part, own: part[at].astype(own.dtype), everything, value)
        )
        return jax.tree.map(lambda a, b: jnp.where(reached, a, b), new, before)

    return lax.fori_loop(0, size, lap, start)


def rounded(value):
    return lax.optimization_barrier(value.astype(jnp.bfloat16)).astype(jnp.float32)


def rms_norm(value, gain):
    return value * lax.rsqrt(jnp.mean(value * value, axis=-1, keepdims=True) + EPS) * gain


def unit_rows(value):
    return value * lax.rsqrt(jnp.sum(value * value, axis=-1, keepdims=True) + EPS)


def sequence_tables(doc_lengths, first_row, row_count, block_size):
    padded = (doc_lengths + block_size - 1) // block_size * block_size
    seq_ends = jnp.cumsum(padded)
    seq_starts = seq_ends - padded
    row_places = first_row + jnp.arange(row_count, dtype=jnp.int32)
    inside_mask = (row_places[:, None] >= seq_starts[None, :]) & (
        row_places[:, None] < seq_ends[None, :]
    )
    live_mask = jnp.any(
        inside_mask & (row_places[:, None] < (seq_starts + doc_lengths)[None, :]), axis=1
    )
    row_start = jnp.sum(jnp.where(inside_mask, seq_starts[None, :], 0), axis=1)
    block_heads = row_places[::block_size]
    fresh_block = jnp.any(block_heads[:, None] == seq_starts[None, :], axis=1)
    return (
        live_mask.astype(jnp.float32),
        row_start,
        row_places,
        jnp.where(fresh_block, 0.0, 1.0).astype(jnp.float32),
    )


def short_conv(mixed_rows, rim_rows, conv_weight, row_start, row_places):
    row_count = mixed_rows.shape[0]
    taps_count = conv_weight.shape[0]
    extended = jnp.concatenate([rim_rows, mixed_rows], axis=0)
    running_sum = jnp.zeros_like(mixed_rows)
    for tap_index in range(taps_count):
        reach_back = taps_count - 1 - tap_index
        within = (row_places - reach_back >= row_start).astype(jnp.float32)
        running_sum = (
            running_sum
            + conv_weight[tap_index] * extended[tap_index : tap_index + row_count] * within[:, None]
        )
    return jax.nn.silu(running_sum)


def split_heads(active, gate_part, a_log, dt_bias, live_rows):
    row_count = active.shape[0]
    head_count = a_log.shape[0]
    key_width = head_count * DK
    value_width = head_count * DV
    queries = unit_rows(active[:, :key_width].reshape(row_count, head_count, DK)) * DK ** (-0.5)
    key_rows = unit_rows(active[:, key_width : 2 * key_width].reshape(row_count, head_count, DK))
    value_rows = active[:, 2 * key_width :].reshape(row_count, head_count, DV)
    beta_rows = jax.nn.sigmoid(gate_part[:, value_width + head_count :]) * live_rows[:, None]
    log_decay = -jnp.exp(a_log) * jax.nn.softplus(
        gate_part[:, value_width : value_width + head_count] + dt_bias
    )
    return (queries, key_rows, value_rows, beta_rows, log_decay, gate_part[:, :value_width])


def to_blocks(array, block_size):
    block_count = array.shape[0] // block_size
    shaped = array.reshape((block_count, block_size) + array.shape[1:])
    if array.ndim == 3:
        return shaped.transpose(0, 2, 1, 3)
    return shaped.transpose(0, 2, 1)


def from_blocks(array):
    if array.ndim == 4:
        moved = array.transpose(0, 2, 1, 3)
        return moved.reshape((moved.shape[0] * moved.shape[1],) + moved.shape[2:])
    moved = array.transpose(0, 2, 1)
    return moved.reshape(moved.shape[0] * moved.shape[1], moved.shape[2])


def block_terms(key_rows, value_rows, beta_rows, log_decay, carry_flag):
    block_size = key_rows.shape[1]
    running = jnp.cumsum(log_decay, axis=1)
    row_ids = lax.broadcasted_iota(jnp.int32, (block_size, block_size), 0)
    col_ids = lax.broadcasted_iota(jnp.int32, (block_size, block_size), 1)
    lower_mask = row_ids >= col_ids
    spread = running[:, :, None] - running[:, None, :]
    decay_table = jnp.where(lower_mask, jnp.exp(jnp.where(lower_mask, spread, 0.0)), 0.0)
    opening = carry_flag * jnp.exp(running)
    closing = jnp.exp(running[:, -1:] - running)
    key_inner = jnp.einsum("hik,hjk->hij", key_rows, key_rows, precision=HIGH)
    strict = jnp.where(row_ids > col_ids, beta_rows[:, :, None] * decay_table * key_inner, 0.0)
    system = strict + jnp.eye(block_size, dtype=jnp.float32)
    right_side = jnp.concatenate(
        [beta_rows[:, :, None] * value_rows, (beta_rows * opening)[:, :, None] * key_rows], axis=2
    )
    solved = jax.scipy.linalg.solve_triangular(system, right_side, lower=True, unit_diagonal=True)
    value_width = value_rows.shape[2]
    return (decay_table, opening, closing, solved[:, :, :value_width], solved[:, :, value_width:])


def block_step(carry_state, queries, key_rows, value_rows, beta_rows, log_decay, carry_flag):
    decay_table, opening, closing, updates, weights = block_terms(
        key_rows, value_rows, beta_rows, log_decay, carry_flag
    )
    corrected = updates - jnp.einsum("hck,hvk->hcv", weights, carry_state, precision=HIGH)
    scores = jnp.einsum("hik,hjk->hij", queries, key_rows, precision=HIGH) * decay_table
    outputs = opening[:, :, None] * jnp.einsum("hck,hvk->hcv", queries, carry_state, precision=HIGH)
    outputs = outputs + jnp.einsum("hij,hjv->hiv", scores, corrected, precision=HIGH)
    keyed_rows = closing[:, :, None] * key_rows
    new_state = opening[:, -1][:, None, None] * carry_state + jnp.einsum(
        "hcv,hck->hvk", corrected, keyed_rows, precision=HIGH
    )
    return (new_state, outputs)


def block_summary(key_rows, value_rows, beta_rows, log_decay, carry_flag):
    decay_table, opening, closing, updates, weights = block_terms(
        key_rows, value_rows, beta_rows, log_decay, carry_flag
    )
    keyed_rows = closing[:, :, None] * key_rows
    eye_key = jnp.eye(key_rows.shape[2], dtype=jnp.float32)
    state_map = opening[:, -1][:, None, None] * eye_key - jnp.einsum(
        "hck,hcl->hkl", weights, keyed_rows, precision=HIGH
    )
    state_add = jnp.einsum("hcv,hck->hvk", updates, keyed_rows, precision=HIGH)
    return (state_map, state_add)


def join_maps(earlier, later):
    joined_map = jnp.einsum("hij,hjk->hik", earlier[0], later[0], precision=HIGH)
    joined_add = jnp.einsum("hvj,hjk->hvk", earlier[1], later[0], precision=HIGH) + later[1]
    return (joined_map, joined_add)


def contract_rows(left, right):
    return lax.dot_general(
        left, right, (((0,), (0,)), ((), ())), preferred_element_type=jnp.float32
    )


def contract_cols(left, right):
    return lax.dot_general(
        left, right, (((1,), (1,)), ((), ())), preferred_element_type=jnp.float32
    )


def shards(
    block_input,
    gain_attn,
    w_query,
    w_key,
    w_value,
    w_gate_out,
    w_decay,
    w_beta,
    conv_query,
    conv_key,
    conv_value,
    a_log,
    dt_bias,
    out_gain,
    w_out,
    gain_mlp,
    w_gate,
    w_up,
    w_down,
    doc_lengths,
    cotangent,
):
    row_count = block_input.shape[0]
    quarter = cotangent.shape[0]
    head_count = a_log.shape[0]
    wide_index = lax.axis_index("wide")
    narrow_index = lax.axis_index("narrow")
    live_rows, row_start, row_places, carry_flags = sequence_tables(
        doc_lengths, wide_index * row_count, row_count, BLOCK
    )
    input_rows = block_input.astype(jnp.float32)

    def fetch_mixer():
        return (
            lax.all_gather(w_query, "wide", axis=0, tiled=True),
            lax.all_gather(w_key, "wide", axis=0, tiled=True),
            lax.all_gather(w_value, "wide", axis=0, tiled=True),
            lax.all_gather(w_gate_out, "wide", axis=0, tiled=True),
            lax.all_gather(w_decay, "wide", axis=0, tiled=True),
            lax.all_gather(w_beta, "wide", axis=0, tiled=True),
            lax.all_gather(w_out, "wide", axis=0, tiled=True),
        )

    fetched = fetch_mixer()
    projection = jnp.concatenate(fetched[:6], axis=1)
    out_weight = fetched[6]
    widths = [weight_piece.shape[1] for weight_piece in fetched[:6]]
    normed, attn_norm_back = jax.vjp(rms_norm, input_rows, gain_attn)
    normed_low = normed.astype(jnp.bfloat16)
    projected = jnp.dot(normed_low, projection, preferred_element_type=jnp.float32)
    mixed_width = widths[0] + widths[1] + widths[2]
    mixed_low = projected[:, :mixed_width].astype(jnp.bfloat16)
    gate_part = projected[:, mixed_width:]
    rim_rows = from_behind(mixed_low[row_count - (CONV - 1) :], "wide", 1)
    conv_weight = jnp.concatenate([conv_query, conv_key, conv_value], axis=1)

    def prepare(mixed_rows, rim_in, gate_in, conv_in, a_log_in, dt_in):
        active = short_conv(mixed_rows, rim_in, conv_in, row_start, row_places)
        return split_heads(active, gate_in, a_log_in, dt_in, live_rows)

    prepared, prepare_back = jax.vjp(
        prepare,
        mixed_low.astype(jnp.float32),
        rim_rows.astype(jnp.float32),
        gate_part,
        conv_weight,
        a_log,
        dt_bias,
    )
    queries_raw, keys_raw, values_raw, beta_rows, log_decay, gate_rows = prepared
    queries = rounded(queries_raw)
    key_rows = rounded(keys_raw)
    value_rows = rounded(values_raw)
    blocked = (
        to_blocks(queries, BLOCK),
        to_blocks(key_rows, BLOCK),
        to_blocks(value_rows, BLOCK),
        to_blocks(beta_rows, BLOCK),
        to_blocks(log_decay, BLOCK),
    )
    eye_key = jnp.broadcast_to(jnp.eye(DK, dtype=jnp.float32), (head_count, DK, DK))
    zero_state = jnp.zeros((head_count, DV, DK), jnp.float32)

    def summarize(accumulated, block_item):
        return (join_maps(accumulated, block_summary(*block_item)), None)

    (state_map, state_add), ignored = lax.scan(
        summarize,
        (eye_key, zero_state),
        (blocked[1], blocked[2], blocked[3], blocked[4], carry_flags),
    )
    entry_state = entering((state_map, state_add), "wide", join_maps, (eye_key, zero_state))[1]

    def mix_local(query_blocks, key_blocks, value_blocks, beta_blocks, decay_blocks, start_state):

        def advance(carry_state, block_item):
            return block_step(carry_state, *block_item)

        last_state, outputs = lax.scan(
            advance,
            start_state,
            (query_blocks, key_blocks, value_blocks, beta_blocks, decay_blocks, carry_flags),
        )
        return (outputs, last_state)

    (mix_out, final_state), mix_back = jax.vjp(
        mix_local, blocked[0], blocked[1], blocked[2], blocked[3], blocked[4], entry_state
    )

    def finish(output_blocks, gate_in, gain_in):
        opened = from_blocks(output_blocks) * live_rows[:, None, None]
        shaped = rms_norm(opened, gain_in) * jax.nn.silu(gate_in.reshape(row_count, head_count, DV))
        return shaped.reshape(row_count, head_count * DV)

    finished, finish_back = jax.vjp(finish, mix_out, gate_rows, out_gain)
    mixer_low = finished.astype(jnp.bfloat16)
    head_part = contract_cols(mixer_low, out_weight)
    residual = input_rows + lax.psum(head_part, "narrow")
    own_rows = lax.dynamic_slice_in_dim(residual, narrow_index * quarter, quarter, 0)
    mlp_normed, mlp_norm_back = jax.vjp(rms_norm, own_rows, gain_mlp)
    mlp_low = mlp_normed.astype(jnp.bfloat16)
    gathered_rows, gathered_cot = (
        lax.all_gather(mlp_low, "wide", axis=0, tiled=True),
        lax.all_gather(cotangent, "wide", axis=0, tiled=True),
    )
    gate_pre = jnp.dot(gathered_rows, w_gate, preferred_element_type=jnp.float32)
    up_pre = jnp.dot(gathered_rows, w_up, preferred_element_type=jnp.float32)
    gate_sig = jax.nn.sigmoid(gate_pre)
    gate_act = gate_pre * gate_sig
    hidden_low = (gate_act * up_pre).astype(jnp.bfloat16)
    grad_hidden = contract_cols(gathered_cot, w_down)
    grad_w_down = contract_rows(hidden_low, gathered_cot)
    grad_gate_low = (grad_hidden * up_pre * gate_sig * (1.0 + gate_pre * (1.0 - gate_sig))).astype(
        jnp.bfloat16
    )
    grad_up_low = (grad_hidden * gate_act).astype(jnp.bfloat16)
    grad_w_gate = contract_rows(gathered_rows, grad_gate_low)
    grad_w_up = contract_rows(gathered_rows, grad_up_low)
    mlp_part = lax.psum_scatter(
        jnp.dot(hidden_low, w_down, preferred_element_type=jnp.float32).astype(jnp.bfloat16),
        "wide",
        scatter_dimension=0,
        tiled=True,
    ).astype(jnp.float32)
    grad_mlp_normed = lax.psum_scatter(
        (contract_cols(grad_gate_low, w_gate) + contract_cols(grad_up_low, w_up)).astype(
            jnp.bfloat16
        ),
        "wide",
        scatter_dimension=0,
        tiled=True,
    ).astype(jnp.float32)
    output = (own_rows + mlp_part).astype(jnp.bfloat16)
    grad_own_norm, grad_gain_mlp = mlp_norm_back(grad_mlp_normed)
    grad_own = cotangent.astype(jnp.float32) + grad_own_norm
    grad_residual = lax.all_gather(
        grad_own.astype(jnp.bfloat16), "narrow", axis=0, tiled=True
    ).astype(grad_own.dtype)
    grad_attn_low = grad_residual.astype(jnp.bfloat16)
    again = fetch_mixer()
    projection_back = jnp.concatenate(again[:6], axis=1)
    out_back = again[6]
    grad_mixer = jnp.dot(grad_attn_low, out_back, preferred_element_type=jnp.float32)
    grad_w_out = contract_rows(grad_attn_low, mixer_low)
    grad_outputs, grad_gate_rows, grad_out_gain = finish_back(grad_mixer)
    direct = mix_back((grad_outputs, jnp.zeros_like(final_state)))[5]
    exit_grad = entering_2(
        (jnp.swapaxes(state_map, 1, 2), direct), "wide", join_maps, (eye_key, zero_state)
    )[1]
    grad_blocks = mix_back((grad_outputs, exit_grad))
    grad_mixed, grad_rim, grad_gates, grad_conv, grad_a_log, grad_dt = prepare_back(
        (
            from_blocks(grad_blocks[0]),
            from_blocks(grad_blocks[1]),
            from_blocks(grad_blocks[2]),
            from_blocks(grad_blocks[3]),
            from_blocks(grad_blocks[4]),
            grad_gate_rows,
        )
    )
    grad_next = from_behind(grad_rim, "wide", -1)
    grad_mixed = grad_mixed.at[row_count - (CONV - 1) :].add(grad_next)
    grad_raw_low = jnp.concatenate([grad_mixed, grad_gates], axis=1).astype(jnp.bfloat16)
    grad_projection = contract_rows(normed_low, grad_raw_low)
    grad_normed = contract_cols(grad_raw_low, projection_back)
    grad_input_part, grad_gain_attn = attn_norm_back(grad_normed)
    shares = (
        lax.psum_scatter(
            grad_input_part.astype(jnp.bfloat16), "narrow", scatter_dimension=0, tiled=True
        ).astype(jnp.float32),
        lax.psum_scatter(
            grad_w_gate.astype(jnp.bfloat16), "narrow", scatter_dimension=0, tiled=True
        ).astype(jnp.float32),
        lax.psum_scatter(
            grad_w_up.astype(jnp.bfloat16), "narrow", scatter_dimension=0, tiled=True
        ).astype(jnp.float32),
        lax.psum_scatter(
            grad_w_down.astype(jnp.bfloat16), "narrow", scatter_dimension=1, tiled=True
        ).astype(jnp.float32),
    )
    grad_input = shares[0] + grad_own
    bounds = [0]
    for width_value in widths:
        bounds.append(bounds[-1] + width_value)
    pieces = [grad_projection[:, bounds[position] : bounds[position + 1]] for position in range(6)]
    summed = (
        lax.psum_scatter(
            pieces[0].astype(jnp.bfloat16), "wide", scatter_dimension=0, tiled=True
        ).astype(jnp.float32),
        lax.psum_scatter(
            pieces[1].astype(jnp.bfloat16), "wide", scatter_dimension=0, tiled=True
        ).astype(jnp.float32),
        lax.psum_scatter(
            pieces[2].astype(jnp.bfloat16), "wide", scatter_dimension=0, tiled=True
        ).astype(jnp.float32),
        lax.psum_scatter(
            pieces[3].astype(jnp.bfloat16), "wide", scatter_dimension=0, tiled=True
        ).astype(jnp.float32),
        lax.psum_scatter(
            pieces[4].astype(jnp.bfloat16), "wide", scatter_dimension=0, tiled=True
        ).astype(jnp.float32),
        lax.psum_scatter(
            pieces[5].astype(jnp.bfloat16), "wide", scatter_dimension=0, tiled=True
        ).astype(jnp.float32),
        lax.psum_scatter(
            grad_w_out.astype(jnp.bfloat16), "wide", scatter_dimension=0, tiled=True
        ).astype(jnp.float32),
    )
    narrow_count = lax.axis_size("narrow")

    def spread_out(piece_value, axis_index):
        block_width = piece_value.shape[axis_index]
        full_shape = list(piece_value.shape)
        full_shape[axis_index] = block_width * narrow_count
        return lax.dynamic_update_slice_in_dim(
            jnp.zeros(full_shape, jnp.float32), piece_value, narrow_index * block_width, axis_index
        )

    key_width = widths[0]
    small = lax.psum(
        (
            grad_gain_attn,
            grad_gain_mlp,
            spread_out(grad_conv[:, :key_width], 1),
            spread_out(grad_conv[:, key_width : 2 * key_width], 1),
            spread_out(grad_conv[:, 2 * key_width :], 1),
            spread_out(grad_a_log, 0),
            spread_out(grad_dt, 0),
            grad_out_gain,
        ),
        ("wide", "narrow"),
    )
    return (
        output,
        grad_input,
        small[0],
        summed[0],
        summed[1],
        summed[2],
        summed[3],
        summed[4],
        summed[5],
        small[2],
        small[3],
        small[4],
        small[5],
        small[6],
        small[7],
        summed[6],
        small[1],
        shares[1],
        shares[2],
        shares[3],
    )


def solution(mesh):
    return jax.shard_map(
        shards,
        mesh=mesh,
        in_specs=(
            P("wide", None),
            P(),
            P("wide", "narrow"),
            P("wide", "narrow"),
            P("wide", "narrow"),
            P("wide", "narrow"),
            P("wide", "narrow"),
            P("wide", "narrow"),
            P(None, "narrow"),
            P(None, "narrow"),
            P(None, "narrow"),
            P("narrow"),
            P("narrow"),
            P(),
            P("wide", "narrow"),
            P(),
            P(None, "wide"),
            P(None, "wide"),
            P("wide", None),
            P(),
            P(("wide", "narrow"), None),
        ),
        out_specs=(
            P(("wide", "narrow"), None),
            P(("wide", "narrow"), None),
            P(),
            P("wide", "narrow"),
            P("wide", "narrow"),
            P("wide", "narrow"),
            P("wide", "narrow"),
            P("wide", "narrow"),
            P("wide", "narrow"),
            P(),
            P(),
            P(),
            P(),
            P(),
            P(),
            P("wide", "narrow"),
            P(),
            P("narrow", "wide"),
            P("narrow", "wide"),
            P("wide", "narrow"),
        ),
        check_vma=False,
    )
```

profile of v0, /device:TPU:10, one launch (start us, length us, event | category | flops | bytes accessed | tf_op | source)
XLA Modules:
  0.0 3296.8 jit_solution(1605816849475867506)
XLA Ops:
  10.9 25.3 all_gather.65
  36.6 26.2 all_gather.66
  71.3 39.7 %all-gather.19.cloned.1.call-done = bf16[2048,512]{1,0:T(8,128)(2,1)} async-done(((bf16[256,512]{1,0:T(8,128)(2,1)}), bf16[2048,512]{1,0:T(8,128)(2,1)}) %all-gather.19.cloned.1.call-update) | async-done | bytes 2097168 | tf_op jit(solution)/shard_map/all_gather | solution.py:243
  111.0 73.4 %all-gather.21.cloned.1.call-done = bf16[2048,1024]{1,0:T(8,128)(2,1)} async-done(((bf16[256,1024]{1,0:T(8,128)(2,1)}), bf16[2048,1024]{1,0:T(8,128)(2,1)}) %all-gather.21.cloned.1.call-update) | async-done | bytes 4194320 | tf_op jit(solution)/shard_map/all_gather | solution.py:244
  184.4 73.7 %all-gather.23.cloned.1.call-done = bf16[2048,1024]{1,0:T(8,128)(2,1)} async-done(((bf16[256,1024]{1,0:T(8,128)(2,1)}), bf16[2048,1024]{1,0:T(8,128)(2,1)}) %all-gather.23.cloned.1.call-update) | async-done | bytes 4194320 | tf_op jit(solution)/shard_map/all_gather | solution.py:245
  344.8 278.6 %while.149 = (s32[]{:T(128)}, f32[4,128,128]{1,2,0:T(8,128)}, f32[4,256,128]{1,2,0:T(8,128)}, f32[8]{0:T(128)}, f32[8,4,64]{2,1,0:T(4,128)S(1)}, /*index=5*/f32[...) while((s32[]{:T(128)}, f32[4,128,128]{1,2,0:T(8,128)}, ...), condition=%wide.region_8.10_spmd.clone, body=%wide.region_6.9_spmd.clone.sunk | while | flops 554529344 | bytes 6714091 | solution.py:294
  634.2 40.6 %all-gather.33.cloned.1.call-done = f32[32,128,128]{2,1,0:T(8,128)} async-done(((f32[4,128,128]{2,1,0:T(8,128)}), f32[32,128,128]{2,1,0:T(8,128)}) %all-gather.33.cloned.1.call-update) | async-done | bytes 2097168 | tf_op jit(solution)/shard_map/all_gather | solution.py:24
  674.8 73.8 %all-gather.35.cloned.1.call-done = f32[32,256,128]{2,1,0:T(8,128)} async-done(((f32[4,256,128]{2,1,0:T(8,128)}), f32[32,256,128]{2,1,0:T(8,128)}) %all-gather.35.cloned.1.call-update) | async-done | bytes 4194320 | tf_op jit(solution)/shard_map/all_gather | solution.py:24
  748.6 40.0 %while.150 = (s32[]{:T(128)}, f32[4,256,128]{1,2,0:T(8,128)}, s32[]{:T(128)}, f32[8,4,128,128]{3,2,1,0:T(8,128)}, f32[8,4,256,128]{3,2,1,0:T(8,128)}, /*index=5*/s32[]{:T(128)}, s32[]{:T(128)}) while((s32[]{:T(128)}, f32[4,256,128]{1,2,0:T(8,128)}, s32[]{:T(128)}, f32[8,4,128,128]{3,2,1,0:T(8,128)}, ...), condition=%wide.region_10.12_spmd.clone, body=%wide.region_9.11_spmd.clone.sunk | while | flops 201850880 | bytes 5507171 | solution.py:33
  797.1 388.9 %while.147 = (s32[]{:T(128)}, f32[4,256,128]{2,1,0:T(8,128)S(1)}, f32[8,4,64,256]{3,1,2,0:T(4,128)}, f32[8,4,64,64]{3,2,1,0:T(8,128)}, f32[8,4,64]{2,1,0:T(4,128...) while((s32[]{:T(128)}, f32[4,256,128]{2,1,0:T(8,128)S(1)}, ...), condition=%wide.region_14.16_spmd.clone.clone, body=%wide.region_12.15_spmd.clone.clone.sunk | while | flops 479319872 | bytes 11213785 | solution.py:306
  805.2 21.0 custom-call.47
  853.8 21.0 custom-call.47
  902.4 21.0 custom-call.47
  951.0 21.0 custom-call.47
  1210.4 79.4 %all-reduce.23.cloned.1.call-done = f32[512,2048]{1,0:T(8,128)} async-done(((f32[512,2048]{1,0:T(8,128)}), f32[512,2048]{1,0:T(8,128)}) %all-reduce.23.cloned.1.call-update) | async-done | bytes 4194320 | tf_op jit(solution)/shard_map/psum | solution.py:325
  1294.1 73.2 %all-gather.27.cloned.1.call-done = bf16[1024,2048]{1,0:T(8,128)(2,1)} async-done(((bf16[128,2048]{1,0:T(8,128)(2,1)}), bf16[1024,2048]{1,0:T(8,128)(2,1)}) %all-gather.27.cloned.1.call-update) | async-done | bytes 4194320 | tf_op jit(solution)/shard_map/all_gather | solution.py:330
  1379.9 61.3 %all-gather.29.cloned.1.call-done = bf16[1024,2048]{1,0:T(8,128)(2,1)} async-done(((bf16[128,2048]{1,0:T(8,128)(2,1)}), bf16[1024,2048]{1,0:T(8,128)(2,1)}) %all-gather.29.cloned.1.call-update) | async-done | bytes 4194320 | tf_op jit(solution)/shard_map/all_gather | solution.py:331
  1458.9 86.7 %reduce-scatter.20.cloned.1.call-done = bf16[128,2048]{1,0:T(8,128)(2,1)} async-done(((bf16[1024,2048]{1,0:T(8,128)(2,1)}), bf16[128,2048]{1,0:T(8,128)(2,1)}) %reduce-scatter.20.cloned.1.call-update) | async-done | bytes 524304 | tf_op jit(solution)/shard_map/reduce_scatter | solution.py:352
  1615.6 66.9 %while.151 = (s32[]{:T(128)}, f32[4,256,128]{2,1,0:T(8,128)S(1)}, f32[8,4,1,1]{1,3,2,0:T(1,128)}, f32[8,4,64,1]{2,1,3,0:T(4,128)}, f32[8,4,64,256]{3,2,1,0:T(8,1...) while((s32[]{:T(128)}, f32[4,256,128]{2,1,0:T(8,128)S(1)}, ...), condition=%wide.region_23.25_spmd.clone, body=%wide.region_22.24_spmd.clone.sunk | while | flops 353173504 | bytes 4724427 | solution.py:306
  1705.8 27.8 all-gather.39.cloned.1.call-done
  1733.6 35.2 %while.152 = (s32[]{:T(128)}, f32[4,256,128]{1,2,0:T(8,128)}, s32[]{:T(128)}, bf16[8,4,128,128]{3,2,1,0:T(8,128)(2,1)}, bf16[8,4,256,128]{3,2,1,0:T(8,128)(2,1)}...) while((s32[]{:T(128)}, f32[4,256,128]{1,2,0:T(8,128)}, s32[]{:T(128)}, ...), condition=%wide.region_25.27_spmd.clone, body=%wide.region_24.26_spmd.clone.sunk | while | flops 201981952 | bytes 4065441 | solution.py:57
  1775.1 488.6 %while.148 = (s32[]{:T(128)}, f32[4,256,128]{2,1,0:T(8,128)S(1)}, f32[8,4,64,128]{3,2,1,0:T(8,128)}, f32[8,4,64,128]{3,2,1,0:T(8,128)}, f32[8,4,64,256]{3,2,1,0:...) while((s32[]{:T(128)}, f32[4,256,128]{2,1,0:T(8,128)S(1)}, ...), condition=%wide.region_37.39_spmd.clone.clone, body=%wide.region_26.38_spmd.clone.clone.sunk | while | flops 971110720 | bytes 20623056 | solution.py:306
  2415.1 63.4 %reduce-scatter.42.cloned.1.call-done = bf16[256,4]{1,0:T(8,128)(2,1)} async-done(((bf16[2048,4]{1,0:T(8,128)(2,1)}), bf16[256,4]{1,0:T(8,128)(2,1)}) %reduce-scatter.42.cloned.1.call-update) | async-done | bytes 2064
  2480.1 89.6 %reduce-scatter.18.cloned.1.call-done = bf16[128,2048]{1,0:T(8,128)(2,1)} async-done(((bf16[1024,2048]{1,0:T(8,128)(2,1)}), bf16[128,2048]{1,0:T(8,128)(2,1)}) %reduce-scatter.18.cloned.1.call-update) | async-done | bytes 524304 | tf_op jit(solution)/shard_map/reduce_scatter | solution.py:346
  2569.7 32.6 reduce-scatter.22.cloned.1.call-done
  2605.7 69.3 %reduce-scatter.24.cloned.1.call-done = bf16[256,512]{0,1:T(8,128)(2,1)} async-done(((bf16[2048,512]{0,1:T(8,128)(2,1)}), bf16[256,512]{0,1:T(8,128)(2,1)}) %reduce-scatter.24.cloned.1.call-update) | async-done | bytes 262160 | tf_op jit(solution)/shard_map/reduce_scatter | solution.py:414
  2676.8 69.2 %reduce-scatter.26.cloned.1.call-done = bf16[256,512]{0,1:T(8,128)(2,1)} async-done(((bf16[2048,512]{0,1:T(8,128)(2,1)}), bf16[256,512]{0,1:T(8,128)(2,1)}) %reduce-scatter.26.cloned.1.call-update) | async-done | bytes 262160 | tf_op jit(solution)/shard_map/reduce_scatter | solution.py:417
  2747.9 90.0 %reduce-scatter.32.cloned.1.call-done = bf16[256,1024]{1,0:T(8,128)(2,1)} async-done(((bf16[2048,1024]{1,0:T(8,128)(2,1)}), bf16[256,1024]{1,0:T(8,128)(2,1)}) %reduce-scatter.32.cloned.1.call-update) | async-done | bytes 524304 | tf_op jit(solution)/shard_map/reduce_scatter | solution.py:432
  2840.0 89.7 %reduce-scatter.28.cloned.1.call-done = bf16[256,1024]{0,1:T(8,128)(2,1)} async-done(((bf16[2048,1024]{0,1:T(8,128)(2,1)}), bf16[256,1024]{0,1:T(8,128)(2,1)}) %reduce-scatter.28.cloned.1.call-update) | async-done | bytes 524304 | tf_op jit(solution)/shard_map/reduce_scatter | solution.py:420
  2932.0 89.9 %reduce-scatter.30.cloned.1.call-done = bf16[256,1024]{0,1:T(8,128)(2,1)} async-done(((bf16[2048,1024]{0,1:T(8,128)(2,1)}), bf16[256,1024]{0,1:T(8,128)(2,1)}) %reduce-scatter.30.cloned.1.call-update) | async-done | bytes 524304 | tf_op jit(solution)/shard_map/reduce_scatter | solution.py:423
  3024.1 122.1 %all-reduce.25.cloned.1.call-done = f32[4,4096]{1,0:T(4,128)} async-done(((f32[4,4096]{1,0:T(4,128)}), f32[4,4096]{1,0:T(4,128)}) %all-reduce.25.cloned.1.call-update) | async-done | bytes 65552 | tf_op jit(solution)/shard_map/psum | solution.py:447
  3146.2 133.3 %all-reduce.27.cloned.1.call-done = (f32[2048]{0:T(1024)}, f32[4,2048]{1,0:T(4,128)}, f32[4,2048]{1,0:T(4,128)}, f32[16]{0:T(128)}, f32[16]{0:T(128)}, /*index=5*/f32[256]{0:T(256)}, f32[2048]{0:T(1024)}) async-done(((f32[2048]{0:T(1024)}, f32[4,2048]{1,0:T(4,128)}, f32[4,2048]{1,0:T(4,128)}, f32[16]{0:T(128)}, f32[16]{0:T(128)}, /*index=5*/f32[256]{0:T(256)}, f32[2048]{0:T(1024)}), (f32[2048]{0:T(1024)}, ...) | async-done | bytes 83088 | tf_op jit(solution)/shard_map/psum | solution.py:447
  (1254 shorter events, 1663.5 us)
Async XLA Ops:
  7.2 1434.0 %copy-start = (bf16[688,2048]{1,0:T(8,128)(2,1)S(1)}, bf16[688,2048]{1,0:T(8,128)(2,1)}, u32[]{:S(2)}) copy-start(bf16[688,2048]{1,0:T(8,128)(2,1)} %param.55) | copy-start | bytes 8454148
  7.2 64.1 %all-gather.17.cloned.1.call-start = ((), (), s32[]{:S(2)}) async-start(), calls=%async_computation.13 | async-start | bytes 2359296 | tf_op jit(solution)/shard_map/all_gather | solution.py:242
  7.9 103.1 %all-gather.19.cloned.1.call-start = ((), (), s32[]{:S(2)}) async-start(), calls=%async_computation.14 | async-start | bytes 2359296 | tf_op jit(solution)/shard_map/all_gather | solution.py:243
  8.7 175.7 %all-gather.21.cloned.1.call-start = ((), (), s32[]{:S(2)}) async-start(), calls=%async_computation.15 | async-start | bytes 4718592 | tf_op jit(solution)/shard_map/all_gather | solution.py:244
  9.4 248.7 %all-gather.23.cloned.1.call-start = ((), (), s32[]{:S(2)}) async-start(), calls=%async_computation.16 | async-start | bytes 4718592 | tf_op jit(solution)/shard_map/all_gather | solution.py:245
  10.0 664.8 %all-gather.33.cloned.1.call-start = ((), (), s32[]{:S(2)}) async-start(), calls=%async_computation.34 | async-start | bytes 2359296 | tf_op jit(solution)/shard_map/all_gather | solution.py:24
  301.0 15.6 collective-permute-start
  330.2 301.2 %copy-start.36 = (f32[512,4]{0,1:T(4,128)}, f32[512,4]{0,1:T(4,128)S(1)}, u32[]{:S(2)}) copy-start(f32[512,4]{0,1:T(4,128)S(1)} %get-tuple-element.2804) | copy-start | bytes 24580
  625.3 123.4 %all-gather.35.cloned.1.call-start = ((), (), s32[]{:S(2)}) async-start(), calls=%async_computation.35 | async-start | bytes 4718592 | tf_op jit(solution)/shard_map/all_gather | solution.py:24
  627.4 571.7 %all-gather.25.cloned.1.call-start = ((), (), s32[]{:S(2)}) async-start(), calls=%async_computation.17 | async-start | bytes 4718592 | tf_op jit(solution)/shard_map/all_gather | solution.py:248
  628.1 661.7 %all-reduce.23.cloned.1.call-start = ((), (), s32[]{:S(2)}) async-start(), calls=%async_computation.18 | async-start | bytes 8388608 | tf_op jit(solution)/shard_map/psum | solution.py:325
  1206.1 161.2 %all-gather.27.cloned.1.call-start = ((), (), s32[]{:S(2)}) async-start(), calls=%async_computation.19 | async-start | bytes 4718592 | tf_op jit(solution)/shard_map/all_gather | solution.py:330
  1293.5 147.7 %all-gather.29.cloned.1.call-start = ((), (), s32[]{:S(2)}) async-start(), calls=%async_computation.21 | async-start | bytes 4718592 | tf_op jit(solution)/shard_map/all_gather | solution.py:331
  1294.1 251.5 %reduce-scatter.20.cloned.1.call-start = ((), (), s32[]{:S(2)}) async-start(), calls=%async_computation.22 | async-start | bytes 4718592 | tf_op jit(solution)/shard_map/reduce_scatter | solution.py:352
  1458.4 113.5 %all-gather.31.cloned.1.call-start = ((), (), s32[]{:S(2)}) async-start(), calls=%async_computation.23 | async-start | bytes 2621440 | tf_op jit(solution)/shard_map/all_gather | solution.py:363
  1550.5 155.3 %all-gather.37.cloned.1.call-start = ((), (), s32[]{:S(2)}) async-start(), calls=%async_computation.36 | async-start | bytes 1179648 | tf_op jit(solution)/shard_map/all_gather | solution.py:39
  1552.2 181.4 %all-gather.39.cloned.1.call-start = ((), (), s32[]{:S(2)}) async-start(), calls=%async_computation.37 | async-start | bytes 2359296 | tf_op jit(solution)/shard_map/all_gather | solution.py:39
  1683.2 710.9 %reduce-scatter.34.cloned.1.call-start = ((), (), s32[]{:S(2)}) async-start(), calls=%async_computation.31 | async-start | bytes 3522560 | tf_op jit(solution)/shard_map/reduce_scatter | solution.py:398
  1690.5 706.0 %reduce-scatter.36.cloned.1.call-start = ((), (), s32[]{:S(2)}) async-start(), calls=%async_computation.32 | async-start | bytes 3522560 | tf_op jit(solution)/shard_map/reduce_scatter | solution.py:401
  1698.1 700.9 %reduce-scatter.38.cloned.1.call-start = ((), (), s32[]{:S(2)}) async-start(), calls=%async_computation.33 | async-start | bytes 3522560 | tf_op jit(solution)/shard_map/reduce_scatter | solution.py:404
  1705.5 708.1 %reduce-scatter.40.cloned.1.call-start = ((), (), s32[]{:S(2)}) async-start(), calls=%async_computation.38 | async-start | bytes 589824
  2311.5 15.3 collective-permute-start.1
  2352.1 126.4 %reduce-scatter.42.cloned.1.call-start = ((), (), s32[]{:S(2)}) async-start(), calls=%async_computation.39 | async-start | bytes 589824
  2353.3 216.5 %reduce-scatter.18.cloned.1.call-start = ((), (), s32[]{:S(2)}) async-start(), calls=%async_computation.20 | async-start | bytes 4718592 | tf_op jit(solution)/shard_map/reduce_scatter | solution.py:346
  2359.8 242.6 %reduce-scatter.22.cloned.1.call-start = ((), (), s32[]{:S(2)}) async-start(), calls=%async_computation.24 | async-start | bytes 2621440 | tf_op jit(solution)/shard_map/reduce_scatter | solution.py:395
  2375.2 299.8 %reduce-scatter.24.cloned.1.call-start = ((), (), s32[]{:S(2)}) async-start(), calls=%async_computation.25 | async-start | bytes 2359296 | tf_op jit(solution)/shard_map/reduce_scatter | solution.py:414
  2380.1 365.9 %reduce-scatter.26.cloned.1.call-start = ((), (), s32[]{:S(2)}) async-start(), calls=%async_computation.26 | async-start | bytes 2359296 | tf_op jit(solution)/shard_map/reduce_scatter | solution.py:417
  2380.8 457.1 %reduce-scatter.32.cloned.1.call-start = ((), (), s32[]{:S(2)}) async-start(), calls=%async_computation.30 | async-start | bytes 4718592 | tf_op jit(solution)/shard_map/reduce_scatter | solution.py:432
  2387.2 542.5 %reduce-scatter.28.cloned.1.call-start = ((), (), s32[]{:S(2)}) async-start(), calls=%async_computation.27 | async-start | bytes 4718592 | tf_op jit(solution)/shard_map/reduce_scatter | solution.py:420
  2393.4 628.5 %reduce-scatter.30.cloned.1.call-start = ((), (), s32[]{:S(2)}) async-start(), calls=%async_computation.28 | async-start | bytes 4718592 | tf_op jit(solution)/shard_map/reduce_scatter | solution.py:423
  2394.0 752.2 %all-reduce.25.cloned.1.call-start = ((), (), s32[]{:S(2)}) async-start(), calls=%async_computation.29 | async-start | bytes 131072 | tf_op jit(solution)/shard_map/psum | solution.py:447
  2402.1 877.5 %all-reduce.27.cloned.1.call-start = ((), (), s32[]{:S(2)}) async-start(), calls=%async_computation.40 | async-start | bytes 167936 | tf_op jit(solution)/shard_map/psum | solution.py:447
  (100 other events, 4602.2 us)
Sparse Core Ops, SparseCore 0:
  10.2 50.7 all-gather.16
  63.1 47.8 all-gather.18
  113.1 71.2 all-gather.20
  186.4 71.6 all-gather.22
  625.4 49.3 all-gather.32
  677.3 71.2 all-gather.34
  750.7 71.6 all-gather.24
  1206.2 83.5 all-reduce.22
  1293.6 73.6 all-gather.26
  1369.5 71.6 all-gather.28
  1458.5 87.0 reduce-scatter.19
  1550.6 21.2 all-gather.30
  1574.5 40.0 all-gather.36
  1683.4 50.2 all-gather.38
  1736.1 33.4 reduce-scatter.33
  1772.2 36.0 reduce-scatter.35
  1810.7 36.0 reduce-scatter.37
  2352.3 61.2 reduce-scatter.39
  2417.5 61.0 reduce-scatter.41
  2482.5 87.2 reduce-scatter.17
  2572.3 30.0 reduce-scatter.21
  2606.3 68.6 reduce-scatter.23
  2678.9 67.0 reduce-scatter.25
  2749.9 87.9 reduce-scatter.31
  2841.5 88.1 reduce-scatter.27
  2933.7 88.1 reduce-scatter.29
  3027.9 118.3 all-reduce.24
  3154.4 125.0 all-reduce.26
where the time goes:
time: 3320 us; the launch traced here: 3300 us
  waiting for transfers between devices  1520 us (46%)
  other arithmetic  787 us (24%)
  matrix products  590 us (18%)
  local copies, waits for them, and re-layouts  317 us (10%)
  blocking collectives  51.6 us (2%)
    another operation x104, other arithmetic, block_terms(): jax.scipy.linalg.solve_triangular(system, right_side, lower=True, unit_di...  497 us
    psum x2, waiting for transfers between devices, shards(): lax.psum((grad_gain_attn, grad_gain_mlp, spread_out(grad_conv[:, :key_wid...  255 us
    all_gather x2, waiting for transfers between devices, entering(): pieces = jax.tree.map(lambda part: lax.all_gather(part, axis), value)  114 us
    reduce_scatter x1, waiting for transfers between devices, shards(): lax.psum_scatter(grad_w_out.astype(jnp.bfloat16), 'wide', scatter_dimensi...  90 us
    reduce_scatter x1, waiting for transfers between devices, shards(): lax.psum_scatter(pieces[3].astype(jnp.bfloat16), 'wide', scatter_dimensio...  89.9 us
    reduce_scatter x1, waiting for transfers between devices, shards(): lax.psum_scatter(pieces[2].astype(jnp.bfloat16), 'wide', scatter_dimensio...  89.7 us
    reduce_scatter x1, waiting for transfers between devices, shards(): lax.psum_scatter(jnp.dot(hidden_low, w_down, preferred_element_type=jnp.f...  89.6 us
    reduce_scatter x1, waiting for transfers between devices, shards(): lax.psum_scatter((contract_cols(grad_gate_low, w_gate) + contract_cols(gr...  86.7 us
  transfers between devices with their start and end apart: 30, of which 23 were waited for; matrix products, arithmetic and copies ran while one was open for 39% of the time, Pallas kernels for 0%

commit v1 on v0

v1 whole, which is shorter than its diff:
```python
import functools
import jax
import jax.numpy as jnp
from jax import lax
from jax.experimental import pallas as pl
from jax.experimental.pallas import tpu as pltpu
from jax.sharding import PartitionSpec as P

DK, DV, BLOCK, EPS = 128, 256, 64, 1e-6
BF = jnp.bfloat16
F32 = jnp.float32


def mm(a, b):
    return jnp.dot(a.astype(BF), b.astype(BF), preferred_element_type=F32)


def mm_nt(a, b):
    return lax.dot_general(a.astype(BF), b.astype(BF), (((1,), (1,)), ((), ())), preferred_element_type=F32)


def mm_tn(a, b):
    return lax.dot_general(a.astype(BF), b.astype(BF), (((0,), (0,)), ((), ())), preferred_element_type=F32)


def split(a):
    high = a.astype(BF)
    return high, (a - high.astype(F32)).astype(BF)


def mm_fine(a, b):
    ah, al = split(a)
    bh, bl = split(b)
    return mm(ah, bh) + (mm(ah, bl) + mm(al, bh))


def unit_lower_inverses(systems, rows, cols):
    gap = rows ^ cols
    below = rows > cols
    unit = jnp.where(rows == cols, 1.0, 0.0)
    found = [unit - jnp.where(below & (gap < 2), a, 0.0) for a in systems]
    size = 2
    while size < systems[0].shape[0]:
        mask = below & (gap >= size) & (gap < 2 * size)
        inner = [mm_fine(jnp.where(mask, a, 0.0), t) for a, t in zip(systems, found)]
        found = [t - mm_fine(t, m) for t, m in zip(found, inner)]
        size *= 2
    return found


def block_tables(g_col, g_row, rows, cols):
    lower = rows >= cols
    return jnp.where(lower, jnp.exp(jnp.where(lower, g_col - g_row, 0.0)), 0.0)


def forward_kernel(heads, q_ref, k_ref, v_ref, beta_ref, open_ref, close_ref, gc_ref, gr_ref,
                   o_ref, e_ref, t_ref, z_ref, end_ref, carry):
    step = pl.program_id(0)
    rows = lax.broadcasted_iota(jnp.int32, (BLOCK, BLOCK), 0)
    cols = lax.broadcasted_iota(jnp.int32, (BLOCK, BLOCK), 1)

    @pl.when(step == 0)
    def _():
        unit = (lax.broadcasted_iota(jnp.int32, (DK, DK), 0) == lax.broadcasted_iota(jnp.int32, (DK, DK), 1)).astype(F32)
        for h in range(heads):
            carry[h, :, :DV] = jnp.zeros((DK, DV), F32)
            carry[h, :, DV:] = unit

    tables, systems = [], []
    for h in range(heads):
        k = k_ref[:, h * DK:(h + 1) * DK]
        table = block_tables(gc_ref[:, h:h + 1], gr_ref[0, h:h + 1, :], rows, cols)
        tables.append(table)
        systems.append(jnp.where(rows > cols, beta_ref[:, h:h + 1] * table * mm_nt(k, k), 0.0))
    inverses = unit_lower_inverses(systems, rows, cols)
    for h in range(heads):
        q = q_ref[:, h * DK:(h + 1) * DK]
        k = k_ref[:, h * DK:(h + 1) * DK]
        v = v_ref[:, h * DV:(h + 1) * DV]
        beta, opening, closing = beta_ref[:, h:h + 1], open_ref[:, h:h + 1], close_ref[:, h:h + 1]
        low_t = inverses[h].astype(BF)
        t_ref[0, h] = low_t
        u = mm(low_t, beta * v.astype(F32))
        w = mm(low_t, (beta * opening) * k.astype(F32))
        scores = mm_nt(q, k) * tables[h]
        state = carry[h]
        low_state = state.astype(BF)
        z_ref[0, h] = low_state
        reach = mm(jnp.concatenate([w.astype(BF), (opening * q.astype(F32)).astype(BF)], axis=0), low_state)
        c = jnp.concatenate([u, jnp.zeros((BLOCK, DK), F32)], axis=1) - reach[:BLOCK]
        low_c = c.astype(BF)
        out = reach[BLOCK:] + mm(scores, low_c)
        o_ref[:, h * DV:(h + 1) * DV] = out[:, :DV]
        e_ref[:, h * DK:(h + 1) * DK] = out[:, DV:].astype(BF)
        new = opening[BLOCK - 1:BLOCK] * state + mm_tn(closing * k.astype(F32), low_c)
        carry[h] = new
        end_ref[h] = new


def forward_blocks(q, k, v, beta, opening, closing, g_col, g_row, heads):
    rows = q.shape[0]
    nb = rows // BLOCK
    row = lambda width: pl.BlockSpec((BLOCK, width), lambda i: (i, 0))
    return pl.pallas_call(
        functools.partial(forward_kernel, heads),
        grid=(nb,),
        in_specs=[row(heads * DK), row(heads * DK), row(heads * DV), row(heads), row(heads), row(heads), row(heads),
                  pl.BlockSpec((1, heads, BLOCK), lambda i: (i, 0, 0))],
        out_specs=[row(heads * DV), row(heads * DK),
                   pl.BlockSpec((1, heads, BLOCK, BLOCK), lambda i: (i, 0, 0, 0)),
                   pl.BlockSpec((1, heads, DK, DV + DK), lambda i: (i, 0, 0, 0)),
                   pl.BlockSpec((heads, DK, DV + DK), lambda i: (0, 0, 0))],
        out_shape=[jax.ShapeDtypeStruct((rows, heads * DV), F32), jax.ShapeDtypeStruct((rows, heads * DK), BF),
                   jax.ShapeDtypeStruct((nb, heads, BLOCK, BLOCK), BF),
                   jax.ShapeDtypeStruct((nb, heads, DK, DV + DK), BF),
                   jax.ShapeDtypeStruct((heads, DK, DV + DK), F32)],
        scratch_shapes=[pltpu.VMEM((heads, DK, DV + DK), F32)],
        compiler_params=pltpu.CompilerParams(vmem_limit_bytes=48 * 2**20),
    )(q, k, v, beta, opening, closing, g_col, g_row)


def finish_kernel(heads, o_ref, e_ref, s_ref, gate_ref, live_ref, gain_ref, m_ref):
    live = live_ref[...]
    gain = gain_ref[...]
    for h in range(heads):
        vs = slice(h * DV, (h + 1) * DV)
        y = (o_ref[:, vs] + mm(e_ref[:, h * DK:(h + 1) * DK], s_ref[h])) * live
        r = lax.rsqrt(jnp.mean(y * y, axis=1, keepdims=True) + EPS)
        gate = gate_ref[:, vs]
        m_ref[:, vs] = (y * r * gain * (gate * jax.nn.sigmoid(gate))).astype(BF)


def finish(o, e, entry, gate, live, gain, heads, tile=128):
    rows = o.shape[0]
    row = lambda width: pl.BlockSpec((tile, width), lambda i: (i, 0))
    return pl.pallas_call(
        functools.partial(finish_kernel, heads),
        grid=(rows // tile,),
        in_specs=[row(heads * DV), row(heads * DK), pl.BlockSpec((heads, DK, DV), lambda i: (0, 0, 0)), row(heads * DV),
                  row(1), pl.BlockSpec((1, DV), lambda i: (0, 0))],
        out_specs=row(heads * DV),
        out_shape=jax.ShapeDtypeStruct((rows, heads * DV), BF),
        compiler_params=pltpu.CompilerParams(vmem_limit_bytes=48 * 2**20),
    )(o, e, entry, gate, live, gain)


def unfinish_kernel(heads, o_ref, e_ref, s_ref, gate_ref, live_ref, gain_ref, gm_ref, go_ref, gg_ref, ggain_ref, direct_ref):
    @pl.when(pl.program_id(0) == 0)
    def _():
        ggain_ref[...] = jnp.zeros_like(ggain_ref)
        direct_ref[...] = jnp.zeros_like(direct_ref)

    live = live_ref[...]
    gain = gain_ref[...]
    total = jnp.zeros((1, DV), F32)
    for h in range(heads):
        vs = slice(h * DV, (h + 1) * DV)
        e = e_ref[:, h * DK:(h + 1) * DK]
        y = (o_ref[:, vs] + mm(e, s_ref[h])) * live
        r = lax.rsqrt(jnp.mean(y * y, axis=1, keepdims=True) + EPS)
        gate = gate_ref[:, vs]
        sig = jax.nn.sigmoid(gate)
        act = gate * sig
        gm = gm_ref[:, vs]
        unit = y * r
        gn = gm * act
        total = total + jnp.sum(gn * unit, axis=0, keepdims=True)
        gn = gn * gain
        gg_ref[:, vs] = (gm * unit * gain * (sig * (1.0 + gate * (1.0 - sig)))).astype(BF)
        go = (r * (gn - unit * jnp.mean(gn * unit, axis=1, keepdims=True)) * live).astype(BF)
        go_ref[:, vs] = go
        direct_ref[h] += mm_tn(e, go)
    ggain_ref[...] += total


def unfinish(o, e, entry, gate, live, gain, gm, heads, tile=128):
    rows = o.shape[0]
    row = lambda width: pl.BlockSpec((tile, width), lambda i: (i, 0))
    return pl.pallas_call(
        functools.partial(unfinish_kernel, heads),
        grid=(rows // tile,),
        in_specs=[row(heads * DV), row(heads * DK), pl.BlockSpec((heads, DK, DV), lambda i: (0, 0, 0)), row(heads * DV),
                  row(1), pl.BlockSpec((1, DV), lambda i: (0, 0)), row(heads * DV)],
        out_specs=[row(heads * DV), row(heads * DV), pl.BlockSpec((1, DV), lambda i: (0, 0)),
                   pl.BlockSpec((heads, DK, DV), lambda i: (0, 0, 0))],
        out_shape=[jax.ShapeDtypeStruct((rows, heads * DV), BF), jax.ShapeDtypeStruct((rows, heads * DV), BF),
                   jax.ShapeDtypeStruct((1, DV), F32), jax.ShapeDtypeStruct((heads, DK, DV), F32)],
        compiler_params=pltpu.CompilerParams(vmem_limit_bytes=48 * 2**20),
    )(o, e, entry, gate, live, gain, gm)


def backward_kernel(heads, q_ref, k_ref, v_ref, beta_ref, open_ref, close_ref, gc_ref, gr_ref, t_ref, z_ref, go_ref,
                    s_ref, exit_ref, dq_ref, dk_ref, dv_ref, db_ref, dg_ref, carry):
    rows = lax.broadcasted_iota(jnp.int32, (BLOCK, BLOCK), 0)
    cols = lax.broadcasted_iota(jnp.int32, (BLOCK, BLOCK), 1)
    last = lax.broadcasted_iota(jnp.int32, (BLOCK, 1), 0) == BLOCK - 1

    @pl.when(pl.program_id(0) == 0)
    def _():
        carry[...] = exit_ref[...]

    for h in range(heads):
        q = q_ref[:, h * DK:(h + 1) * DK]
        k = k_ref[:, h * DK:(h + 1) * DK]
        v = v_ref[:, h * DV:(h + 1) * DV]
        qf, kf, vf = q.astype(F32), k.astype(F32), v.astype(F32)
        beta, opening, closing = beta_ref[:, h:h + 1], open_ref[:, h:h + 1], close_ref[:, h:h + 1]
        gamma = opening[BLOCK - 1:BLOCK]
        table = block_tables(gc_ref[:, h:h + 1], gr_ref[0, h:h + 1, :], rows, cols)
        strict = rows > cols
        kk = mm_nt(k, k)
        scores = mm_nt(q, k) * table
        low_t = t_ref[0, h]
        u = mm(low_t, beta * vf)
        w = mm(low_t, (beta * opening) * kf)
        low_w = w.astype(BF)
        state = z_ref[0, h, :, :DV].astype(F32) + mm(z_ref[0, h, :, DV:], s_ref[h])
        low_s = state.astype(BF)
        c = u - mm(low_w, low_s)
        low_c = c.astype(BF)
        go = go_ref[:, h * DV:(h + 1) * DV]
        g = carry[h]
        low_g = g.astype(BF)
        low_ck = (closing * kf).astype(BF)
        low_oq = (opening * qf).astype(BF)
        dc = mm_tn(scores, go) + mm(low_ck, low_g)
        low_dc = dc.astype(BF)
        both = jnp.concatenate([go, low_dc], axis=0)
        carry[h] = gamma * g + mm_tn(jnp.concatenate([low_oq, -low_w], axis=0), both)
        dkeyed = mm_nt(low_c, low_g)
        dgamma = jnp.sum(jnp.sum(state * g, axis=1, keepdims=True), axis=0, keepdims=True)
        dscore = jnp.where(rows >= cols, mm_nt(go, low_c), 0.0)
        back = mm_nt(both, low_s)
        doq, dw = back[:BLOCK], -back[BLOCK:]
        drv = mm_tn(low_t, low_dc)
        drw = mm_tn(low_t, dw)
        low_drv, low_drw = drv.astype(BF), drw.astype(BF)
        da = jnp.where(strict, -(mm_nt(low_drv, u) + mm_nt(low_drw, low_w)), 0.0)
        dat = da * table
        dkk = (beta * dat).astype(BF)
        dqk = (dscore * table).astype(BF)
        dq_ref[:, h * DK:(h + 1) * DK] = opening * doq + mm(dqk, k)
        dk_ref[:, h * DK:(h + 1) * DK] = (mm_tn(dqk, q) + mm(dkk, k) + mm_tn(dkk, k) + closing * dkeyed
                                          + (beta * opening) * drw)
        dv_ref[:, h * DV:(h + 1) * DV] = beta * drv
        rk = jnp.sum(drw * kf, axis=1, keepdims=True)
        atk = dat * kk
        db_ref[:, h:h + 1] = (jnp.sum(drv * vf, axis=1, keepdims=True) + opening * rk
                              + jnp.sum(atk, axis=1, keepdims=True))
        dopen = opening * (jnp.sum(doq * qf, axis=1, keepdims=True) + beta * rk)
        dclose = closing * jnp.sum(dkeyed * kf, axis=1, keepdims=True)
        e = dscore * scores + beta * atk
        by_col = lax.dot_general(e, jnp.ones((BLOCK, 8), F32), (((0,), (0,)), ((), ())),
                                 precision=lax.Precision.HIGHEST, preferred_element_type=F32)[:, :1]
        dg = jnp.sum(e, axis=1, keepdims=True) - by_col + dopen - dclose
        dg = dg + jnp.where(last, jnp.sum(dclose, axis=0, keepdims=True) + dgamma * gamma, 0.0)
        dg_ref[:, h:h + 1] = dg


def backward_blocks(q, k, v, beta, opening, closing, g_col, g_row, t, z, go, entry, leaving, heads):
    rows = q.shape[0]
    nb = rows // BLOCK
    row = lambda width: pl.BlockSpec((BLOCK, width), lambda i: (nb - 1 - i, 0))
    whole = pl.BlockSpec((heads, DK, DV), lambda i: (0, 0, 0))
    return pl.pallas_call(
        functools.partial(backward_kernel, heads),
        grid=(nb,),
        in_specs=[row(heads * DK), row(heads * DK), row(heads * DV), row(heads), row(heads), row(heads), row(heads),
                  pl.BlockSpec((1, heads, BLOCK), lambda i: (nb - 1 - i, 0, 0)),
                  pl.BlockSpec((1, heads, BLOCK, BLOCK), lambda i: (nb - 1 - i, 0, 0, 0)),
                  pl.BlockSpec((1, heads, DK, DV + DK), lambda i: (nb - 1 - i, 0, 0, 0)),
                  row(heads * DV), whole, whole],
        out_specs=[row(heads * DK), row(heads * DK), row(heads * DV), row(heads), row(heads)],
        out_shape=[jax.ShapeDtypeStruct((rows, heads * DK), F32), jax.ShapeDtypeStruct((rows, heads * DK), F32),
                   jax.ShapeDtypeStruct((rows, heads * DV), F32), jax.ShapeDtypeStruct((rows, heads), F32),
                   jax.ShapeDtypeStruct((rows, heads), F32)],
        scratch_shapes=[pltpu.VMEM((heads, DK, DV), F32)],
        compiler_params=pltpu.CompilerParams(vmem_limit_bytes=48 * 2**20),
    )(q, k, v, beta, opening, closing, g_col, g_row, t, z, go, entry, leaving)


def block_decays(log_decay, flags, heads):
    rows = log_decay.shape[0]
    nb = rows // BLOCK
    blocked = log_decay.reshape(nb, BLOCK, heads)
    run = jnp.cumsum(blocked, axis=1)
    opening = flags[:, None, None] * jnp.exp(run)
    closing = jnp.exp(run[:, -1:] - run)
    flat = lambda a: a.reshape(rows, heads)
    return flat(opening), flat(closing), flat(run), run.transpose(0, 2, 1)


CONV = 4


def rms_norm(value, gain):
    return value * lax.rsqrt(jnp.mean(value * value, axis=-1, keepdims=True) + EPS) * gain


def unit_rows(value):
    return value * lax.rsqrt(jnp.sum(value * value, axis=-1, keepdims=True) + EPS)


def rounded(value):
    return lax.optimization_barrier(value.astype(BF)).astype(F32)


def from_behind(value, axis, steps):
    count = lax.axis_size(axis)
    initial, last = (max(0, -steps), min(count, count - steps))
    return lax.ppermute(value, axis, [(source, source + steps) for source in range(initial, last)])


def turn(value, k):
    count = lax.axis_size("wide")
    if k % (count // 2) == 0:
        return value
    return lax.ppermute(value, "wide", [(w, (w + 2 * k) % count) for w in range(count)])


def across(value, axis, bit):
    return lax.ppermute(value, axis, [(i, i ^ bit) for i in range(lax.axis_size(axis))])


def gather_wide(value):
    places = lax.axis_size("wide") // 2
    own = [turn(value, k) for k in range(places)]
    return [piece for part in own for piece in (part, across(part, "wide", 1))]


def scatter_wide(parts):
    places = lax.axis_size("wide") // 2
    own = [(parts[2 * k].astype(F32) + across(parts[2 * k + 1], "wide", 1).astype(F32)) for k in range(places)]
    total = own[0]
    for k in range(1, places):
        total = total + turn(own[k].astype(BF), places - k).astype(F32)
    return total


def relative(value, axis):
    count = lax.axis_size("wide")
    me = lax.axis_index("wide")
    place, side = me // 2, me % 2
    size = value.shape[axis] // count
    pieces = [
        lax.dynamic_slice_in_dim(value, (2 * ((place - k) % (count // 2)) + (side ^ s)) * size, size, axis)
        for k in range(count // 2) for s in range(2)
    ]
    return jnp.concatenate(pieces, axis=axis)


def gather_narrow(value):
    near = across(value, "narrow", 1)
    return [value, near, across(value, "narrow", 2), across(near, "narrow", 2)]


def scatter_narrow(parts):
    first = parts[0].astype(F32) + across(parts[1], "narrow", 1).astype(F32)
    second = (parts[2].astype(F32) + across(parts[3], "narrow", 1).astype(F32)).astype(parts[2].dtype)
    return first + across(second, "narrow", 2).astype(F32)


def blocks_of(value, axis, count):
    me = lax.axis_index("narrow")
    size = value.shape[axis] // count
    return [lax.dynamic_slice_in_dim(value, (me ^ j) * size, size, axis) for j in range(count)]


def placed(pieces, axis):
    me = lax.axis_index("narrow")
    size = pieces[0].shape[axis]
    shape = list(pieces[0].shape)
    shape[axis] = size * len(pieces)
    whole = jnp.zeros(shape, pieces[0].dtype)
    for j, piece in enumerate(pieces):
        whole = lax.dynamic_update_slice_in_dim(whole, piece, (me ^ j) * size, axis)
    return whole


def sum_all(value, axis):
    bit = 1
    while bit < lax.axis_size(axis):
        value = value + across(value, axis, bit)
        bit *= 2
    return value


def sequence_tables(doc_lengths, first_row, row_count, block_size):
    padded = (doc_lengths + block_size - 1) // block_size * block_size
    seq_ends = jnp.cumsum(padded)
    seq_starts = seq_ends - padded
    row_places = first_row + jnp.arange(row_count, dtype=jnp.int32)
    inside_mask = (row_places[:, None] >= seq_starts[None, :]) & (row_places[:, None] < seq_ends[None, :])
    live_mask = jnp.any(inside_mask & (row_places[:, None] < (seq_starts + doc_lengths)[None, :]), axis=1)
    row_start = jnp.sum(jnp.where(inside_mask, seq_starts[None, :], 0), axis=1)
    block_heads = row_places[::block_size]
    fresh_block = jnp.any(block_heads[:, None] == seq_starts[None, :], axis=1)
    return live_mask.astype(F32), row_start, row_places, jnp.where(fresh_block, 0.0, 1.0).astype(F32)


def short_conv(mixed_rows, rim_rows, conv_weight, row_start, row_places):
    row_count = mixed_rows.shape[0]
    taps_count = conv_weight.shape[0]
    extended = jnp.concatenate([rim_rows, mixed_rows], axis=0)
    running_sum = jnp.zeros_like(mixed_rows)
    for tap_index in range(taps_count):
        reach_back = taps_count - 1 - tap_index
        within = (row_places - reach_back >= row_start).astype(F32)
        running_sum = running_sum + conv_weight[tap_index] * extended[tap_index:tap_index + row_count] * within[:, None]
    return jax.nn.silu(running_sum)


def split_heads(active, decay_part, beta_part, a_log, dt_bias, live_rows):
    row_count = active.shape[0]
    head_count = a_log.shape[0]
    key_width = head_count * DK
    queries = unit_rows(active[:, :key_width].reshape(row_count, head_count, DK)) * DK ** (-0.5)
    key_rows = unit_rows(active[:, key_width:2 * key_width].reshape(row_count, head_count, DK))
    value_rows = active[:, 2 * key_width:]
    beta_rows = jax.nn.sigmoid(beta_part) * live_rows[:, None]
    log_decay = -jnp.exp(a_log) * jax.nn.softplus(decay_part + dt_bias)
    flat = lambda a: a.reshape(row_count, key_width)
    return flat(queries), flat(key_rows), value_rows, beta_rows, log_decay


def contract_rows(left, right):
    return lax.dot_general(left, right, (((0,), (0,)), ((), ())), preferred_element_type=F32)


def contract_cols(left, right):
    return lax.dot_general(left, right, (((1,), (1,)), ((), ())), preferred_element_type=F32)


def heads_dot(left, right):
    return jnp.einsum("hij,hjk->hik", left, right, preferred_element_type=F32)


def heads_dot_t(left, right):
    return jnp.einsum("hji,hjk->hik", left, right, preferred_element_type=F32)


def pick(value, side):
    half = value.shape[0] // 2
    return lax.dynamic_slice_in_dim(value, side * half, half, 0)


def join_halves(own, other, side):
    return jnp.concatenate([jnp.where(side == 0, own, other), jnp.where(side == 0, other, own)], axis=0)


def entering(end, place, side):
    places = lax.axis_size("wide") // 2
    mine = end.astype(BF)
    theirs = across(mine, "wide", 1)
    early = jnp.where(side == 0, mine, theirs)
    late = jnp.where(side == 0, theirs, mine)
    early_half, late_half = pick(early, side), pick(late, side)
    joined = heads_dot(late_half[:, :, DV:], early_half)
    joined = jnp.concatenate([joined[:, :, :DV] + late_half[:, :, :DV].astype(F32), joined[:, :, DV:]], axis=2).astype(BF)
    turned = [turn(joined, k) for k in range(places)]
    state = jnp.zeros(joined.shape[:2] + (DV,), F32)
    for k in range(places - 1, 0, -1):
        longer = heads_dot(turned[k][:, :, DV:], state.astype(BF)) + turned[k][:, :, :DV].astype(F32)
        state = jnp.where(place >= k, longer, state)
    state = state.astype(BF)
    state = join_halves(state, across(state, "wide", 1), side)
    after = (heads_dot(theirs[:, :, DV:], state) + theirs[:, :, :DV].astype(F32)).astype(BF)
    entry = jnp.where(side == 0, state, after)
    return entry, (mine[:, :, DV:], theirs[:, :, DV:], [t[:, :, DV:] for t in turned])


def leaving(direct, maps, place, side):
    mine_map, their_map, turned_maps = maps
    places = len(turned_maps)
    mine = direct.astype(BF)
    theirs = across(mine, "wide", 1)
    early = jnp.where(side == 0, mine, theirs)
    late = jnp.where(side == 0, theirs, mine)
    early_map = jnp.where(side == 0, mine_map, their_map)
    joined = (heads_dot_t(pick(early_map, side), pick(late, side)) + pick(early, side).astype(F32)).astype(BF)
    turned = [turn(joined, k) for k in range(places)]
    state = jnp.zeros(joined.shape, F32)
    for k in range(1, places):
        longer = heads_dot_t(turned_maps[k], state.astype(BF)) + turned[k].astype(F32)
        state = jnp.where(k > place, longer, state)
    state = state.astype(BF)
    state = join_halves(state, across(state, "wide", 1), side)
    before = (heads_dot_t(their_map, state) + theirs.astype(F32)).astype(BF)
    return jnp.where(side == 1, state, before).astype(F32)


def shards(block_input, gain_attn, w_query, w_key, w_value, w_gate_out, w_decay, w_beta, conv_query, conv_key,
           conv_value, a_log, dt_bias, out_gain, w_out, gain_mlp, w_gate, w_up, w_down, doc_lengths, cotangent):
    row_count = block_input.shape[0]
    quarter = cotangent.shape[0]
    heads = a_log.shape[0]
    narrow = lax.axis_size("narrow")
    wide_index = lax.axis_index("wide")
    place, side = wide_index // 2, wide_index % 2
    live_rows, row_start, row_places, flags = sequence_tables(doc_lengths, wide_index * row_count, row_count, BLOCK)
    live_col = live_rows[:, None]
    gain_row = out_gain[None, :]
    key_width, value_width = heads * DK, heads * DV

    w_first = jnp.concatenate([w_query, w_key, w_value, w_decay, w_beta], axis=1)
    first = jnp.concatenate(gather_wide(w_first), axis=0)
    gate_weight = jnp.concatenate(gather_wide(w_gate_out), axis=0)
    out_weight = jnp.concatenate(gather_wide(w_out), axis=0)
    cot_parts = gather_wide(cotangent)

    input_rel = relative(block_input, 1).astype(F32)
    gain_rel = relative(gain_attn, 0)
    normed, attn_norm_back = jax.vjp(rms_norm, input_rel, gain_rel)
    normed_low = normed.astype(BF)
    projected = jnp.dot(normed_low, first, preferred_element_type=F32)
    mixed_width = 2 * key_width + value_width
    mixed_low = projected[:, :mixed_width].astype(BF)
    decay_part = projected[:, mixed_width:mixed_width + heads]
    beta_part = projected[:, mixed_width + heads:]
    rim_rows = from_behind(mixed_low[row_count - (CONV - 1):], "wide", 1)
    conv_weight = jnp.concatenate([conv_query, conv_key, conv_value], axis=1)

    def prepare(mixed_rows, rim_in, decay_in, beta_in, conv_in, a_log_in, dt_in):
        active = short_conv(mixed_rows, rim_in, conv_in, row_start, row_places)
        return split_heads(active, decay_in, beta_in, a_log_in, dt_in, live_rows)

    prepared, prepare_back = jax.vjp(prepare, mixed_low.astype(F32), rim_rows.astype(F32), decay_part, beta_part,
                                     conv_weight, a_log, dt_bias)
    queries, keys, values = [a.astype(BF) for a in prepared[:3]]
    beta_rows, log_decay = prepared[3:]
    opening, closing, run_col, run_row = block_decays(log_decay, flags, heads)
    local_out, reach, inverses, states, end = forward_blocks(queries, keys, values, beta_rows, opening, closing, run_col,
                                                             run_row, heads)
    entry, maps = entering(end, place, side)
    gate_rows = jnp.dot(normed_low, gate_weight, preferred_element_type=F32)
    mixer_low = finish(local_out, reach, entry, gate_rows, live_col, gain_row, heads)
    head_part = contract_cols(mixer_low, out_weight)
    own_rel = scatter_narrow(blocks_of(head_part, 0, narrow))
    own_rows = relative(own_rel, 1) + lax.dynamic_slice_in_dim(
        block_input, lax.axis_index("narrow") * quarter, quarter, 0).astype(F32)
    mlp_normed, mlp_norm_back = jax.vjp(rms_norm, own_rows, gain_mlp)
    mlp_low = mlp_normed.astype(BF)
    gathered_rows = jnp.concatenate(gather_wide(mlp_low), axis=0)
    gathered_cot = jnp.concatenate(cot_parts, axis=0)
    gate_pre = jnp.dot(gathered_rows, w_gate, preferred_element_type=F32)
    up_pre = jnp.dot(gathered_rows, w_up, preferred_element_type=F32)
    gate_sig = jax.nn.sigmoid(gate_pre)
    gate_act = gate_pre * gate_sig
    hidden_low = (gate_act * up_pre).astype(BF)
    grad_hidden = contract_cols(gathered_cot, w_down)
    grad_gate_low = (grad_hidden * up_pre * gate_sig * (1.0 + gate_pre * (1.0 - gate_sig))).astype(BF)
    grad_up_low = (grad_hidden * gate_act).astype(BF)
    grad_rows = (contract_cols(grad_gate_low, w_gate) + contract_cols(grad_up_low, w_up)).astype(BF)
    row_blocks = lambda a: [a[j * quarter:(j + 1) * quarter] for j in range(a.shape[0] // quarter)]
    grad_mlp_normed = scatter_wide(row_blocks(grad_rows))
    grad_own_norm, grad_gain_mlp = mlp_norm_back(grad_mlp_normed)
    grad_own = cotangent.astype(F32) + grad_own_norm
    grad_attn_low = placed(gather_narrow(grad_own.astype(BF)), 0)
    grad_attn_rel = relative(grad_attn_low, 1)

    down_rows = jnp.dot(hidden_low, w_down, preferred_element_type=F32).astype(BF)
    output = (own_rows + scatter_wide(row_blocks(down_rows))).astype(BF)
    grad_w_down = contract_rows(hidden_low, gathered_cot).astype(BF)
    grad_w_gate = contract_rows(gathered_rows, grad_gate_low).astype(BF)
    grad_w_up = contract_rows(gathered_rows, grad_up_low).astype(BF)
    share_gate = scatter_narrow(blocks_of(grad_w_gate, 0, narrow))
    share_up = scatter_narrow(blocks_of(grad_w_up, 0, narrow))
    share_down = scatter_narrow(blocks_of(grad_w_down, 1, narrow))

    grad_mixer = jnp.dot(grad_attn_rel, out_weight, preferred_element_type=F32)
    grad_outputs, grad_gate_rows, grad_out_gain, direct = unfinish(local_out, reach, entry, gate_rows, live_col, gain_row,
                                                                   grad_mixer, heads)
    exit_grad = leaving(direct, maps, place, side)
    grad_w_out = contract_rows(grad_attn_rel, mixer_low).astype(BF)
    grad_w_gate_out = contract_rows(normed_low, grad_gate_rows).astype(BF)
    wide_count = lax.axis_size("wide")
    depth = w_query.shape[0]
    depth_blocks = lambda a: [a[j * depth:(j + 1) * depth] for j in range(wide_count)]
    sum_w_out = scatter_wide(depth_blocks(grad_w_out))
    sum_w_gate_out = scatter_wide(depth_blocks(grad_w_gate_out))

    grad_q, grad_k, grad_v, grad_beta, grad_run = backward_blocks(queries, keys, values, beta_rows, opening, closing,
                                                                  run_col, run_row, inverses, states, grad_outputs,
                                                                  entry, exit_grad, heads)
    nb = row_count // BLOCK
    grad_decay = lax.cumsum(grad_run.reshape(nb, BLOCK, heads), axis=1, reverse=True).reshape(row_count, heads)
    grad_mixed, grad_rim, grad_decay_part, grad_beta_part, grad_conv, grad_a_log, grad_dt = prepare_back(
        (grad_q, grad_k, grad_v, grad_beta, grad_decay))
    grad_next = from_behind(grad_rim, "wide", -1)
    grad_mixed = grad_mixed.at[row_count - (CONV - 1):].add(grad_next)
    grad_first = jnp.concatenate([grad_mixed, grad_decay_part, grad_beta_part], axis=1).astype(BF)
    grad_projection = contract_rows(normed_low, grad_first).astype(BF)
    grad_normed = contract_cols(grad_first, first) + contract_cols(grad_gate_rows, gate_weight)
    grad_input_part, grad_gain_rel = attn_norm_back(grad_normed)
    sum_first = scatter_wide(depth_blocks(grad_projection))
    bounds = [0, key_width, 2 * key_width, mixed_width, mixed_width + heads, mixed_width + 2 * heads]
    sums = [sum_first[:, bounds[i]:bounds[i + 1]] for i in range(5)]
    grad_input = relative(scatter_narrow(blocks_of(grad_input_part.astype(BF), 0, narrow)), 1) + grad_own

    columns = mixed_width
    head_sums = jnp.concatenate([grad_conv.reshape(-1), grad_a_log, grad_dt])
    whole_sums = jnp.concatenate([relative(grad_gain_rel, 0), grad_gain_mlp, grad_out_gain[0]])
    small = sum_all(jnp.concatenate([head_sums, whole_sums]), "wide")
    parts = small[:head_sums.shape[0]]
    whole_sums = sum_all(small[head_sums.shape[0]:], "narrow")
    every = placed([p[None] for p in gather_narrow(parts)], 0)
    conv_all = every[:, :CONV * columns].reshape(narrow, CONV, columns).transpose(1, 0, 2)
    conv_parts = [conv_all[:, :, lo:hi].reshape(CONV, -1) for lo, hi in
                  ((0, key_width), (key_width, 2 * key_width), (2 * key_width, columns))]
    d_model = gain_attn.shape[0]
    return (
        output, grad_input, whole_sums[:d_model], sums[0], sums[1], sums[2], sum_w_gate_out, sums[3], sums[4],
        conv_parts[0], conv_parts[1], conv_parts[2],
        every[:, CONV * columns:CONV * columns + heads].reshape(-1), every[:, CONV * columns + heads:].reshape(-1),
        whole_sums[2 * d_model:], sum_w_out, whole_sums[d_model:2 * d_model], share_gate, share_up, share_down,
    )


def solution(mesh):
    both = P("wide", "narrow")
    rows = P(("wide", "narrow"), None)
    return jax.shard_map(
        shards,
        mesh=mesh,
        in_specs=(P("wide", None), P(), both, both, both, both, both, both, P(None, "narrow"), P(None, "narrow"),
                  P(None, "narrow"), P("narrow"), P("narrow"), P(), both, P(), P(None, "wide"), P(None, "wide"),
                  P("wide", None), P(), rows),
        out_specs=(rows, rows, P(), both, both, both, both, both, both, P(), P(), P(), P(), P(), P(), both, P(),
                   P("narrow", "wide"), P("narrow", "wide"), both),
        check_vma=False,
    )
```

time: 3320 us -> 1210 us (0.36)
  waiting for transfers between devices: 1520 us -> 695 us
  other arithmetic: 787 us -> 98.3 us
  matrix products: 590 us -> 82.6 us
  local copies, waits for them, and re-layouts: 317 us -> 127 us
  starting transfers between devices: 7.37 us -> 110 us
  Pallas kernels: 0 us -> 67.1 us
  blocking collectives: 51.6 us -> 0 us
    ppermute x0 -> x106, waiting for transfers between devices: none -> 687 us  [the longest x36 355 us: turn(): lax.ppermute(value, 'wide', [(w, (w + 2 * k) % count) for w in range(coun...]
    reduce_scatter x11 -> x0, waiting for transfers between devices: 617 us -> none  [the longest x1 90 us: shards(): lax.psum_scatter(grad_w_out.astype(jnp.bfloat16), 'wide', scatter_dimensi...]
    another operation x151 -> x5, other arithmetic: 518 us -> 0.72 us  [the longest x1 0.34 us: shards(): lax.cumsum(grad_run.reshape(nb, BLOCK, heads), axis=1, reverse=True)]
    all_gather x12 -> x0, waiting for transfers between devices: 482 us -> none  [the longest x2 114 us: entering(): pieces = jax.tree.map(lambda part: lax.all_gather(part, axis), value)]
    dot_general x244 -> x16, matrix products: 471 us -> 27.2 us  [the longest x1 5.12 us: shards(): projected = jnp.dot(normed_low, first, preferred_element_type=F32)]
    psum x3 -> x0, waiting for transfers between devices: 335 us -> none  [the longest x2 255 us: shards(): lax.psum((grad_gain_attn, grad_gain_mlp, spread_out(grad_conv[:, :key_wid...]
    ppermute x0 -> x106, starting transfers between devices: none -> 102 us  [the longest x70 57.5 us: across(): lax.ppermute(value, axis, [(i, i ^ bit) for i in range(lax.axis_size(axis...]
    unnamed x30 -> x0, waiting for transfers between devices: 79.2 us -> none
  transfers between devices with their start and end apart: 30 -> 108, of which waited for: 23 -> 55; matrix products, arithmetic and copies ran while one was open for 39% -> 21% of each run, Pallas kernels for 0% -> 5%
where the time goes in v1:
time: 1210 us; the launch traced here: 1180 us
  waiting for transfers between devices  695 us (57%)
  local copies, waits for them, and re-layouts  127 us (10%)
  starting transfers between devices  110 us (9%)
  other arithmetic  98.3 us (8%)
  matrix products  82.6 us (7%)
  Pallas kernels  67.1 us (6%)
    ppermute x36, waiting for transfers between devices, turn(): lax.ppermute(value, 'wide', [(w, (w + 2 * k) % count) for w in range(coun...  355 us
    ppermute x70, waiting for transfers between devices, across(): lax.ppermute(value, axis, [(i, i ^ bit) for i in range(lax.axis_size(axis...  332 us
    unnamed x329, local copies, waits for them, and re-layouts  72 us
    ppermute x70, starting transfers between devices, across(): lax.ppermute(value, axis, [(i, i ^ bit) for i in range(lax.axis_size(axis...  57.5 us
    ppermute x36, starting transfers between devices, turn(): lax.ppermute(value, 'wide', [(w, (w + 2 * k) % count) for w in range(coun...  44.9 us
    dot_general x6, matrix products, contract_cols(): lax.dot_general(left, right, (((1,), (1,)), ((), ())), preferred_element_...  33.8 us
    pallas_call x1, Pallas kernels, backward_blocks(): pl.pallas_call(functools.partial(backward_kernel, heads), grid=(nb,), in_...  32.5 us
    pallas_call x1, Pallas kernels, forward_blocks(): pl.pallas_call(functools.partial(forward_kernel, heads), grid=(nb,), in_s...  25.6 us
  transfers between devices with their start and end apart: 108, of which 55 were waited for; matrix products, arithmetic and copies ran while one was open for 21% of the time, Pallas kernels for 5%

profile of v1, /device:TPU:10, one launch (start us, length us, event | category | flops | bytes accessed | tf_op | source)
XLA Modules:
  0.0 1183.3 jit_solution(2149650534095052726)
XLA Ops:
  42.7 17.3 %collective-permute-done.16 = bf16[256,1024]{1,0:T(8,128)(2,1)} collective-permute-done((bf16[256,1024]{1,0:T(8,128)(2,1)}, bf16[256,1024]{1,0:T(8,128)(2,1)}, u32[]{:S(2)}, u32[]{:S(2)}) %collective-permute-start.16) | collective-permute-done | bytes 524320 | tf_op jit(solution)/shard_map/ppermute | solution.py:318
  61.5 33.0 %collective-permute-done.18 = bf16[256,1024]{1,0:T(8,128)(2,1)} collective-permute-done((bf16[256,1024]{1,0:T(8,128)(2,1)}, bf16[256,1024]{1,0:T(8,128)(2,1)}, u32[]{:S(2)}, u32[]{:S(2)}) %collective-permute-start.18) | collective-permute-done | bytes 524320 | tf_op jit(solution)/shard_map/ppermute | solution.py:318
  109.6 11.2 collective-permute-done.19
  141.1 49.3 %collective-permute-done.25 = bf16[256,1024]{1,0:T(8,128)(2,1)} collective-permute-done((bf16[256,1024]{1,0:T(8,128)(2,1)S(1)}, bf16[256,1024]{1,0:T(8,128)(2,1)}, u32[]{:S(2)}, u32[]{:S(2)}) %collective-permute-start.25) | collective-permute-done | bytes 524320 | tf_op jit(solution)/shard_map/ppermute | solution.py:318
  202.9 36.2 %collective-permute-done.4 = bf16[256,2056]{0,1:T(8,128)(2,1)S(1)} collective-permute-done((bf16[256,2056]{0,1:T(8,128)(2,1)S(1)}, bf16[256,2056]{0,1:T(8,128)(2,1)S(1)}, u32[]{:S(2)}, u32[]{:S(2)}) %collective-permute-start.4) | collective-permute-done | bytes 1052704 | tf_op jit(solution)/shard_map/ppermute | solution.py:322
  239.4 21.3 %collective-permute-done.6 = bf16[256,2056]{0,1:T(8,128)(2,1)S(1)} collective-permute-done((bf16[256,2056]{0,1:T(8,128)(2,1)S(1)}, bf16[256,2056]{0,1:T(8,128)(2,1)S(1)}, u32[]{:S(2)}, u32[]{:S(2)}) %collective-permute-start.6) | collective-permute-done | bytes 1052704 | tf_op jit(solution)/shard_map/ppermute | solution.py:322
  276.9 12.5 %fusion.11 = (f32[512,2048]{1,0:T(8,128)S(1)}, f32[512,2048]{1,0:T(8,128)}) fusion(f32[512]{0:T(512)S(1)} %get-tuple-element.297, f32[512,2048]{1,0:T(8,128)} %slice_convert_fusion.1, f32[2048]{0:T(1024)S(1)} %bitcast.137, f32[512]{0:T(512)S(1)} %get-tuple-element.298, f32[3,2048]{1,0:T(4,128)S(1)} %convert_element_type.467, f32[2048]{0:T(1024)S(1)} %bitcast.139, ...), kind=kLoop, calls=%fused_computation.28 | loop fusion | flops 18874368 | bytes 12648448 | tf_op jit(solution)/shard_map/jvp(jit(silu))/mul | solution.py:410
  310.3 25.6 %shard_map.356 = (f32[512,1024]{1,0:T(8,128)}, bf16[512,512]{1,0:T(8,128)(2,1)S(1)}, bf16[8,4,64,64]{3,2,1,0:T(8,128)(2,1)S(1)}, bf16[8,4,128,384]{3,2,1,0:T(8,128)(2,1)}, f32[4,128,384]{2,1,0:T(8,128)S(1)}) custom-call(bf16[512,512]{1,0:T(8,128)(2,1)S(1)} %get-tuple-element.253.q_ref, bf16[512,512]{1,0:T(8,128)(2,1)S(1)} %get-tuple-element.252.k_ref, ...), custom_call_target="tpu_custom_call" | custom-call | tf_op jit(solution)/shard_map/pallas_call | solution.py:104
  396.2 28.2 %collective-permute-done.47 = bf16[128,2048]{1,0:T(8,128)(2,1)} collective-permute-done((bf16[128,2048]{1,0:T(8,128)(2,1)}, bf16[128,2048]{1,0:T(8,128)(2,1)}, u32[]{:S(2)}, u32[]{:S(2)}) %collective-permute-start.47) | collective-permute-done | bytes 524320 | tf_op jit(solution)/shard_map/ppermute | solution.py:318
  455.6 28.3 %collective-permute-done.33 = bf16[128,2048]{1,0:T(8,128)(2,1)S(1)} collective-permute-done((bf16[128,2048]{1,0:T(8,128)(2,1)S(1)}, bf16[128,2048]{1,0:T(8,128)(2,1)S(1)}, u32[]{:S(2)}, u32[]{:S(2)}) %collective-permute-start.33) | collective-permute-done | bytes 524320 | tf_op jit(solution)/shard_map/ppermute | solution.py:318
  486.1 12.6 %collective-permute-done.34 = bf16[128,2048]{1,0:T(8,128)(2,1)S(1)} collective-permute-done((bf16[128,2048]{1,0:T(8,128)(2,1)S(1)}, bf16[128,2048]{1,0:T(8,128)(2,1)S(1)}, u32[]{:S(2)}, u32[]{:S(2)}) %collective-permute-start.34) | collective-permute-done | bytes 524320 | tf_op jit(solution)/shard_map/ppermute | solution.py:322
  549.3 11.4 collective-permute-done.52
  560.9 11.0 collective-permute-done.54
  572.2 11.0 collective-permute-done.56
  584.0 10.4 collective-permute-done.38
  594.4 11.2 collective-permute-done.40
  605.9 11.0 collective-permute-done.42
  627.1 27.0 %collective-permute-done.53 = bf16[128,2048]{1,0:T(8,128)(2,1)S(1)} collective-permute-done((bf16[128,2048]{1,0:T(8,128)(2,1)S(1)}, bf16[128,2048]{1,0:T(8,128)(2,1)S(1)}, u32[]{:S(2)}, u32[]{:S(2)}) %collective-permute-start.53) | collective-permute-done | bytes 524320 | tf_op jit(solution)/shard_map/ppermute | solution.py:318
  654.7 9.8 collective-permute-done.57
  674.8 13.1 %collective-permute-done.104 = bf16[512,688]{0,1:T(8,128)(2,1)S(1)} collective-permute-done((bf16[512,688]{0,1:T(8,128)(2,1)S(1)}, bf16[512,688]{0,1:T(8,128)(2,1)S(1)}, u32[]{:S(2)}, u32[]{:S(2)}) %collective-permute-start.104) | collective-permute-done | bytes 704544 | tf_op jit(solution)/shard_map/ppermute | solution.py:322
  689.8 13.1 %collective-permute-done.101 = bf16[512,688]{0,1:T(8,128)(2,1)S(1)} collective-permute-done((bf16[512,688]{0,1:T(8,128)(2,1)S(1)}, bf16[512,688]{0,1:T(8,128)(2,1)S(1)}, u32[]{:S(2)}, u32[]{:S(2)}) %collective-permute-start.101) | collective-permute-done | bytes 704544 | tf_op jit(solution)/shard_map/ppermute | solution.py:322
  704.4 9.7 collective-permute-done.59
  714.2 10.8 collective-permute-done.60
  770.8 24.1 %collective-permute-done.65 = bf16[2,128,256]{2,1,0:T(8,128)(2,1)S(1)} collective-permute-done((bf16[2,128,256]{2,1,0:T(8,128)(2,1)S(1)}, bf16[2,128,256]{2,1,0:T(8,128)(2,1)S(1)}, u32[]{:S(2)}, u32[]{:S(2)}) %collective-permute-start.65) | collective-permute-done | bytes 131104 | tf_op jit(solution)/shard_map/ppermute | solution.py:322
  795.6 32.5 %shard_map.359 = (f32[512,512]{1,0:T(8,128)S(1)}, f32[512,512]{1,0:T(8,128)S(1)}, f32[512,1024]{1,0:T(8,128)}, f32[512,4]{1,0:T(8,128)S(1)}, f32[512,4]{1,0:T(8,128)S(1)}) custom-call(bf16[512,512]{1,0:T(8,128)(2,1)S(1)} %copy-done.6, bf16[512,512]{1,0:T(8,128)(2,1)S(1)} %get-tuple-element.252.k_ref, bf16[512,1024]{1,0:T(8,128)(2,1)} %slice.564.v_ref, ...), custom_call_target="tpu_custom_call" | custom-call | tf_op jit(solution)/shard_map/pallas_call | solution.py:265
  898.9 10.9 fusion.3
  949.3 20.2 %collective-permute-done.94 = bf16[256,1024]{1,0:T(8,128)(2,1)S(1)} collective-permute-done((bf16[256,1024]{1,0:T(8,128)(2,1)}, bf16[256,1024]{1,0:T(8,128)(2,1)S(1)}, u32[]{:S(2)}, u32[]{:S(2)}) %collective-permute-start.94) | collective-permute-done | bytes 524320 | tf_op jit(solution)/shard_map/ppermute | solution.py:318
  972.1 32.4 %collective-permute-done.98 = bf16[256,1024]{1,0:T(8,128)(2,1)} collective-permute-done((bf16[256,1024]{1,0:T(8,128)(2,1)}, bf16[256,1024]{1,0:T(8,128)(2,1)}, u32[]{:S(2)}, u32[]{:S(2)}) %collective-permute-start.98) | collective-permute-done | bytes 524320 | tf_op jit(solution)/shard_map/ppermute | solution.py:318
  1042.0 22.6 %collective-permute-done.78 = bf16[256,2056]{0,1:T(8,128)(2,1)S(1)} collective-permute-done((bf16[256,2056]{0,1:T(8,128)(2,1)}, bf16[256,2056]{0,1:T(8,128)(2,1)S(1)}, u32[]{:S(2)}, u32[]{:S(2)}) %collective-permute-start.78) | collective-permute-done | bytes 1052704 | tf_op jit(solution)/shard_map/ppermute | solution.py:322
  1064.8 22.3 %collective-permute-done.80 = bf16[256,2056]{0,1:T(8,128)(2,1)S(1)} collective-permute-done((bf16[256,2056]{0,1:T(8,128)(2,1)S(1)}, bf16[256,2056]{0,1:T(8,128)(2,1)S(1)}, u32[]{:S(2)}, u32[]{:S(2)}) %collective-permute-start.80) | collective-permute-done | bytes 1052704 | tf_op jit(solution)/shard_map/ppermute | solution.py:322
  1103.8 13.4 %collective-permute-done.75 = bf16[256,2056]{0,1:T(8,128)(2,1)S(1)} collective-permute-done((bf16[256,2056]{0,1:T(8,128)(2,1)S(1)}, bf16[256,2056]{0,1:T(8,128)(2,1)S(1)}, u32[]{:S(2)}, u32[]{:S(2)}) %collective-permute-start.75) | collective-permute-done | bytes 1052704 | tf_op jit(solution)/shard_map/ppermute | solution.py:322
  1117.2 52.4 %collective-permute-done.77 = bf16[256,2056]{0,1:T(8,128)(2,1)S(1)} collective-permute-done((bf16[256,2056]{0,1:T(8,128)(2,1)S(1)}, bf16[256,2056]{0,1:T(8,128)(2,1)S(1)}, u32[]{:S(2)}, u32[]{:S(2)}) %collective-permute-start.77) | collective-permute-done | bytes 1052704 | tf_op jit(solution)/shard_map/ppermute | solution.py:318
  (710 shorter events, 524.1 us)
Async XLA Ops:
  5.1 89.4 %collective-permute-start.18 = (bf16[256,1024]{1,0:T(8,128)(2,1)}, bf16[256,1024]{1,0:T(8,128)(2,1)}, u32[]{:S(2)}, u32[]{:S(2)}) collective-permute-start(bf16[256,1024]{1,0:T(8,128)(2,1)} %param.28), channel_id=1, source_target_pairs={{0,24},{4,28},{8,0},{12,4},{16,8},{20,12},{24,16},{28,20},{1,25},{... | collective-permute-start | bytes 1572872 | tf_op jit(solution)/shard_map/ppermute | solution.py:318
  6.9 89.1 %collective-permute-start.21 = (bf16[256,1024]{1,0:T(8,128)(2,1)}, bf16[256,1024]{1,0:T(8,128)(2,1)}, u32[]{:S(2)}, u32[]{:S(2)}) collective-permute-start(bf16[256,1024]{1,0:T(8,128)(2,1)} %param.37), channel_id=1, source_target_pairs={{0,8},{4,12},{8,16},{12,20},{16,24},{20,28},{24,0},{28,4},{1,9},{5... | collective-permute-start | bytes 1572872 | tf_op jit(solution)/shard_map/ppermute | solution.py:318
  37.0 61.6 %collective-permute-start.20 = (bf16[256,1024]{1,0:T(8,128)(2,1)}, bf16[256,1024]{1,0:T(8,128)(2,1)}, u32[]{:S(2)}, u32[]{:S(2)}) collective-permute-start(bf16[256,1024]{1,0:T(8,128)(2,1)} %param.37), channel_id=1, source_target_pairs={{0,4},{4,0},{8,12},{12,8},{16,20},{20,16},{24,28},{28,24},{1,5},{5... | collective-permute-start | bytes 1572872 | tf_op jit(solution)/shard_map/ppermute | solution.py:322
  40.5 58.3 %collective-permute-start.23 = (bf16[256,1024]{1,0:T(8,128)(2,1)}, bf16[256,1024]{1,0:T(8,128)(2,1)}, u32[]{:S(2)}, u32[]{:S(2)}) collective-permute-start(bf16[256,1024]{1,0:T(8,128)(2,1)} %param.37), channel_id=1, source_target_pairs={{0,16},{4,20},{8,24},{12,28},{16,0},{20,4},{24,8},{28,12},{1,17},{... | collective-permute-start | bytes 1572872 | tf_op jit(solution)/shard_map/ppermute | solution.py:318
  102.2 89.6 %collective-permute-start = (bf16[256,2056]{0,1:T(8,128)(2,1)}, bf16[256,2056]{0,1:T(8,128)(2,1)S(1)}, u32[]{:S(2)}, u32[]{:S(2)}) collective-permute-start(bf16[256,2056]{0,1:T(8,128)(2,1)} %concatenate.61), channel_id=1, source_target_pairs={{0,4},{4,0},{8,12},{12,8},{16,20},{20,16},{24,28},{28,24},{1,5},{5... | collective-permute-start | bytes 3158024 | tf_op jit(solution)/shard_map/ppermute | solution.py:322
  109.6 90.7 %collective-permute-start.3 = (bf16[256,2056]{0,1:T(8,128)(2,1)}, bf16[256,2056]{0,1:T(8,128)(2,1)S(1)}, u32[]{:S(2)}, u32[]{:S(2)}) collective-permute-start(bf16[256,2056]{0,1:T(8,128)(2,1)} %concatenate.61), channel_id=1, source_target_pairs={{0,16},{4,20},{8,24},{12,28},{16,0},{20,4},{24,8},{28,12},{1,17},{... | collective-permute-start | bytes 3158024 | tf_op jit(solution)/shard_map/ppermute | solution.py:318
  120.8 81.0 %collective-permute-start.5 = (bf16[256,2056]{0,1:T(8,128)(2,1)}, bf16[256,2056]{0,1:T(8,128)(2,1)S(1)}, u32[]{:S(2)}, u32[]{:S(2)}) collective-permute-start(bf16[256,2056]{0,1:T(8,128)(2,1)} %concatenate.61), channel_id=1, source_target_pairs={{0,24},{4,28},{8,0},{12,4},{16,8},{20,12},{24,16},{28,20},{1,25},{... | collective-permute-start | bytes 3158024 | tf_op jit(solution)/shard_map/ppermute | solution.py:318
  131.9 58.4 %collective-permute-start.25 = (bf16[256,1024]{1,0:T(8,128)(2,1)S(1)}, bf16[256,1024]{1,0:T(8,128)(2,1)}, u32[]{:S(2)}, u32[]{:S(2)}) collective-permute-start(bf16[256,1024]{1,0:T(8,128)(2,1)S(1)} %copy-done.60), channel_id=1, source_target_pairs={{0,24},{4,28},{8,0},{12,4},{16,8},{20,12},{24,16},{28,20},{1,25},{... | collective-permute-start | bytes 1572872 | tf_op jit(solution)/shard_map/ppermute | solution.py:318
  135.7 66.9 %collective-permute-start.2 = (bf16[256,2056]{0,1:T(8,128)(2,1)S(1)}, bf16[256,2056]{0,1:T(8,128)(2,1)S(1)}, u32[]{:S(2)}, u32[]{:S(2)}) collective-permute-start(bf16[256,2056]{0,1:T(8,128)(2,1)S(1)} %collective-permute-done.1), channel_id=1, source_target_pairs={{0,4},{4,0},{8,12},{12,8},{16,20},{20,16},{24,28},{28,24},{1,5},{5... | collective-permute-start | bytes 3158024 | tf_op jit(solution)/shard_map/ppermute | solution.py:322
  190.3 157.2 %collective-permute-start.24 = (bf16[256,1024]{1,0:T(8,128)(2,1)}, bf16[256,1024]{1,0:T(8,128)(2,1)}, u32[]{:S(2)}, u32[]{:S(2)}) collective-permute-start(bf16[256,1024]{1,0:T(8,128)(2,1)} %collective-permute-done.23), channel_id=1, source_target_pairs={{0,4},{4,0},{8,12},{12,8},{16,20},{20,16},{24,28},{28,24},{1,5},{5... | collective-permute-start | bytes 1572872 | tf_op jit(solution)/shard_map/ppermute | solution.py:322
  191.9 173.4 %collective-permute-start.26 = (bf16[256,1024]{1,0:T(8,128)(2,1)}, bf16[256,1024]{1,0:T(8,128)(2,1)}, u32[]{:S(2)}, u32[]{:S(2)}) collective-permute-start(bf16[256,1024]{1,0:T(8,128)(2,1)} %collective-permute-done.25), channel_id=1, source_target_pairs={{0,4},{4,0},{8,12},{12,8},{16,20},{20,16},{24,28},{28,24},{1,5},{5... | collective-permute-start | bytes 1572872 | tf_op jit(solution)/shard_map/ppermute | solution.py:322
  201.8 59.0 %collective-permute-start.6 = (bf16[256,2056]{0,1:T(8,128)(2,1)S(1)}, bf16[256,2056]{0,1:T(8,128)(2,1)S(1)}, u32[]{:S(2)}, u32[]{:S(2)}) collective-permute-start(bf16[256,2056]{0,1:T(8,128)(2,1)S(1)} %collective-permute-done.5), channel_id=1, source_target_pairs={{0,4},{4,0},{8,12},{12,8},{16,20},{20,16},{24,28},{28,24},{1,5},{5... | collective-permute-start | bytes 3158024 | tf_op jit(solution)/shard_map/ppermute | solution.py:322
  535.2 83.2 %collective-permute-start.106 = (bf16[688,512]{1,0:T(8,128)(2,1)S(1)}, bf16[688,512]{1,0:T(8,128)(2,1)S(1)}, u32[]{:S(2)}, u32[]{:S(2)}) collective-permute-start(bf16[688,512]{1,0:T(8,128)(2,1)S(1)} %get-tuple-element.257), channel_id=1, source_target_pairs={{0,1},{1,0},{2,3},{3,2},{4,5},{5,4},{6,7},{7,6},{8,9},{9,8},{10,11... | collective-permute-start | bytes 2113544 | tf_op jit(solution)/shard_map/ppermute | solution.py:322
  538.8 83.0 %collective-permute-start.103 = (bf16[512,688]{0,1:T(8,128)(2,1)S(1)}, bf16[512,688]{0,1:T(8,128)(2,1)S(1)}, u32[]{:S(2)}, u32[]{:S(2)}) collective-permute-start(bf16[512,688]{0,1:T(8,128)(2,1)S(1)} %get-tuple-element.259), channel_id=1, source_target_pairs={{0,1},{1,0},{2,3},{3,2},{4,5},{5,4},{6,7},{7,6},{8,9},{9,8},{10,11... | collective-permute-start | bytes 2113544 | tf_op jit(solution)/shard_map/ppermute | solution.py:322
  754.5 111.0 %collective-permute-start.93 = (bf16[256,1024]{1,0:T(8,128)(2,1)}, bf16[256,1024]{1,0:T(8,128)(2,1)}, u32[]{:S(2)}, u32[]{:S(2)}) collective-permute-start(bf16[256,1024]{1,0:T(8,128)(2,1)} %get-tuple-element.219), channel_id=1, source_target_pairs={{0,4},{4,0},{8,12},{12,8},{16,20},{20,16},{24,28},{28,24},{1,5},{5... | collective-permute-start | bytes 1572872 | tf_op jit(solution)/shard_map/ppermute | solution.py:322
  754.9 112.3 %collective-permute-start.95 = (bf16[256,1024]{1,0:T(8,128)(2,1)}, bf16[256,1024]{1,0:T(8,128)(2,1)}, u32[]{:S(2)}, u32[]{:S(2)}) collective-permute-start(bf16[256,1024]{1,0:T(8,128)(2,1)} %get-tuple-element.218), channel_id=1, source_target_pairs={{0,4},{4,0},{8,12},{12,8},{16,20},{20,16},{24,28},{28,24},{1,5},{5... | collective-permute-start | bytes 1572872 | tf_op jit(solution)/shard_map/ppermute | solution.py:322
  756.6 111.0 %collective-permute-start.97 = (bf16[256,1024]{1,0:T(8,128)(2,1)}, bf16[256,1024]{1,0:T(8,128)(2,1)}, u32[]{:S(2)}, u32[]{:S(2)}) collective-permute-start(bf16[256,1024]{1,0:T(8,128)(2,1)} %get-tuple-element.217), channel_id=1, source_target_pairs={{0,4},{4,0},{8,12},{12,8},{16,20},{20,16},{24,28},{28,24},{1,5},{5... | collective-permute-start | bytes 1572872 | tf_op jit(solution)/shard_map/ppermute | solution.py:322
  770.5 102.2 %collective-permute-start.83 = (bf16[256,1024]{1,0:T(8,128)(2,1)}, bf16[256,1024]{1,0:T(8,128)(2,1)}, u32[]{:S(2)}, u32[]{:S(2)}) collective-permute-start(bf16[256,1024]{1,0:T(8,128)(2,1)} %get-tuple-element.226), channel_id=1, source_target_pairs={{0,4},{4,0},{8,12},{12,8},{16,20},{20,16},{24,28},{28,24},{1,5},{5... | collective-permute-start | bytes 1572872 | tf_op jit(solution)/shard_map/ppermute | solution.py:322
  794.9 81.5 %collective-permute-start.85 = (bf16[256,1024]{1,0:T(8,128)(2,1)}, bf16[256,1024]{1,0:T(8,128)(2,1)}, u32[]{:S(2)}, u32[]{:S(2)}) collective-permute-start(bf16[256,1024]{1,0:T(8,128)(2,1)} %get-tuple-element.225), channel_id=1, source_target_pairs={{0,4},{4,0},{8,12},{12,8},{16,20},{20,16},{24,28},{28,24},{1,5},{5... | collective-permute-start | bytes 1572872 | tf_op jit(solution)/shard_map/ppermute | solution.py:322
  867.2 75.9 %collective-permute-start.92 = (bf16[256,1024]{1,0:T(8,128)(2,1)}, bf16[256,1024]{1,0:T(8,128)(2,1)}, u32[]{:S(2)}, u32[]{:S(2)}) collective-permute-start(bf16[256,1024]{1,0:T(8,128)(2,1)} %get-tuple-element.216), channel_id=1, source_target_pairs={{0,4},{4,0},{8,12},{12,8},{16,20},{20,16},{24,28},{28,24},{1,5},{5... | collective-permute-start | bytes 1572872 | tf_op jit(solution)/shard_map/ppermute | solution.py:322
  867.6 81.7 %collective-permute-start.82 = (bf16[256,1024]{1,0:T(8,128)(2,1)}, bf16[256,1024]{1,0:T(8,128)(2,1)}, u32[]{:S(2)}, u32[]{:S(2)}) collective-permute-start(bf16[256,1024]{1,0:T(8,128)(2,1)} %get-tuple-element.223), channel_id=1, source_target_pairs={{0,4},{4,0},{8,12},{12,8},{16,20},{20,16},{24,28},{28,24},{1,5},{5... | collective-permute-start | bytes 1572872 | tf_op jit(solution)/shard_map/ppermute | solution.py:322
  943.1 61.4 %collective-permute-start.98 = (bf16[256,1024]{1,0:T(8,128)(2,1)}, bf16[256,1024]{1,0:T(8,128)(2,1)}, u32[]{:S(2)}, u32[]{:S(2)}) collective-permute-start(bf16[256,1024]{1,0:T(8,128)(2,1)} %get-tuple-element.221), channel_id=1, source_target_pairs={{0,8},{4,12},{8,16},{12,20},{16,24},{20,28},{24,0},{28,4},{1,9},{5... | collective-permute-start | bytes 1572872 | tf_op jit(solution)/shard_map/ppermute | solution.py:318
  949.3 66.3 %collective-permute-start.84 = (bf16[256,1024]{1,0:T(8,128)(2,1)}, bf16[256,1024]{1,0:T(8,128)(2,1)S(1)}, u32[]{:S(2)}, u32[]{:S(2)}) collective-permute-start(bf16[256,1024]{1,0:T(8,128)(2,1)} %get-tuple-element.227), channel_id=1, source_target_pairs={{0,24},{4,28},{8,0},{12,4},{16,8},{20,12},{24,16},{28,20},{1,25},{... | collective-permute-start | bytes 1572872 | tf_op jit(solution)/shard_map/ppermute | solution.py:318
  969.5 57.4 %collective-permute-start.88 = (bf16[256,1024]{1,0:T(8,128)(2,1)}, bf16[256,1024]{1,0:T(8,128)(2,1)S(1)}, u32[]{:S(2)}, u32[]{:S(2)}) collective-permute-start(bf16[256,1024]{1,0:T(8,128)(2,1)} %get-tuple-element.228), channel_id=1, source_target_pairs={{0,8},{4,12},{8,16},{12,20},{16,24},{20,28},{24,0},{28,4},{1,9},{5... | collective-permute-start | bytes 1572872 | tf_op jit(solution)/shard_map/ppermute | solution.py:318
  972.1 59.4 %collective-permute-start.67 = (bf16[128,2048]{1,0:T(8,128)(2,1)}, bf16[128,2048]{1,0:T(8,128)(2,1)S(1)}, u32[]{:S(2)}, u32[]{:S(2)}) collective-permute-start(bf16[128,2048]{1,0:T(8,128)(2,1)} %get-tuple-element.266), channel_id=1, source_target_pairs={{0,1},{1,0},{2,3},{3,2},{4,5},{5,4},{6,7},{7,6},{8,9},{9,8},{10,11... | collective-permute-start | bytes 1572872 | tf_op jit(solution)/shard_map/ppermute | solution.py:322
  1026.9 60.2 %collective-permute-start.80 = (bf16[256,2056]{0,1:T(8,128)(2,1)S(1)}, bf16[256,2056]{0,1:T(8,128)(2,1)S(1)}, u32[]{:S(2)}, u32[]{:S(2)}) collective-permute-start(bf16[256,2056]{0,1:T(8,128)(2,1)S(1)} %copy-done.56), channel_id=1, source_target_pairs={{0,4},{4,0},{8,12},{12,8},{16,20},{20,16},{24,28},{28,24},{1,5},{5... | collective-permute-start | bytes 3158024 | tf_op jit(solution)/shard_map/ppermute | solution.py:322
  1031.5 66.8 %collective-permute-start.37 = (bf16[128,2048]{1,0:T(8,128)(2,1)S(1)}, bf16[128,2048]{1,0:T(8,128)(2,1)S(1)}, u32[]{:S(2)}, u32[]{:S(2)}) collective-permute-start(bf16[128,2048]{1,0:T(8,128)(2,1)S(1)} %copy-done.61), channel_id=1, source_target_pairs={{0,4},{4,0},{8,12},{12,8},{16,20},{20,16},{24,28},{28,24},{1,5},{5... | collective-permute-start | bytes 1572872 | tf_op jit(solution)/shard_map/ppermute | solution.py:322
  1031.6 66.8 %collective-permute-start.39 = (bf16[128,2048]{1,0:T(8,128)(2,1)S(1)}, bf16[128,2048]{1,0:T(8,128)(2,1)S(1)}, u32[]{:S(2)}, u32[]{:S(2)}) collective-permute-start(bf16[128,2048]{1,0:T(8,128)(2,1)S(1)} %copy-done.59), channel_id=1, source_target_pairs={{0,24},{4,28},{8,0},{12,4},{16,8},{20,12},{24,16},{28,20},{1,25},{... | collective-permute-start | bytes 1572872 | tf_op jit(solution)/shard_map/ppermute | solution.py:318
  1042.0 57.5 %collective-permute-start.41 = (bf16[128,2048]{1,0:T(8,128)(2,1)S(1)}, bf16[128,2048]{1,0:T(8,128)(2,1)S(1)}, u32[]{:S(2)}, u32[]{:S(2)}) collective-permute-start(bf16[128,2048]{1,0:T(8,128)(2,1)S(1)} %copy-done.58), channel_id=1, source_target_pairs={{0,16},{4,20},{8,24},{12,28},{16,0},{20,4},{24,8},{28,12},{1,17},{... | collective-permute-start | bytes 1572872 | tf_op jit(solution)/shard_map/ppermute | solution.py:318
  1098.3 71.3 %collective-permute-start.77 = (bf16[256,2056]{0,1:T(8,128)(2,1)S(1)}, bf16[256,2056]{0,1:T(8,128)(2,1)S(1)}, u32[]{:S(2)}, u32[]{:S(2)}) collective-permute-start(bf16[256,2056]{0,1:T(8,128)(2,1)S(1)} %get-tuple-element.206), channel_id=1, source_target_pairs={{0,24},{4,28},{8,0},{12,4},{16,8},{20,12},{24,16},{28,20},{1,25},{... | collective-permute-start | bytes 3158024 | tf_op jit(solution)/shard_map/ppermute | solution.py:318
  1098.3 71.3 %collective-permute-start.79 = (bf16[256,2056]{0,1:T(8,128)(2,1)S(1)}, bf16[256,2056]{0,1:T(8,128)(2,1)S(1)}, u32[]{:S(2)}, u32[]{:S(2)}) collective-permute-start(bf16[256,2056]{0,1:T(8,128)(2,1)S(1)} %get-tuple-element.208), channel_id=1, source_target_pairs={{0,16},{4,20},{8,24},{12,28},{16,0},{20,4},{24,8},{28,12},{1,17},{... | collective-permute-start | bytes 3158024 | tf_op jit(solution)/shard_map/ppermute | solution.py:318
  1099.4 73.4 %collective-permute-start.81 = (bf16[256,2056]{0,1:T(8,128)(2,1)S(1)}, bf16[256,2056]{0,1:T(8,128)(2,1)S(1)}, u32[]{:S(2)}, u32[]{:S(2)}) collective-permute-start(bf16[256,2056]{0,1:T(8,128)(2,1)S(1)} %get-tuple-element.207), channel_id=1, source_target_pairs={{0,8},{4,12},{8,16},{12,20},{16,24},{20,28},{24,0},{28,4},{1,9},{5... | collective-permute-start | bytes 3158024 | tf_op jit(solution)/shard_map/ppermute | solution.py:318
  (200 other events, 7480.1 us)

commit v2 on v1

v2 whole, which is shorter than its diff:
```python
import functools
import jax
import jax.numpy as jnp
from jax import lax
from jax.experimental import pallas as pl
from jax.experimental.pallas import tpu as pltpu
from jax.sharding import PartitionSpec as P

DK, DV, BLOCK, EPS = 128, 256, 64, 1e-6
BF = jnp.bfloat16
F32 = jnp.float32


def mm(a, b):
    return jnp.dot(a.astype(BF), b.astype(BF), preferred_element_type=F32)


def mm_nt(a, b):
    return lax.dot_general(a.astype(BF), b.astype(BF), (((1,), (1,)), ((), ())), preferred_element_type=F32)


def mm_tn(a, b):
    return lax.dot_general(a.astype(BF), b.astype(BF), (((0,), (0,)), ((), ())), preferred_element_type=F32)


def split(a):
    high = a.astype(BF)
    return high, (a - high.astype(F32)).astype(BF)


def mm_fine(a, b):
    ah, al = split(a)
    bh, bl = split(b)
    return mm(ah, bh) + (mm(ah, bl) + mm(al, bh))


def unit_lower_inverses(systems, rows, cols):
    gap = rows ^ cols
    below = rows > cols
    unit = jnp.where(rows == cols, 1.0, 0.0)
    found = [unit - jnp.where(below & (gap < 2), a, 0.0) for a in systems]
    size = 2
    while size < systems[0].shape[0]:
        mask = below & (gap >= size) & (gap < 2 * size)
        inner = [mm_fine(jnp.where(mask, a, 0.0), t) for a, t in zip(systems, found)]
        found = [t - mm_fine(t, m) for t, m in zip(found, inner)]
        size *= 2
    return found


def block_tables(g_col, g_row, rows, cols):
    lower = rows >= cols
    return jnp.where(lower, jnp.exp(jnp.where(lower, g_col - g_row, 0.0)), 0.0)


def shifted(rows, before, back):
    if back == 0:
        return rows
    return jnp.concatenate([before[8 - back:], rows[:rows.shape[0] - back]], axis=0)


def conv_rows(rows, before, taps):
    count = taps.shape[0]
    total = taps[count - 1:count] * rows
    for back in range(1, count):
        total = total + taps[count - 1 - back:count - back] * shifted(rows, before, back)
    return total


def head_slices(heads, h):
    key = heads * DK
    return slice(h * DK, (h + 1) * DK), slice(key + h * DK, key + (h + 1) * DK), slice(2 * key + h * DV, 2 * key + (h + 1) * DV)


def unit_factor(rows):
    return lax.rsqrt(jnp.sum(rows * rows, axis=1, keepdims=True) + EPS)


def exact_tn(a, b):
    return lax.dot_general(a, b, (((0,), (0,)), ((), ())), precision=lax.Precision.HIGHEST, preferred_element_type=F32)


def softplus(x):
    return jnp.maximum(x, 0.0) + jnp.log(1.0 + jnp.exp(-jnp.abs(x)))


def decay_tables(heads, small, a_log, dt_bias, live, rows, cols):
    speed = -jnp.exp(a_log)
    biased = small[:, :heads] + dt_bias
    log_decay = speed * softplus(biased)
    sig = jax.nn.sigmoid(small[:, heads:2 * heads])
    upto = jnp.where(rows <= cols, 1.0, 0.0)
    run = exact_tn(upto, log_decay)
    run_row = exact_tn(log_decay, upto)
    return speed, biased, log_decay, sig, sig * live, run, run_row


def forward_kernel(heads, flag_ref, x_ref, rim_ref, taps_ref, small_ref, live_ref, alog_ref, dt_ref,
                   o_ref, e_ref, t_ref, z_ref, end_ref, carry, before_ref):
    step = pl.program_id(0)
    rows = lax.broadcasted_iota(jnp.int32, (BLOCK, BLOCK), 0)
    cols = lax.broadcasted_iota(jnp.int32, (BLOCK, BLOCK), 1)
    flag = flag_ref[step]

    @pl.when(step == 0)
    def _():
        before_ref[...] = rim_ref[8:16, :].astype(F32)
        unit = jnp.where(lax.broadcasted_iota(jnp.int32, (DK, DK), 0) == lax.broadcasted_iota(jnp.int32, (DK, DK), 1), 1.0, 0.0)
        for h in range(heads):
            carry[h, :, :DV] = jnp.zeros((DK, DV), F32)
            carry[h, :, DV:] = unit

    _, _, _, _, betas, run, run_row = decay_tables(heads, small_ref[...], alog_ref[...], dt_ref[...], live_ref[...], rows, cols)
    openings = flag * jnp.exp(run)
    closings = jnp.exp(run[BLOCK - 1:BLOCK] - run)

    def active(columns):
        c = conv_rows(x_ref[:, columns].astype(F32), before_ref[:, columns] * flag, taps_ref[:, columns])
        return c * jax.nn.sigmoid(c)

    tables, systems, parts = [], [], []
    for h in range(heads):
        qs, ks, vs = head_slices(heads, h)
        q, k, v = active(qs), active(ks), active(vs).astype(BF)
        q = (q * unit_factor(q) * DK ** (-0.5)).astype(BF)
        k = (k * unit_factor(k)).astype(BF)
        parts.append((q, k, v))
        table = block_tables(run[:, h:h + 1], run_row[h:h + 1, :], rows, cols)
        tables.append(table)
        systems.append(jnp.where(rows > cols, betas[:, h:h + 1] * table * mm_nt(k, k), 0.0))
    before_ref[...] = x_ref[BLOCK - 8:, :].astype(F32)
    inverses = unit_lower_inverses(systems, rows, cols)
    for h in range(heads):
        q, k, v = parts[h]
        beta, opening, closing = betas[:, h:h + 1], openings[:, h:h + 1], closings[:, h:h + 1]
        low_t = inverses[h].astype(BF)
        t_ref[0, h] = low_t
        u = mm(low_t, beta * v.astype(F32))
        w = mm(low_t, (beta * opening) * k.astype(F32))
        scores = mm_nt(q, k) * tables[h]
        state = carry[h]
        low_state = state.astype(BF)
        z_ref[0, h] = low_state
        reach = mm(jnp.concatenate([w.astype(BF), (opening * q.astype(F32)).astype(BF)], axis=0), low_state)
        c = jnp.concatenate([u, jnp.zeros((BLOCK, DK), F32)], axis=1) - reach[:BLOCK]
        low_c = c.astype(BF)
        out = reach[BLOCK:] + mm(scores, low_c)
        o_ref[:, h * DV:(h + 1) * DV] = out[:, :DV]
        e_ref[:, h * DK:(h + 1) * DK] = out[:, DV:].astype(BF)
        new = opening[BLOCK - 1:BLOCK] * state + mm_tn(closing * k.astype(F32), low_c)
        carry[h] = new
        end_ref[h] = new


def finish_kernel(heads, o_ref, e_ref, s_ref, gate_ref, live_ref, gain_ref, m_ref):
    live = live_ref[...]
    gain = gain_ref[...]
    for h in range(heads):
        vs = slice(h * DV, (h + 1) * DV)
        y = (o_ref[:, vs] + mm(e_ref[:, h * DK:(h + 1) * DK], s_ref[h])) * live
        r = lax.rsqrt(jnp.mean(y * y, axis=1, keepdims=True) + EPS)
        gate = gate_ref[:, vs]
        m_ref[:, vs] = (y * r * gain * (gate * jax.nn.sigmoid(gate))).astype(BF)


def finish(o, e, entry, gate, live, gain, heads, tile=128):
    rows = o.shape[0]
    row = lambda width: pl.BlockSpec((tile, width), lambda i: (i, 0))
    return pl.pallas_call(
        functools.partial(finish_kernel, heads),
        grid=(rows // tile,),
        in_specs=[row(heads * DV), row(heads * DK), pl.BlockSpec((heads, DK, DV), lambda i: (0, 0, 0)), row(heads * DV),
                  row(1), pl.BlockSpec((1, DV), lambda i: (0, 0))],
        out_specs=row(heads * DV),
        out_shape=jax.ShapeDtypeStruct((rows, heads * DV), BF),
        compiler_params=pltpu.CompilerParams(vmem_limit_bytes=48 * 2**20),
    )(o, e, entry, gate, live, gain)


def unfinish_kernel(heads, o_ref, e_ref, s_ref, gate_ref, live_ref, gain_ref, gm_ref, go_ref, gg_ref, ggain_ref, direct_ref):
    @pl.when(pl.program_id(0) == 0)
    def _():
        ggain_ref[...] = jnp.zeros_like(ggain_ref)
        direct_ref[...] = jnp.zeros_like(direct_ref)

    live = live_ref[...]
    gain = gain_ref[...]
    total = jnp.zeros((1, DV), F32)
    for h in range(heads):
        vs = slice(h * DV, (h + 1) * DV)
        e = e_ref[:, h * DK:(h + 1) * DK]
        y = (o_ref[:, vs] + mm(e, s_ref[h])) * live
        r = lax.rsqrt(jnp.mean(y * y, axis=1, keepdims=True) + EPS)
        gate = gate_ref[:, vs]
        sig = jax.nn.sigmoid(gate)
        act = gate * sig
        gm = gm_ref[:, vs]
        unit = y * r
        gn = gm * act
        total = total + jnp.sum(gn * unit, axis=0, keepdims=True)
        gn = gn * gain
        gg_ref[:, vs] = (gm * unit * gain * (sig * (1.0 + gate * (1.0 - sig)))).astype(BF)
        go = (r * (gn - unit * jnp.mean(gn * unit, axis=1, keepdims=True)) * live).astype(BF)
        go_ref[:, vs] = go
        direct_ref[h] += mm_tn(e, go)
    ggain_ref[...] += total


def unfinish(o, e, entry, gate, live, gain, gm, heads, tile=128):
    rows = o.shape[0]
    row = lambda width: pl.BlockSpec((tile, width), lambda i: (i, 0))
    return pl.pallas_call(
        functools.partial(unfinish_kernel, heads),
        grid=(rows // tile,),
        in_specs=[row(heads * DV), row(heads * DK), pl.BlockSpec((heads, DK, DV), lambda i: (0, 0, 0)), row(heads * DV),
                  row(1), pl.BlockSpec((1, DV), lambda i: (0, 0)), row(heads * DV)],
        out_specs=[row(heads * DV), row(heads * DV), pl.BlockSpec((1, DV), lambda i: (0, 0)),
                   pl.BlockSpec((heads, DK, DV), lambda i: (0, 0, 0))],
        out_shape=[jax.ShapeDtypeStruct((rows, heads * DV), BF), jax.ShapeDtypeStruct((rows, heads * DV), BF),
                   jax.ShapeDtypeStruct((1, DV), F32), jax.ShapeDtypeStruct((heads, DK, DV), F32)],
        compiler_params=pltpu.CompilerParams(vmem_limit_bytes=48 * 2**20),
    )(o, e, entry, gate, live, gain, gm)


def silu_back(c, grad):
    sig = jax.nn.sigmoid(c)
    return grad * (sig * (1.0 + c * (1.0 - sig)))


def backward_kernel(heads, flag_ref, x_ref, prev_ref, rim_ref, taps_ref, small_ref, live_ref, alog_ref, dt_ref, t_ref, z_ref,
                    go_ref, s_ref, exit_ref, gx_ref, gsmall_ref, gtaps_ref, gscalar_ref, carry, after_ref):
    step = pl.program_id(0)
    nb = pl.num_programs(0)
    at = nb - 1 - step
    rows = lax.broadcasted_iota(jnp.int32, (BLOCK, BLOCK), 0)
    cols = lax.broadcasted_iota(jnp.int32, (BLOCK, BLOCK), 1)
    last = lax.broadcasted_iota(jnp.int32, (BLOCK, 1), 0) == BLOCK - 1
    flag = flag_ref[at]
    taps_count = taps_ref.shape[0]

    @pl.when(step == 0)
    def _():
        carry[...] = exit_ref[...].astype(F32)
        after_ref[...] = jnp.zeros_like(after_ref)
        gtaps_ref[...] = jnp.zeros_like(gtaps_ref)
        gscalar_ref[...] = jnp.zeros_like(gscalar_ref)

    live = live_ref[...]
    speed, biased, log_decay, sig, betas, run, run_row = decay_tables(
        heads, small_ref[...], alog_ref[...], dt_ref[...], live, rows, cols)
    openings = flag * jnp.exp(run)
    closings = jnp.exp(run[BLOCK - 1:BLOCK] - run)
    row_block = pl.ds(pl.multiple_of(at * BLOCK, BLOCK), BLOCK)

    def inputs(columns):
        x = x_ref[:, columns].astype(F32)
        before = jnp.where(at == 0, rim_ref[8:16, columns].astype(F32), prev_ref[8:16, columns].astype(F32)) * flag
        return x, before, conv_rows(x, before, taps_ref[:, columns])

    def conv_back(columns, x, before, grad):
        taps = taps_ref[:, columns]
        later = after_ref[:, columns]
        longer = jnp.concatenate([grad, later], axis=0)
        gx = taps[taps_count - 1:taps_count] * grad
        sums = [jnp.sum(grad * x, axis=0, keepdims=True)]
        for back in range(1, taps_count):
            gx = gx + taps[taps_count - 1 - back:taps_count - back] * longer[back:back + BLOCK]
            sums.append(jnp.sum(grad * shifted(x, before, back), axis=0, keepdims=True))
        gx_ref[row_block, columns] = gx.astype(BF)
        gtaps_ref[:, columns] += jnp.concatenate(sums[::-1], axis=0)
        after_ref[:, columns] = grad[:8] * flag

    grad_runs, grad_betas = [], []
    for h in range(heads):
        qs, ks, vs = head_slices(heads, h)
        xq, bq, cq = inputs(qs)
        xk, bk, ck = inputs(ks)
        xv, bv, cv = inputs(vs)
        aq, ak = cq * jax.nn.sigmoid(cq), ck * jax.nn.sigmoid(ck)
        rq, rk_unit = unit_factor(aq), unit_factor(ak)
        uq, uk = aq * rq, ak * rk_unit
        q, k = (uq * DK ** (-0.5)).astype(BF), uk.astype(BF)
        v = (cv * jax.nn.sigmoid(cv)).astype(BF)
        qf, kf, vf = q.astype(F32), k.astype(F32), v.astype(F32)
        beta, opening, closing = betas[:, h:h + 1], openings[:, h:h + 1], closings[:, h:h + 1]
        gamma = opening[BLOCK - 1:BLOCK]
        table = block_tables(run[:, h:h + 1], run_row[h:h + 1, :], rows, cols)
        kk = mm_nt(k, k)
        scores = mm_nt(q, k) * table
        low_t = t_ref[0, h]
        u = mm(low_t, beta * vf)
        w = mm(low_t, (beta * opening) * kf)
        low_w = w.astype(BF)
        state = z_ref[0, h, :, :DV].astype(F32) + mm(z_ref[0, h, :, DV:], s_ref[h])
        low_s = state.astype(BF)
        c = u - mm(low_w, low_s)
        low_c = c.astype(BF)
        go = go_ref[:, h * DV:(h + 1) * DV]
        g = carry[h]
        low_g = g.astype(BF)
        low_ck = (closing * kf).astype(BF)
        low_oq = (opening * qf).astype(BF)
        dc = mm_tn(scores, go) + mm(low_ck, low_g)
        low_dc = dc.astype(BF)
        both = jnp.concatenate([go, low_dc], axis=0)
        carry[h] = gamma * g + mm_tn(jnp.concatenate([low_oq, -low_w], axis=0), both)
        dkeyed = mm_nt(low_c, low_g)
        dgamma = jnp.sum(jnp.sum(state * g, axis=1, keepdims=True), axis=0, keepdims=True)
        dscore = jnp.where(rows >= cols, mm_nt(go, low_c), 0.0)
        back = mm_nt(both, low_s)
        doq, dw = back[:BLOCK], -back[BLOCK:]
        drv = mm_tn(low_t, low_dc)
        drw = mm_tn(low_t, dw)
        low_drv, low_drw = drv.astype(BF), drw.astype(BF)
        da = jnp.where(rows > cols, -(mm_nt(low_drv, u) + mm_nt(low_drw, low_w)), 0.0)
        dat = da * table
        dkk = (beta * dat).astype(BF)
        dqk = (dscore * table).astype(BF)
        gq = (opening * doq + mm(dqk, k)) * DK ** (-0.5)
        gk = mm_tn(dqk, q) + mm(dkk, k) + mm_tn(dkk, k) + closing * dkeyed + (beta * opening) * drw
        gq = rq * (gq - uq * jnp.sum(gq * uq, axis=1, keepdims=True))
        gk = rk_unit * (gk - uk * jnp.sum(gk * uk, axis=1, keepdims=True))
        conv_back(qs, xq, bq, silu_back(cq, gq))
        conv_back(ks, xk, bk, silu_back(ck, gk))
        conv_back(vs, xv, bv, silu_back(cv, beta * drv))
        rk = jnp.sum(drw * kf, axis=1, keepdims=True)
        atk = dat * kk
        grad_betas.append(jnp.sum(drv * vf, axis=1, keepdims=True) + opening * rk + jnp.sum(atk, axis=1, keepdims=True))
        dopen = opening * (jnp.sum(doq * qf, axis=1, keepdims=True) + beta * rk)
        dclose = closing * jnp.sum(dkeyed * kf, axis=1, keepdims=True)
        e = dscore * scores + beta * atk
        by_col = exact_tn(e, jnp.ones((BLOCK, 8), F32))[:, :1]
        dg = jnp.sum(e, axis=1, keepdims=True) - by_col + dopen - dclose
        grad_runs.append(dg + jnp.where(last, jnp.sum(dclose, axis=0, keepdims=True) + dgamma * gamma, 0.0))

    lane = lax.broadcasted_iota(jnp.int32, (BLOCK, heads), 1)
    grad_run = sum(jnp.where(lane == h, grad_runs[h], 0.0) for h in range(heads))
    grad_beta = sum(jnp.where(lane == h, grad_betas[h], 0.0) for h in range(heads))
    grad_log = exact_tn(jnp.where(cols <= rows, 1.0, 0.0), grad_run)
    grad_biased = grad_log * speed * jax.nn.sigmoid(biased)
    gsmall_ref[:, :heads] = grad_biased
    gsmall_ref[:, heads:] = grad_beta * live * sig * (1.0 - sig)
    gscalar_ref[0:1, :] += jnp.sum(grad_log * log_decay, axis=0, keepdims=True)
    gscalar_ref[1:2, :] += jnp.sum(grad_biased, axis=0, keepdims=True)

    @pl.when(step == nb - 1)
    def _():
        longer = jnp.concatenate([jnp.zeros((16, taps_ref.shape[1]), F32), after_ref[...]], axis=0)
        gx = jnp.zeros((16, taps_ref.shape[1]), F32)
        for back in range(1, taps_count):
            gx = gx + taps_ref[taps_count - 1 - back:taps_count - back, :] * longer[back:back + 16]
        gx_ref[pl.ds(nb * BLOCK, 16), :] = gx.astype(BF)


MESH = pl.DeviceIdType.MESH


def line_position():
    w = lax.axis_index("wide")
    return w, w // 2, w % 2, lax.axis_index("narrow")


def greet_line(places, w, place, side, n):
    barrier = pltpu.get_barrier_semaphore()
    pl.semaphore_signal(barrier, inc=1, device_id=(w + 1 - 2 * side, n), device_id_type=MESH)

    @pl.when(place > 0)
    def _():
        pl.semaphore_signal(barrier, inc=1, device_id=(w - 2, n), device_id_type=MESH)

    @pl.when(place < places - 1)
    def _():
        pl.semaphore_signal(barrier, inc=1, device_id=(w + 2, n), device_id_type=MESH)

    pl.semaphore_wait(barrier, 1 + jnp.where(place > 0, 1, 0) + jnp.where(place < places - 1, 1, 0))


def row_cuts(rows, chunks):
    units = rows // 16
    chunks = min(chunks, units)
    edges = [16 * (units * c // chunks) for c in range(chunks + 1)]
    return [(edges[c], edges[c + 1] - edges[c], chunks >= 5 and c == 0) for c in range(chunks)]


class LineGather:
    def __init__(self, places, cuts, sources, targets, local_sems, send_sems, recv_sems):
        self.places, self.sources, self.targets = places, sources, targets
        self.local_sems, self.send_sems, self.recv_sems = local_sems, send_sems, recv_sems
        self.w, self.place, self.side, self.n = line_position()
        self.items = [(i,) + cut for i, found in enumerate(cuts) for cut in found]

    def copy(self, item, slot, way, own=False):
        number, (i, start, size, _) = item, self.items[item]
        rows = pl.ds(start, size)
        source = self.sources[i].at[rows] if own else self.targets[i].at[slot, rows]
        device = [self.w + 1 - 2 * self.side, self.w + 2, self.w - 2][way]
        return pltpu.make_async_remote_copy(
            src_ref=source, dst_ref=self.targets[i].at[slot, rows], send_sem=self.send_sems.at[way, slot, number],
            recv_sem=self.recv_sems.at[slot, number], device_id=(device, self.n), device_id_type=MESH)

    def start(self):
        for i, source in enumerate(self.sources):
            pltpu.make_async_copy(source, self.targets[i].at[self.w], self.local_sems.at[i]).start()
        for item in range(len(self.items)):
            self.copy(item, self.w, 0, True).start()
            self.along(item, self.w, 1, True)
            self.along(item, self.w, 2, True)

    def along(self, item, slot, way, own=False):
        @pl.when(self.place < self.places - 1 if way == 1 else self.place > 0)
        def _():
            self.copy(item, slot, way, own).start()

    def events(self):
        found = []
        for item in range(len(self.items)):
            if self.items[item][3]:
                found.append((item, 0, -1))
        for t in range(1, self.places):
            for item in range(len(self.items)):
                found += [(item, t, s) for s in ((0, 1) if self.items[item][3] else (0,))]
        return found

    def run(self, event):
        item, t, s = event
        if s < 0:
            slot = self.w + 1 - 2 * self.side
            self.copy(item, slot, 0).wait_recv()
            self.along(item, slot, 1)
            self.along(item, slot, 2)
            return

        for way, there in ((1, self.place - t), (2, self.place + t)):
            slot = 2 * there + (self.side if s == 0 else 1 - self.side)

            @pl.when((there >= 0) & (there < self.places))
            def _():
                self.copy(item, slot, way).wait_recv()
                self.along(item, slot, way)
                if not self.items[item][3]:
                    self.copy(item, slot, 0).start()

    def finish(self):
        for item in range(len(self.items)):
            if not self.items[item][3]:
                for t in range(self.places):
                    self.copy(item, 2 * t + 1 - self.side, 0).wait_recv()
        for i, source in enumerate(self.sources):
            pltpu.make_async_copy(source, self.targets[i].at[self.w], self.local_sems.at[i]).wait()
        for item in range(len(self.items)):
            both = self.items[item][3]
            for t in range(self.places):
                slot = 2 * t + self.side
                if both:
                    @pl.when(t == self.place)
                    def _():
                        self.copy(item, slot, 0).wait_send()
                else:
                    self.copy(item, slot, 0).wait_send()
                for s in ((0, 1) if both else (0,)):
                    slot = 2 * t + (self.side if s == 0 else 1 - self.side)

                    @pl.when((self.place < self.places - 1) & (t <= self.place))
                    def _():
                        self.copy(item, slot, 1).wait_send()

                    @pl.when((self.place > 0) & (t >= self.place))
                    def _():
                        self.copy(item, slot, 2).wait_send()

    @staticmethod
    def scratch(count, cuts):
        items = sum(len(found) for found in cuts)
        return [pltpu.SemaphoreType.DMA((len(cuts),)), pltpu.SemaphoreType.DMA((3, count, items)),
                pltpu.SemaphoreType.DMA((count, items))]


def gather_kernel(places, cuts, *refs):
    amount = len(cuts)
    gather = LineGather(places, cuts, refs[:amount], refs[amount:2 * amount], *refs[2 * amount:])
    greet_line(places, gather.w, gather.place, gather.side, gather.n)
    gather.start()
    for event in gather.events():
        gather.run(event)
    gather.finish()


def line_gather(values, call_id, chunks=6):
    count = lax.axis_size("wide")
    cuts = [row_cuts(value.shape[0], chunks if value.shape[0] > 64 else 1) for value in values]
    hbm = pl.BlockSpec(memory_space=pl.ANY)
    gathered = pl.pallas_call(
        functools.partial(gather_kernel, count // 2, cuts),
        out_shape=[jax.ShapeDtypeStruct((count,) + value.shape, value.dtype) for value in values],
        in_specs=[hbm] * len(values),
        out_specs=[hbm] * len(values),
        scratch_shapes=LineGather.scratch(count, cuts),
        compiler_params=pltpu.CompilerParams(collective_id=call_id, has_side_effects=True),
    )(*values)
    return [g.reshape((count * g.shape[1],) + g.shape[2:]) for g in gathered]


class LineScatter:
    def __init__(self, places, cuts, sources, owns, pairs, lines, load_sems, pair_send, pair_recv, right_send,
                 right_recv, left_send, left_recv):
        self.places, self.sources, self.owns, self.pairs, self.lines = places, sources, owns, pairs, lines
        self.load_sems, self.pair_sems = load_sems, (pair_send, pair_recv)
        self.right_sems, self.left_sems = (right_send, right_recv), (left_send, left_recv)
        self.w, self.place, self.side, self.n = line_position()
        self.items = [(i,) + cut[:2] for i, found in enumerate(cuts) for cut in found]
        self.order = [t for j in range(places // 2) for t in (places - 1 - j, j)]

    def remote(self, source, target, sems, t, item, device):
        return pltpu.make_async_remote_copy(src_ref=source, dst_ref=target, send_sem=sems[0].at[t, item],
                                            recv_sem=sems[1].at[t, item], device_id=(device, self.n), device_id_type=MESH)

    def at(self, t, item):
        i, start, size = self.items[item]
        return t, pl.ds(start, size)

    def across(self, t, item):
        i = self.items[item][0]
        source = self.sources[i].at[2 * t + 1 - self.side, self.at(t, item)[1]]
        return self.remote(source, self.pairs[i].at[self.at(t, item)], self.pair_sems, t, item, self.w + 1 - 2 * self.side)

    def load(self, t, item):
        i = self.items[item][0]
        return pltpu.make_async_copy(self.sources[i].at[2 * t + self.side, self.at(t, item)[1]],
                                     self.owns[i].at[self.at(t, item)], self.load_sems.at[t, item])

    def right(self, t, item):
        i, at = self.items[item][0], self.at(t, item)
        return self.remote(self.owns[i].at[at], self.lines[i].at[at], self.right_sems, t, item, self.w + 2)

    def left(self, t, item, arriving=False):
        i, at = self.items[item][0], self.at(t, item)
        slot = jnp.where(t == self.place - (0 if arriving else 1), self.places, t)
        return self.remote(self.owns[i].at[at], self.lines[i].at[slot, at[1]], self.left_sems, t, item, self.w - 2)

    def start(self):
        for t in self.order:
            for item in range(len(self.items)):
                self.across(t, item).start()
                self.load(t, item).start()

    def events(self):
        return [(t, item) for t in self.order for item in range(len(self.items))]

    def run(self, event):
        t, item = event
        i, at = self.items[item][0], self.at(t, item)
        own, place, places = self.owns[i], self.place, self.places

        def add(other):
            own[at] = (own[at].astype(F32) + other[at].astype(F32)).astype(own.dtype)

        self.load(t, item).wait()
        self.across(t, item).wait_recv()
        add(self.pairs[i])

        @pl.when(t > place)
        def _():
            @pl.when(place > 0)
            def _():
                self.right(t, item).wait_recv()
                add(self.lines[i])

            self.right(t, item).start()

        @pl.when(t < place)
        def _():
            @pl.when(place < places - 1)
            def _():
                self.left(t, item, True).wait_recv()
                add(self.lines[i])

            self.left(t, item).start()

    def finish(self, outs):
        place = self.place
        for item in range(len(self.items)):
            i, at = self.items[item][0], self.at(place, item)
            out, own = outs[i], self.owns[i]
            out[at[1]] = own[at].astype(F32)

            @pl.when(place > 0)
            def _():
                self.right(place, item).wait_recv()
                out[at[1]] = out[at[1]] + self.lines[i][at].astype(F32)

            @pl.when(place < self.places - 1)
            def _():
                self.left(place, item, True).wait_recv()
                out[at[1]] = out[at[1]] + self.lines[i][self.places, at[1]].astype(F32)
        for t in range(self.places):
            for item in range(len(self.items)):
                self.across(t, item).wait_send()

                @pl.when(t > place)
                def _():
                    self.right(t, item).wait_send()

                @pl.when(t < place)
                def _():
                    self.left(t, item).wait_send()

    @staticmethod
    def scratch(places, cuts, values):
        buffers = [pltpu.VMEM((places,) + value.shape[1:], value.dtype) for value in values]
        lines = [pltpu.VMEM((places + 1,) + value.shape[1:], value.dtype) for value in values]
        items = sum(len(found) for found in cuts)
        return buffers * 2 + lines + [pltpu.SemaphoreType.DMA((places, items))] * 7


def scatter_kernel(places, cuts, *refs):
    m = len(cuts)
    sources, outs, owns, pairs, lines = [refs[m * g:m * (g + 1)] for g in range(5)]
    scatter = LineScatter(places, cuts, sources, owns, pairs, lines, *refs[5 * m:])
    greet_line(places, scatter.w, scatter.place, scatter.side, scatter.n)
    scatter.start()
    for event in scatter.events():
        scatter.run(event)
    scatter.finish(outs)


def line_scatter(values, call_id, chunks=4):
    count = values[0].shape[0]
    cuts = [row_cuts(value.shape[1], chunks if value.shape[1] > 64 else 1) for value in values]
    return pl.pallas_call(
        functools.partial(scatter_kernel, count // 2, cuts),
        out_shape=[jax.ShapeDtypeStruct(value.shape[1:], F32) for value in values],
        in_specs=[pl.BlockSpec(memory_space=pl.ANY)] * len(values),
        out_specs=[pl.BlockSpec(memory_space=pltpu.VMEM)] * len(values),
        scratch_shapes=LineScatter.scratch(count // 2, cuts, values),
        compiler_params=pltpu.CompilerParams(collective_id=call_id, has_side_effects=True, vmem_limit_bytes=56 * 2**20),
    )(*values)


def forward_gather_kernel(heads, nb, places, cuts, *refs):
    m = len(cuts)
    inputs, sources, refs = refs[:8], refs[8:8 + m], refs[8 + m:]
    outs, targets, refs = refs[:5], refs[5:5 + m], refs[5 + m:]
    gather = LineGather(places, cuts, sources, targets, *refs[2:])
    step = pl.program_id(0)

    @pl.when(step == 0)
    def _():
        greet_line(places, gather.w, gather.place, gather.side, gather.n)
        gather.start()

    forward_kernel(heads, *inputs, *outs, *refs[:2])
    events = gather.events()
    for i in range(nb):
        @pl.when(step == i)
        def _():
            for event in events[len(events) * i // nb:len(events) * (i + 1) // nb]:
                gather.run(event)

    @pl.when(step == nb - 1)
    def _():
        gather.finish()


def forward_gather(flags, mixed, taps, small, live, a_log, dt_bias, heads, blocks, call_id, chunks=2):
    rows, width = live.shape[0], mixed.shape[1]
    nb = rows // BLOCK
    count = lax.axis_size("wide")
    cuts = [row_cuts(block.shape[0], chunks) for block in blocks]
    row = lambda width: pl.BlockSpec((BLOCK, width), lambda i: (i, 0))
    same = lambda *shape: pl.BlockSpec(shape, lambda i: (0,) * len(shape))
    hbm = pl.BlockSpec(memory_space=pl.ANY)
    found = pl.pallas_call(
        functools.partial(forward_gather_kernel, heads, nb, count // 2, cuts),
        grid=(nb,),
        in_specs=[pl.BlockSpec(memory_space=pltpu.SMEM), row(width), pl.BlockSpec((16, width), lambda i: (rows // 16, 0)),
                  same(*taps.shape), row(small.shape[1]), row(1), same(1, heads), same(1, heads)]
                 + [hbm] * len(blocks),
        out_specs=[row(heads * DV), row(heads * DK),
                   pl.BlockSpec((1, heads, BLOCK, BLOCK), lambda i: (i, 0, 0, 0)),
                   pl.BlockSpec((1, heads, DK, DV + DK), lambda i: (i, 0, 0, 0)),
                   same(heads, DK, DV + DK)] + [hbm] * len(blocks),
        out_shape=[jax.ShapeDtypeStruct((rows, heads * DV), F32), jax.ShapeDtypeStruct((rows, heads * DK), BF),
                   jax.ShapeDtypeStruct((nb, heads, BLOCK, BLOCK), BF),
                   jax.ShapeDtypeStruct((nb, heads, DK, DV + DK), BF),
                   jax.ShapeDtypeStruct((heads, DK, DV + DK), F32)]
                  + [jax.ShapeDtypeStruct((count,) + block.shape, block.dtype) for block in blocks],
        scratch_shapes=[pltpu.VMEM((heads, DK, DV + DK), F32), pltpu.VMEM((8, width), F32)]
                       + LineGather.scratch(count, cuts),
        compiler_params=pltpu.CompilerParams(collective_id=call_id, has_side_effects=True, vmem_limit_bytes=48 * 2**20),
    )(flags, mixed, mixed, taps, small, live, a_log, dt_bias, *blocks)
    return found[:5], [g.reshape((count * g.shape[1],) + g.shape[2:]) for g in found[5:]]


def backward_scatter_kernel(heads, nb, places, cuts, *refs):
    m = len(cuts)
    inputs, sources, refs = refs[:14], refs[14:14 + m], refs[14 + m:]
    outs, sums, refs = refs[:4], refs[4:4 + m], refs[4 + m:]
    scratch, refs = refs[:2], refs[2:]
    owns, pairs, lines = (refs[m * g:m * (g + 1)] for g in range(3))
    scatter = LineScatter(places, cuts, sources, owns, pairs, lines, *refs[3 * m:])
    step = pl.program_id(0)

    @pl.when(step == 0)
    def _():
        greet_line(places, scatter.w, scatter.place, scatter.side, scatter.n)
        scatter.start()

    backward_kernel(heads, *inputs, *outs, *scratch)
    events = scatter.events()
    for i in range(nb):
        @pl.when(step == i)
        def _():
            for event in events[len(events) * i // nb:len(events) * (i + 1) // nb]:
                scatter.run(event)

    @pl.when(step == nb - 1)
    def _():
        scatter.finish(sums)


def backward_scatter(flags, mixed, taps, small, live, a_log, dt_bias, t, z, go, entry, leaving, heads, terms, call_id,
                     chunks=2):
    rows, width = live.shape[0], mixed.shape[1]
    nb = rows // BLOCK
    count = terms[0].shape[0]
    cuts = [row_cuts(term.shape[1], chunks) for term in terms]
    row = lambda width: pl.BlockSpec((BLOCK, width), lambda i: (nb - 1 - i, 0))
    same = lambda *shape: pl.BlockSpec(shape, lambda i: (0,) * len(shape))
    prev = pl.BlockSpec((16, width), lambda i: (jnp.maximum((nb - 1 - i) * (BLOCK // 16) - 1, 0), 0))
    found = pl.pallas_call(
        functools.partial(backward_scatter_kernel, heads, nb, count // 2, cuts),
        grid=(nb,),
        in_specs=[pl.BlockSpec(memory_space=pltpu.SMEM), row(width), prev,
                  pl.BlockSpec((16, width), lambda i: (rows // 16, 0)), same(*taps.shape), row(small.shape[1]), row(1),
                  same(1, heads), same(1, heads),
                  pl.BlockSpec((1, heads, BLOCK, BLOCK), lambda i: (nb - 1 - i, 0, 0, 0)),
                  pl.BlockSpec((1, heads, DK, DV + DK), lambda i: (nb - 1 - i, 0, 0, 0)),
                  row(heads * DV), same(heads, DK, DV), same(heads, DK, DV)]
                 + [pl.BlockSpec(memory_space=pl.ANY)] * len(terms),
        out_specs=[same(rows + 16, width), row(2 * heads), same(*taps.shape), same(8, heads)]
                  + [same(*term.shape[1:]) for term in terms],
        out_shape=[jax.ShapeDtypeStruct((rows + 16, width), BF), jax.ShapeDtypeStruct((rows, 2 * heads), F32),
                   jax.ShapeDtypeStruct(taps.shape, F32), jax.ShapeDtypeStruct((8, heads), F32)]
                  + [jax.ShapeDtypeStruct(term.shape[1:], F32) for term in terms],
        scratch_shapes=[pltpu.VMEM((heads, DK, DV), F32), pltpu.VMEM((8, width), F32)]
                       + LineScatter.scratch(count // 2, cuts, terms),
        compiler_params=pltpu.CompilerParams(collective_id=call_id, has_side_effects=True, vmem_limit_bytes=58 * 2**20),
    )(flags, mixed, mixed, mixed, taps, small, live, a_log, dt_bias, t, z, go, entry, leaving, *terms)
    return found[:4], found[4:]


def greet_places(places, w, place, side, n):
    barrier = pltpu.get_barrier_semaphore()
    pl.semaphore_signal(barrier, inc=1, device_id=(w + 1 - 2 * side, n), device_id_type=MESH)
    for k in range(1, places):
        @pl.when(place + k < places)
        def _():
            pl.semaphore_signal(barrier, inc=1, device_id=(w + 2 * k, n), device_id_type=MESH)

        @pl.when(place - k >= 0)
        def _():
            pl.semaphore_signal(barrier, inc=1, device_id=(w - 2 * k, n), device_id_type=MESH)

    pl.semaphore_wait(barrier, places)


def pass_kernel(places, heads, forward, *refs):
    if forward:
        end_ref, entry_ref, their_map_ref, joined_map_ref = refs[:4]
        refs = refs[4:]
    else:
        direct_ref, my_map_ref, their_map_ref, joined_map_ref, entry_ref = refs[:5]
        refs = refs[5:]
    mine, theirs, joined, turned, total, states, near_send, near_recv, far_send, far_recv = refs
    w, place, side, n = line_position()
    half = heads // 2
    partner = w + 1 - 2 * side
    my_half, other_half = pl.ds(side * half, half), pl.ds((1 - side) * half, half)
    mine[...] = (end_ref if forward else direct_ref)[...].astype(BF)
    greet_places(places, w, place, side, n)

    def near(source, target, part, which):
        return pltpu.make_async_remote_copy(
            src_ref=source.at[part], dst_ref=target.at[part], send_sem=near_send.at[which], recv_sem=near_recv.at[which],
            device_id=(partner, n), device_id_type=MESH)

    def far(k, step):
        return pltpu.make_async_remote_copy(
            src_ref=joined, dst_ref=turned.at[k], send_sem=far_send.at[k], recv_sem=far_recv.at[k],
            device_id=(w + 2 * step, n), device_id_type=MESH)

    ahead = 1 if forward else -1
    near(mine, theirs, other_half, 0).start()
    near(mine, theirs, my_half, 1).start()
    near(mine, theirs, my_half, 0).wait_recv()
    for i in range(half):
        own, other = mine[side * half + i], theirs[side * half + i]
        early, late = jnp.where(side == 0, own, other), jnp.where(side == 0, other, own)
        if forward:
            both = mm(late[:, DV:], early)
            joined[i, :, :DV] = (both[:, :DV] + late[:, :DV].astype(F32)).astype(BF)
            joined[i, :, DV:] = both[:, DV:].astype(BF)
            joined_map_ref[i] = both[:, DV:].astype(BF)
        else:
            early_map = jnp.where(side == 0, my_map_ref[side * half + i], their_map_ref[side * half + i])
            joined[i, :, :DV] = (mm_tn(early_map, late) + early.astype(F32)).astype(BF)
            joined[i, :, DV:] = joined_map_ref[i]
    for k in range(1, places):
        @pl.when((place + ahead * k >= 0) & (place + ahead * k < places))
        def _():
            far(k, ahead * k).start()

    total[...] = jnp.zeros_like(total)
    for k in range(places - 1, 0, -1):
        @pl.when((place - ahead * k >= 0) & (place - ahead * k < places))
        def _():
            far(k, ahead * k).wait_recv()
            for i in range(half):
                apply = mm if forward else mm_tn
                total[i] = apply(turned[k, i, :, DV:], total[i]) + turned[k, i, :, :DV].astype(F32)

    states[my_half] = total[...].astype(BF)
    near(states, states, my_half, 2).start()
    near(mine, theirs, other_half, 1).wait_recv()
    near(states, states, other_half, 2).wait_recv()
    through = 1 if forward else 0
    for h in range(heads):
        if forward:
            their_map_ref[h] = theirs[h, :, DV:]
        state = states[h]
        if forward:
            passed = mm(theirs[h, :, DV:], state) + theirs[h, :, :DV].astype(F32)
        else:
            passed = mm_tn(their_map_ref[h], state) + theirs[h].astype(F32)
        entry_ref[h] = jnp.where(side == through, passed, state.astype(F32)).astype(BF)
    near(mine, theirs, other_half, 0).wait_send()
    near(mine, theirs, my_half, 1).wait_send()
    near(states, states, my_half, 2).wait_send()
    for k in range(1, places):
        @pl.when((place + ahead * k >= 0) & (place + ahead * k < places))
        def _():
            far(k, ahead * k).wait_send()


def pass_states(operands, heads, forward, call_id):
    places = lax.axis_size("wide") // 2
    half = heads // 2
    width = DV + DK if forward else DV
    vmem = pl.BlockSpec(memory_space=pltpu.VMEM)
    out_shape = [jax.ShapeDtypeStruct((heads, DK, DV), BF)]
    if forward:
        out_shape += [jax.ShapeDtypeStruct((heads, DK, DK), BF), jax.ShapeDtypeStruct((half, DK, DK), BF)]
    return pl.pallas_call(
        functools.partial(pass_kernel, places, heads, forward),
        in_specs=[vmem] * len(operands),
        out_specs=[vmem] * len(out_shape),
        out_shape=out_shape,
        scratch_shapes=[pltpu.VMEM((heads, DK, width), BF), pltpu.VMEM((heads, DK, width), BF),
                        pltpu.VMEM((half, DK, DV + DK), BF), pltpu.VMEM((places, half, DK, DV + DK), BF),
                        pltpu.VMEM((half, DK, DV), F32), pltpu.VMEM((heads, DK, DV), BF),
                        pltpu.SemaphoreType.DMA((3,)), pltpu.SemaphoreType.DMA((3,)),
                        pltpu.SemaphoreType.DMA((places,)), pltpu.SemaphoreType.DMA((places,))],
        compiler_params=pltpu.CompilerParams(collective_id=call_id, has_side_effects=True, vmem_limit_bytes=32 * 2**20),
    )(*operands)


CONV = 4


def rms_norm(value, gain):
    return value * lax.rsqrt(jnp.mean(value * value, axis=-1, keepdims=True) + EPS) * gain


def after(value, *others):
    return lax.optimization_barrier((value,) + others)[0]


def from_behind(value, axis, steps):
    count = lax.axis_size(axis)
    initial, last = (max(0, -steps), min(count, count - steps))
    return lax.ppermute(value, axis, [(source, source + steps) for source in range(initial, last)])


def turn(value, k):
    count = lax.axis_size("wide")
    if k % (count // 2) == 0:
        return value
    return lax.ppermute(value, "wide", [(w, (w + 2 * k) % count) for w in range(count)])


def across(value, axis, bit):
    return lax.ppermute(value, axis, [(i, i ^ bit) for i in range(lax.axis_size(axis))])


def turn_gather(value):
    places = lax.axis_size("wide") // 2
    own = [turn(value, k) for k in range(places)]
    return assemble([piece for part in own for piece in (part, across(part, "wide", 1))])


def turn_scatter(value):
    places = value.shape[0] // 2
    me = lax.axis_index("wide")
    place, side = me // 2, me % 2
    paired = value.reshape((places, 2) + value.shape[1:])
    theirs = across(lax.dynamic_index_in_dim(paired, 1 - side, 1, keepdims=False), "wide", 1)
    total = None
    for k in list(range(1, places)) + [0]:
        at = (place + k) % places
        block = lax.dynamic_slice(paired, (at, side, 0, 0), (1, 1) + value.shape[1:])[0, 0].astype(F32)
        block = block + lax.dynamic_index_in_dim(theirs, at, 0, keepdims=False).astype(F32)
        if k:
            block = turn(block.astype(BF), k).astype(F32)
        total = block if total is None else total + block
    return total


def gather_narrow(value):
    near = across(value, "narrow", 1)
    return [value, near, across(value, "narrow", 2), across(near, "narrow", 2)]


def scatter_narrow(parts):
    first = parts[0].astype(F32) + across(parts[1], "narrow", 1).astype(F32)
    second = (parts[2].astype(F32) + across(parts[3], "narrow", 1).astype(F32)).astype(parts[2].dtype)
    return first + across(second, "narrow", 2).astype(F32)


def blocks_of(value, axis, count):
    me = lax.axis_index("narrow")
    size = value.shape[axis] // count
    return [lax.dynamic_slice_in_dim(value, (me ^ j) * size, size, axis) for j in range(count)]


def placed(pieces, axis):
    me = lax.axis_index("narrow")
    size = pieces[0].shape[axis]
    shape = list(pieces[0].shape)
    shape[axis] = size * len(pieces)
    whole = jnp.zeros(shape, pieces[0].dtype)
    for j, piece in enumerate(pieces):
        whole = lax.dynamic_update_slice_in_dim(whole, piece, (me ^ j) * size, axis)
    return whole


def sum_all(value, axis):
    bit = 1
    while bit < lax.axis_size(axis):
        value = value + across(value, axis, bit)
        bit *= 2
    return value


def sequence_tables(doc_lengths, first_row, row_count, block_size):
    padded = (doc_lengths + block_size - 1) // block_size * block_size
    seq_ends = jnp.cumsum(padded)
    seq_starts = seq_ends - padded
    row_places = first_row + jnp.arange(row_count, dtype=jnp.int32)
    inside_mask = (row_places[:, None] >= seq_starts[None, :]) & (row_places[:, None] < seq_ends[None, :])
    live_mask = jnp.any(inside_mask & (row_places[:, None] < (seq_starts + doc_lengths)[None, :]), axis=1, keepdims=True)
    fresh_block = jnp.any(row_places[::block_size][:, None] == seq_starts[None, :], axis=1)
    return live_mask.astype(F32), jnp.where(fresh_block, 0.0, 1.0).astype(F32)


def contract_rows(left, right):
    return lax.dot_general(left, right, (((0,), (0,)), ((), ())), preferred_element_type=F32)


def contract_cols(left, right):
    return lax.dot_general(left, right, (((1,), (1,)), ((), ())), preferred_element_type=F32)


def shards(block_input, gain_attn, w_query, w_key, w_value, w_gate_out, w_decay, w_beta, conv_query, conv_key,
           conv_value, a_log, dt_bias, out_gain, w_out, gain_mlp, w_gate, w_up, w_down, doc_lengths, cotangent):
    row_count, d_model = block_input.shape
    quarter = cotangent.shape[0]
    depth = w_query.shape[0]
    heads = a_log.shape[0]
    narrow = lax.axis_size("narrow")
    wide = lax.axis_size("wide")
    wide_index = lax.axis_index("wide")
    live, flags = sequence_tables(doc_lengths, wide_index * row_count, row_count, BLOCK)
    gain_row, a_row, dt_row = out_gain[None, :], a_log[None, :], dt_bias[None, :]
    key_width, value_width = heads * DK, heads * DV
    columns = 2 * key_width + value_width
    depth_blocks = lambda a: a.astype(BF).reshape(wide, depth, a.shape[1])
    row_blocks = lambda a: a.astype(BF).reshape(wide, quarter, a.shape[1])

    padded = lambda a: jnp.pad(a, ((0, 16 - 2 * heads), (0, 0)))
    small_shard = padded(jnp.concatenate([w_decay.T, w_beta.T], axis=0))
    rim_input = from_behind(block_input[row_count - 16:], "wide", 1)
    input_rows = jnp.concatenate([block_input, rim_input], axis=0).astype(F32)
    normed_low = rms_norm(input_rows, gain_attn).astype(BF)
    first, small_weight = line_gather([jnp.concatenate([w_query, w_key, w_value], axis=1), small_shard], 1)
    small_weight = small_weight.reshape(wide, 16, depth)[:, :2 * heads].transpose(1, 0, 2).reshape(2 * heads, d_model)
    taps = jnp.concatenate([conv_query, conv_key, conv_value], axis=1)
    mixed = jnp.dot(normed_low, first, preferred_element_type=F32).astype(BF)
    small = contract_cols(normed_low[:row_count], small_weight)

    (local_out, reach, inverses, states, end), (gate_weight, out_weight) = forward_gather(
        flags, mixed, taps, small, live, a_row, dt_row, heads, [w_gate_out, w_out], 7)
    entry, their_map, joined_map = pass_states((end,), heads, True, 2)
    gate_rows = jnp.dot(normed_low[:row_count], gate_weight, preferred_element_type=F32)
    mixer_low = finish(local_out, reach, entry, gate_rows, live, gain_row, heads)
    gathered_cot = lax.all_gather(after(cotangent, entry), "wide", axis=0, tiled=True)
    head_part = contract_cols(mixer_low, out_weight)
    own_rows = scatter_narrow(blocks_of(head_part, 0, narrow)) + lax.dynamic_slice_in_dim(
        block_input, lax.axis_index("narrow") * quarter, quarter, 0).astype(F32)
    mlp_normed, mlp_norm_back = jax.vjp(rms_norm, own_rows, gain_mlp)
    gathered_rows = line_gather([mlp_normed.astype(BF)], 3)[0]
    gate_pre = jnp.dot(gathered_rows, w_gate, preferred_element_type=F32)
    up_pre = jnp.dot(gathered_rows, w_up, preferred_element_type=F32)
    gate_sig = jax.nn.sigmoid(gate_pre)
    gate_act = gate_pre * gate_sig
    hidden_low = (gate_act * up_pre).astype(BF)
    grad_hidden = contract_cols(gathered_cot, w_down)
    grad_gate_low = (grad_hidden * up_pre * gate_sig * (1.0 + gate_pre * (1.0 - gate_sig))).astype(BF)
    grad_up_low = (grad_hidden * gate_act).astype(BF)
    grad_rows = contract_cols(grad_gate_low, w_gate) + contract_cols(grad_up_low, w_up)
    grad_mlp_normed = line_scatter([row_blocks(grad_rows)], 4)[0]
    grad_own_norm, grad_gain_mlp = mlp_norm_back(grad_mlp_normed)
    grad_own = cotangent.astype(F32) + grad_own_norm
    grad_attn = placed(gather_narrow(grad_own.astype(BF)), 0)

    hidden_late, cot_late, rows_late = after((hidden_low, gathered_cot, gathered_rows), grad_mlp_normed)
    down_rows = jnp.dot(hidden_late, w_down, preferred_element_type=F32)
    grad_w_down = contract_rows(hidden_late, cot_late).astype(BF)
    grad_w_gate = contract_rows(rows_late, grad_gate_low).astype(BF)
    grad_w_up = contract_rows(rows_late, grad_up_low).astype(BF)
    grad_w_down, grad_w_gate, grad_w_up = after((grad_w_down, grad_w_gate, grad_w_up), grad_attn)
    share_gate = scatter_narrow(blocks_of(grad_w_gate, 0, narrow))
    share_up = scatter_narrow(blocks_of(grad_w_up, 0, narrow))
    share_down = scatter_narrow(blocks_of(grad_w_down, 1, narrow))

    grad_mixer = jnp.dot(grad_attn, out_weight, preferred_element_type=F32)
    grad_outputs, grad_gate_rows, grad_out_gain, direct = unfinish(local_out, reach, entry, gate_rows, live, gain_row,
                                                                   grad_mixer, heads)
    leaving = pass_states((direct, end[:, :, DV:].astype(BF), their_map, joined_map), heads, False, 5)[0]
    leaving = after(leaving, share_gate, share_up, share_down)
    terms = [depth_blocks(contract_rows(grad_attn, mixer_low)),
             depth_blocks(contract_rows(normed_low[:row_count], grad_gate_rows)), row_blocks(down_rows)]
    (grad_mixed, grad_small, grad_taps, grad_scalars), (sum_w_out, sum_w_gate_out, sum_down) = backward_scatter(
        flags, mixed, taps, small, live, a_row, dt_row, inverses, states, grad_outputs, entry, leaving, heads, terms, 8)
    output = (own_rows + sum_down).astype(BF)
    grad_small = grad_small.astype(BF)
    grad_first = contract_rows(normed_low, grad_mixed)
    grad_small_weight = contract_rows(grad_small, normed_low[:row_count]).astype(BF)
    small_blocks = padded(grad_small_weight).reshape(16, wide, depth).transpose(1, 0, 2)
    grad_normed = contract_cols(grad_mixed, first)
    grad_next = from_behind(grad_normed[row_count:], "wide", -1)
    grad_normed = (grad_normed[:row_count] + contract_cols(grad_gate_rows, gate_weight)
                   + jnp.dot(grad_small, small_weight, preferred_element_type=F32))
    grad_normed = grad_normed.at[row_count - 16:].add(grad_next)
    _, attn_norm_back = jax.vjp(rms_norm, block_input.astype(F32), gain_attn)
    grad_input_part, grad_gain_attn = attn_norm_back(grad_normed)
    grad_input = scatter_narrow(blocks_of(grad_input_part.astype(BF), 0, narrow)) + grad_own

    head_sums = jnp.concatenate([grad_taps.reshape(-1), grad_scalars[0], grad_scalars[1]])
    whole_sums = jnp.concatenate([grad_gain_attn, grad_gain_mlp, grad_out_gain[0]])
    sums = sum_all(jnp.concatenate([head_sums, whole_sums]), "wide")
    whole_sums = sum_all(sums[head_sums.shape[0]:], "narrow")
    every = placed([p[None] for p in gather_narrow(sums[:head_sums.shape[0]])], 0)
    conv_all = every[:, :CONV * columns].reshape(narrow, CONV, columns).transpose(1, 0, 2)
    conv_parts = [conv_all[:, :, lo:hi].reshape(CONV, -1) for lo, hi in
                  ((0, key_width), (key_width, 2 * key_width), (2 * key_width, columns))]
    sum_first, sum_small = line_scatter([depth_blocks(grad_first), small_blocks], 6)
    return (
        output, grad_input, whole_sums[:d_model],
        sum_first[:, :key_width], sum_first[:, key_width:2 * key_width], sum_first[:, 2 * key_width:], sum_w_gate_out,
        sum_small[:heads].T, sum_small[heads:2 * heads].T, conv_parts[0], conv_parts[1], conv_parts[2],
        every[:, CONV * columns:CONV * columns + heads].reshape(-1), every[:, CONV * columns + heads:].reshape(-1),
        whole_sums[2 * d_model:], sum_w_out, whole_sums[d_model:2 * d_model], share_gate, share_up, share_down,
    )


def solution(mesh):
    both = P("wide", "narrow")
    rows = P(("wide", "narrow"), None)
    return jax.shard_map(
        shards,
        mesh=mesh,
        in_specs=(P("wide", None), P(), both, both, both, both, both, both, P(None, "narrow"), P(None, "narrow"),
                  P(None, "narrow"), P("narrow"), P("narrow"), P(), both, P(), P(None, "wide"), P(None, "wide"),
                  P("wide", None), P(), rows),
        out_specs=(rows, rows, P(), both, both, both, both, both, both, P(), P(), P(), P(), P(), P(), both, P(),
                   P("narrow", "wide"), P("narrow", "wide"), both),
        check_vma=False,
    )
```

time: 1210 us -> 906 us (0.75); the launches traced: 1180 us -> 897 us
  waiting for transfers between devices: 695 us -> 59 us
  Pallas kernels: 67.1 us -> 628 us
  local copies, waits for them, and re-layouts: 127 us -> 35 us
  starting transfers between devices: 110 us -> 20.3 us
  other arithmetic: 98.3 us -> 37.2 us
  matrix products: 82.6 us -> 101 us
    pallas_call x2 -> x8, Pallas kernels: 58 us -> 620 us  [the longest x2 168 us: line_scatter(): pl.pallas_call(functools.partial(scatter_kernel, count // 2, cuts), out_s...]
    ppermute x36 -> x0, waiting for transfers between devices: 355 us -> none  [turn(): lax.ppermute(value, 'wide', [(w, (w + 2 * k) % count) for w in range(coun...]
    ppermute x70 -> x26, waiting for transfers between devices: 332 us -> 59 us  [across(): lax.ppermute(value, axis, [(i, i ^ bit) for i in range(lax.axis_size(axis...]
    unnamed x329 -> x182, local copies, waits for them, and re-layouts: 72 us -> 13.5 us
    ppermute x36 -> x0, starting transfers between devices: 44.9 us -> none  [turn(): lax.ppermute(value, 'wide', [(w, (w + 2 * k) % count) for w in range(coun...]
    ppermute x70 -> x26, starting transfers between devices: 57.5 us -> 15 us  [across(): lax.ppermute(value, axis, [(i, i ^ bit) for i in range(lax.axis_size(axis...]
    mul x8 -> x0, other arithmetic: 20.7 us -> none  [the longest x1 12.5 us: short_conv(): return jax.nn.silu(running_sum)]
    concatenate x14 -> x2, local copies, waits for them, and re-layouts: 15.8 us -> 0.09 us  [the longest x1 0.08 us: shards(): sums = sum_all(jnp.concatenate([head_sums, whole_sums]), 'wide')]
  transfers between devices with their start and end apart: 108 -> 29, of which waited for: 55 -> 8; matrix products, arithmetic and copies ran while one was open for 21% -> 10% of each run, Pallas kernels for 5% -> 34%
where the time goes in v2:
time: 906 us; the launch traced here: 897 us
  Pallas kernels  628 us (69%)
  matrix products  101 us (11%)
  waiting for transfers between devices  59 us (7%)
  other arithmetic  37.2 us (4%)
  local copies, waits for them, and re-layouts  35 us (4%)
  starting transfers between devices  20.3 us (2%)
  between operations  15.6 us (2%)
    pallas_call x2, Pallas kernels, line_scatter(): pl.pallas_call(functools.partial(scatter_kernel, count // 2, cuts), out_s...  168 us
    pallas_call x2, Pallas kernels, line_gather(): pl.pallas_call(functools.partial(gather_kernel, count // 2, cuts), out_sh...  161 us
    pallas_call x1, Pallas kernels, backward_scatter(): pl.pallas_call(functools.partial(backward_scatter_kernel, heads, nb, coun...  155 us
    pallas_call x1, Pallas kernels, forward_gather(): pl.pallas_call(functools.partial(forward_gather_kernel, heads, nb, count...  92.1 us
    ppermute x26, waiting for transfers between devices, across(): lax.ppermute(value, axis, [(i, i ^ bit) for i in range(lax.axis_size(axis...  59 us
    pallas_call x2, Pallas kernels, pass_states(): pl.pallas_call(functools.partial(pass_kernel, places, heads, forward), in...  43.6 us
    dot_general x7, matrix products, contract_cols(): lax.dot_general(left, right, (((1,), (1,)), ((), ())), preferred_element_...  34.1 us
    dot_general x7, matrix products, contract_rows(): lax.dot_general(left, right, (((0,), (0,)), ((), ())), preferred_element_...  28.2 us
  transfers between devices with their start and end apart: 29, of which 8 were waited for; matrix products, arithmetic and copies ran while one was open for 10% of the time, Pallas kernels for 34%

profile of v2, /device:TPU:10, one launch (start us, length us, event | category | flops | bytes accessed | tf_op | source)
XLA Modules:
  0.0 896.9 jit_solution(9132111274168112731)
XLA Ops:
  8.3 3.4 collective-permute-start
  17.2 91.1 %shard_map.356 = (bf16[8,256,2048]{2,1,0:T(8,128)(2,1)}, bf16[8,16,256]{2,1,0:T(8,128)(2,1)}) custom-call(bf16[256,2048]{1,0:T(8,128)(2,1)} %pad_maximum_fusion.1.refs_0_, bf16[16,256]{1,0:T(8,128)(2,1)} %fusion.22.refs_1_), custom_call_target="tpu_custom_call" | custom-call | tf_op jit(solution)/shard_map/pallas_call | solution.py:492
  112.2 10.1 %convolution_convert_fusion.7.refs_1_.refs_2_.refs_3_ = bf16[528,2048]{1,0:T(8,128)(2,1)} fusion(bf16[528,2048]{1,0:T(8,128)(2,1)S(1)} %fusion.2, bf16[2048,2048]{1,0:T(8,128)(2,1)} %bitcast.120), kind=kOutput, calls=%fused_computation.25 | convolution fusion | flops 4430266368 | bytes 12713984 | tf_op jit(solution)/shard_map/dot_general | solution.py:997
  123.5 92.1 %shard_map.357 = (f32[512,1024]{1,0:T(8,128)S(1)}, bf16[512,512]{1,0:T(8,128)(2,1)S(1)}, bf16[8,4,64,64]{3,2,1,0:T(8,128)(2,1)S(1)}, bf16[8,4,128,384]{3,2,1,0:T...) custom-call(f32[8]{0:T(128)S(1)} %broadcast_select_fusion.refs_0_, ...), custom_call_target="tpu_custom_call" | custom-call | tf_op jit(solution)/shard_map/pallas_call | solution.py:672
  217.8 18.9 %shard_map.358 = (bf16[4,128,256]{2,1,0:T(8,128)(2,1)S(1)}, bf16[4,128,128]{2,1,0:T(8,128)(2,1)S(1)}, bf16[2,128,128]{2,1,0:T(8,128)(2,1)S(1)}) custom-call(f32[4,128,384]{2,1,0:T(8,128)S(1)} %get-tuple-element.69.refs_0_), custom_call_target="tpu_custom_call" | custom-call | tf_op jit(solution)/shard_map/pallas_call | solution.py:853
  238.3 6.6 fusion.12.gate_ref
  245.0 3.4 shard_map.359
  263.3 21.3 %collective-permute-done.3 = f32[128,2048]{1,0:T(8,128)} collective-permute-done((f32[128,2048]{1,0:T(8,128)}, f32[128,2048]{1,0:T(8,128)}, u32[]{:S(2)}, u32[]{:S(2)}) %collective-permute-start.3) | collective-permute-done | bytes 1048608 | tf_op jit(solution)/shard_map/ppermute | solution.py:892
  289.0 70.4 %shard_map.360 = bf16[8,128,2048]{2,1,0:T(8,128)(2,1)} custom-call(bf16[128,2048]{1,0:T(8,128)(2,1)} %multiply_convert_fusion.3.refs_0_), custom_call_target="tpu_custom_call" | custom-call | tf_op jit(solution)/shard_map/pallas_call | solution.py:492
  359.5 7.7 fusion.34
  367.2 5.9 fusion.33
  373.2 5.1 multiply_convert_fusion
  378.3 3.5 fusion.35
  381.8 5.5 add_convert_fusion
  387.3 57.2 %shard_map.361 = f32[128,2048]{1,0:T(8,128)} custom-call(bf16[8,128,2048]{2,1,0:T(8,128)(2,1)} %bitcast.97), custom_call_target="tpu_custom_call" | custom-call | tf_op jit(solution)/shard_map/pallas_call | solution.py:629
  448.2 3.3 convolution_convert_fusion.4
  460.0 5.1 convolution_convert_fusion.1
  465.2 7.9 collective-permute-done.6
  473.2 3.6 fusion.36.gm_ref
  480.9 5.4 shard_map.362
  486.3 7.1 fusion.38
  493.4 4.4 convolution_convert_fusion.3
  507.0 4.4 convolution_convert_fusion.2
  511.3 24.8 %shard_map.363.refs_13_ = bf16[4,128,256]{2,1,0:T(8,128)(2,1)S(1)} custom-call(f32[4,128,256]{2,1,0:T(8,128)S(1)} %get-tuple-element.77.refs_0_, bf16[4,128,128]{2,1,0:T(8,128)(2,1)S(1)} %slice.163.refs_1_, bf16[4,128,128]{2,1,0:T(8,128)(2,1)S(1)} %copy-done.21, bf16[2,128,128]{2,1,0:T(8,128)(2,1)S(1)} %get-tuple-element.79.refs_3_), custom_call_target="tpu_custom_call" | custom-call | tf_op jit(solution)/shard_map/pallas_call | solution.py:853
  539.0 10.2 %collective-permute-done.9 = bf16[512,688]{0,1:T(8,128)(2,1)S(1)} collective-permute-done((bf16[512,688]{0,1:T(8,128)(2,1)S(1)}, bf16[512,688]{0,1:T(8,128)(2,1)S(1)}, u32[]{:S(2)}, u32[]{:S(2)}) %collective-permute-start.9) | collective-permute-done | bytes 704544 | tf_op jit(solution)/shard_map/ppermute | solution.py:892
  550.6 154.8 %shard_map.364 = (bf16[528,2048]{1,0:T(8,128)(2,1)}, f32[512,8]{1,0:T(8,128)}, f32[4,2048]{1,0:T(4,128)}, f32[8,4]{1,0:T(8,128)}, f32[256,1024]{1,0:T(8,128)}, /*index=5*/f32[256,1024]{1,0:T(8,128)}, f32[128,2048]{1,0:T(8,128)}) custom-call(f32[8]{0:T(128)} %copy-done.25, bf16[528,2048]{1,0:T(8,128)(2,1)} %convolution_convert_fusion.7.refs_1_.refs_2_.refs_3_, ...), custom_call_target="tpu_custom_call" | custom-call | tf_op jit(solution)/shard_map/pallas_call | solution.py:730
  705.4 9.1 %fusion.37 = f32[528,2048]{1,0:T(8,128)S(1)} fusion(bf16[528,2048]{1,0:T(8,128)(2,1)} %get-tuple-element.89, bf16[2048,2048]{1,0:T(8,128)(2,1)} %bitcast.121), kind=kOutput, calls=%fused_computation.119 | convolution fusion | flops 4429185024 | bytes 14876672 | tf_op jit(solution)/shard_map/dot_general | solution.py:970
  714.5 9.1 %convolution_convert_fusion = bf16[2048,2048]{1,0:T(8,128)(2,1)} fusion(bf16[528,2048]{1,0:T(8,128)(2,1)S(1)} %copy-done.33, bf16[528,2048]{1,0:T(8,128)(2,1)S(1)} %copy-done.79), kind=kOutput, calls=%fused_computation.1 | convolution fusion | flops 4433379328 | bytes 12713984 | tf_op jit(solution)/shard_map/dot_general | solution.py:966
  727.4 110.4 %shard_map.365 = (f32[256,2048]{1,0:T(8,128)}, f32[16,256]{1,0:T(8,128)}) custom-call(bf16[8,256,2048]{2,1,0:T(8,128)(2,1)} %bitcast.96, bf16[8,16,256]{2,1,0:T(8,128)(2,1)} %bitcast.107), custom_call_target="tpu_custom_call" | custom-call | tf_op jit(solution)/shard_map/pallas_call | solution.py:629
  845.7 4.1 collective-permute-done.21
  873.7 9.1 %collective-permute-done.19 = bf16[128,2048]{1,0:T(8,128)(2,1)S(1)} collective-permute-done((bf16[128,2048]{1,0:T(8,128)(2,1)S(1)}, bf16[128,2048]{1,0:T(8,128)(2,1)S(1)}, u32[]{:S(2)}, u32[]{:S(2)}) %collective-permute-start.19) | collective-permute-done | bytes 524320 | tf_op jit(solution)/shard_map/ppermute | solution.py:892
  883.6 4.3 add_add_fusion.2
  (319 shorter events, 102.0 us)
Async XLA Ops:
  7.2 365.9 %copy-start = (bf16[2048,688]{0,1:T(8,128)(2,1)S(1)}, bf16[2048,688]{0,1:T(8,128)(2,1)}, u32[]{:S(2)}) copy-start(bf16[2048,688]{0,1:T(8,128)(2,1)} %param.40) | copy-start | bytes 8454148
  7.2 359.9 %all-gather.2.cloned.1.call-start = ((), (), s32[]{:S(2)}) async-start(), calls=%async_computation | async-start | bytes 4718592 | tf_op jit(solution)/shard_map/all_gather | solution.py:1005
  8.3 101.2 %collective-permute-start = (bf16[16,2048]{1,0:T(8,128)(2,1)S(1)}, bf16[16,2048]{1,0:T(8,128)(2,1)S(1)}, u32[]{:S(2)}, u32[]{:S(2)}) collective-permute-start(bf16[16,2048]{1,0:T(8,128)(2,1)S(1)} %slice.99), channel_id=1, source_target_pairs={{0,4},{4,8},{8,12},{12,16},{16,20},{20,24},{24,28},{1,5},{5,9},{9,... | collective-permute-start | bytes 196616 | tf_op jit(solution)/shard_map/ppermute | solution.py:881
  13.6 467.3 %copy-start.5 = (f32[512,1]{1,0:T(8,128)}, f32[512,1]{1,0:T(8,128)S(1)}, u32[]{:S(2)}) copy-start(f32[512,1]{1,0:T(8,128)S(1)} %copy.53.refs_5_.live_ref.refs_6_) | copy-start | bytes 6148
  238.2 242.6 %copy-start.6 = (bf16[4,128,256]{2,1,0:T(8,128)(2,1)}, bf16[4,128,256]{2,1,0:T(8,128)(2,1)S(1)}, u32[]{:S(2)}) copy-start(bf16[4,128,256]{2,1,0:T(8,128)(2,1)S(1)} %get-tuple-element.70.s_ref.refs_12_) | copy-start | bytes 786436
  253.4 3.0 collective-permute-start.2
  253.4 9.8 %collective-permute-start.1 = (f32[128,2048]{1,0:T(8,128)}, f32[128,2048]{1,0:T(8,128)}, u32[]{:S(2)}, u32[]{:S(2)}) collective-permute-start(f32[128,2048]{1,0:T(8,128)} %get-tuple-element.111), channel_id=1, source_target_pairs={{0,1},{1,0},{2,3},{3,2},{4,5},{5,4},{6,7},{7,6},{8,9},{9,8},{10,11... | collective-permute-start | bytes 3145736 | tf_op jit(solution)/shard_map/ppermute | solution.py:892
  259.1 25.5 %collective-permute-start.3 = (f32[128,2048]{1,0:T(8,128)}, f32[128,2048]{1,0:T(8,128)}, u32[]{:S(2)}, u32[]{:S(2)}) collective-permute-start(f32[128,2048]{1,0:T(8,128)} %dynamic-slice_add_fusion), channel_id=1, source_target_pairs={{0,2},{1,3},{2,0},{3,1},{4,6},{5,7},{6,4},{7,5},{8,10},{9,11},{10,... | collective-permute-start | bytes 3145736 | tf_op jit(solution)/shard_map/ppermute | solution.py:892
  447.5 11.0 %collective-permute-start.4 = (bf16[128,2048]{1,0:T(8,128)(2,1)S(1)}, bf16[128,2048]{1,0:T(8,128)(2,1)S(1)}, u32[]{:S(2)}, u32[]{:S(2)}) collective-permute-start(bf16[128,2048]{1,0:T(8,128)(2,1)S(1)} %get-tuple-element.103), channel_id=1, source_target_pairs={{0,1},{1,0},{2,3},{3,2},{4,5},{5,4},{6,7},{7,6},{8,9},{9,8},{10,11... | collective-permute-start | bytes 1572872 | tf_op jit(solution)/shard_map/ppermute | solution.py:892
  447.5 17.6 %collective-permute-start.5 = (bf16[128,2048]{1,0:T(8,128)(2,1)S(1)}, bf16[128,2048]{1,0:T(8,128)(2,1)S(1)}, u32[]{:S(2)}, u32[]{:S(2)}) collective-permute-start(bf16[128,2048]{1,0:T(8,128)(2,1)S(1)} %get-tuple-element.103), channel_id=1, source_target_pairs={{0,2},{1,3},{2,0},{3,1},{4,6},{5,7},{6,4},{7,5},{8,10},{9,11},{10,... | collective-permute-start | bytes 1572872 | tf_op jit(solution)/shard_map/ppermute | solution.py:892
  458.4 14.7 %collective-permute-start.6 = (bf16[128,2048]{1,0:T(8,128)(2,1)S(1)}, bf16[128,2048]{1,0:T(8,128)(2,1)S(1)}, u32[]{:S(2)}, u32[]{:S(2)}) collective-permute-start(bf16[128,2048]{1,0:T(8,128)(2,1)S(1)} %collective-permute-done.4), channel_id=1, source_target_pairs={{0,2},{1,3},{2,0},{3,1},{4,6},{5,7},{6,4},{7,5},{8,10},{9,11},{10,... | collective-permute-start | bytes 1572872 | tf_op jit(solution)/shard_map/ppermute | solution.py:892
  477.9 20.5 %collective-permute-start.14 = (bf16[688,512]{1,0:T(8,128)(2,1)S(1)}, bf16[688,512]{1,0:T(8,128)(2,1)S(1)}, u32[]{:S(2)}, u32[]{:S(2)}) collective-permute-start(bf16[688,512]{1,0:T(8,128)(2,1)S(1)} %get-tuple-element.114), channel_id=1, source_target_pairs={{0,1},{1,0},{2,3},{3,2},{4,5},{5,4},{6,7},{7,6},{8,9},{9,8},{10,11... | collective-permute-start | bytes 2113544 | tf_op jit(solution)/shard_map/ppermute | solution.py:892
  479.1 22.1 %collective-permute-start.11 = (bf16[512,688]{0,1:T(8,128)(2,1)}, bf16[512,688]{0,1:T(8,128)(2,1)}, u32[]{:S(2)}, u32[]{:S(2)}) collective-permute-start(bf16[512,688]{0,1:T(8,128)(2,1)} %get-tuple-element.116), channel_id=1, source_target_pairs={{0,1},{1,0},{2,3},{3,2},{4,5},{5,4},{6,7},{7,6},{8,9},{9,8},{10,11... | collective-permute-start | bytes 2113544 | tf_op jit(solution)/shard_map/ppermute | solution.py:892
  480.8 22.6 %collective-permute-start.8 = (bf16[512,688]{0,1:T(8,128)(2,1)}, bf16[512,688]{0,1:T(8,128)(2,1)}, u32[]{:S(2)}, u32[]{:S(2)}) collective-permute-start(bf16[512,688]{0,1:T(8,128)(2,1)} %get-tuple-element.118), channel_id=1, source_target_pairs={{0,1},{1,0},{2,3},{3,2},{4,5},{5,4},{6,7},{7,6},{8,9},{9,8},{10,11... | collective-permute-start | bytes 2113544 | tf_op jit(solution)/shard_map/ppermute | solution.py:892
  497.8 8.2 collective-permute-start.13
  498.3 39.2 %collective-permute-start.10 = (bf16[512,688]{0,1:T(8,128)(2,1)}, bf16[512,688]{0,1:T(8,128)(2,1)S(1)}, u32[]{:S(2)}, u32[]{:S(2)}) collective-permute-start(bf16[512,688]{0,1:T(8,128)(2,1)} %get-tuple-element.115), channel_id=1, source_target_pairs={{0,1},{1,0},{2,3},{3,2},{4,5},{5,4},{6,7},{7,6},{8,9},{9,8},{10,11... | collective-permute-start | bytes 2113544 | tf_op jit(solution)/shard_map/ppermute | solution.py:892
  499.2 39.8 %collective-permute-start.7 = (bf16[512,688]{0,1:T(8,128)(2,1)S(1)}, bf16[512,688]{0,1:T(8,128)(2,1)S(1)}, u32[]{:S(2)}, u32[]{:S(2)}) collective-permute-start(bf16[512,688]{0,1:T(8,128)(2,1)S(1)} %copy-done.50), channel_id=1, source_target_pairs={{0,1},{1,0},{2,3},{3,2},{4,5},{5,4},{6,7},{7,6},{8,9},{9,8},{10,11... | collective-permute-start | bytes 2113544 | tf_op jit(solution)/shard_map/ppermute | solution.py:892
  501.2 34.9 %collective-permute-start.15 = (bf16[688,512]{1,0:T(8,128)(2,1)S(1)}, bf16[688,512]{1,0:T(8,128)(2,1)S(1)}, u32[]{:S(2)}, u32[]{:S(2)}) collective-permute-start(bf16[688,512]{1,0:T(8,128)(2,1)S(1)} %add_convert_fusion.1), channel_id=1, source_target_pairs={{0,2},{1,3},{2,0},{3,1},{4,6},{5,7},{6,4},{7,5},{8,10},{9,11},{10,... | collective-permute-start | bytes 2113544 | tf_op jit(solution)/shard_map/ppermute | solution.py:892
  503.4 34.1 %collective-permute-start.12 = (bf16[512,688]{0,1:T(8,128)(2,1)S(1)}, bf16[512,688]{0,1:T(8,128)(2,1)S(1)}, u32[]{:S(2)}, u32[]{:S(2)}) collective-permute-start(bf16[512,688]{0,1:T(8,128)(2,1)S(1)} %add_convert_fusion.2), channel_id=1, source_target_pairs={{0,2},{1,3},{2,0},{3,1},{4,6},{5,7},{6,4},{7,5},{8,10},{9,11},{10,... | collective-permute-start | bytes 2113544 | tf_op jit(solution)/shard_map/ppermute | solution.py:892
  506.1 43.1 %collective-permute-start.9 = (bf16[512,688]{0,1:T(8,128)(2,1)S(1)}, bf16[512,688]{0,1:T(8,128)(2,1)S(1)}, u32[]{:S(2)}, u32[]{:S(2)}) collective-permute-start(bf16[512,688]{0,1:T(8,128)(2,1)S(1)} %add_convert_fusion.3), channel_id=1, source_target_pairs={{0,2},{1,3},{2,0},{3,1},{4,6},{5,7},{6,4},{7,5},{8,10},{9,11},{10,... | collective-permute-start | bytes 2113544 | tf_op jit(solution)/shard_map/ppermute | solution.py:892
  724.8 113.8 %collective-permute-start.16 = (f32[16,2048]{1,0:T(8,128)S(1)}, f32[16,2048]{1,0:T(8,128)S(1)}, u32[]{:S(2)}, u32[]{:S(2)}) collective-permute-start(f32[16,2048]{1,0:T(8,128)S(1)} %slice.128), channel_id=1, source_target_pairs={{4,0},{8,4},{12,8},{16,12},{20,16},{24,20},{28,24},{5,1},{9,5},{13... | collective-permute-start | bytes 393224 | tf_op jit(solution)/shard_map/ppermute | solution.py:881
  840.8 4.8 collective-permute-start.20
  845.6 4.2 collective-permute-start.21
  849.8 5.1 collective-permute-start.22
  855.0 2.5 collective-permute-start.23
  856.1 12.2 %collective-permute-start.18 = (bf16[128,2048]{1,0:T(8,128)(2,1)}, bf16[128,2048]{1,0:T(8,128)(2,1)S(1)}, u32[]{:S(2)}, u32[]{:S(2)}) collective-permute-start(bf16[128,2048]{1,0:T(8,128)(2,1)} %get-tuple-element.122), channel_id=1, source_target_pairs={{0,1},{1,0},{2,3},{3,2},{4,5},{5,4},{6,7},{7,6},{8,9},{9,8},{10,11... | collective-permute-start | bytes 1572872 | tf_op jit(solution)/shard_map/ppermute | solution.py:892
  856.6 4.9 collective-permute-start.25
  856.7 5.7 collective-permute-start.26
  857.6 6.7 collective-permute-start.24
  860.5 13.2 %collective-permute-start.17 = (bf16[128,2048]{1,0:T(8,128)(2,1)}, bf16[128,2048]{1,0:T(8,128)(2,1)S(1)}, u32[]{:S(2)}, u32[]{:S(2)}) collective-permute-start(bf16[128,2048]{1,0:T(8,128)(2,1)} %get-tuple-element.121), channel_id=1, source_target_pairs={{0,1},{1,0},{2,3},{3,2},{4,5},{5,4},{6,7},{7,6},{8,9},{9,8},{10,11... | collective-permute-start | bytes 1572872 | tf_op jit(solution)/shard_map/ppermute | solution.py:892
  863.3 4.0 collective-permute-start.27
  869.5 13.3 %collective-permute-start.19 = (bf16[128,2048]{1,0:T(8,128)(2,1)S(1)}, bf16[128,2048]{1,0:T(8,128)(2,1)S(1)}, u32[]{:S(2)}, u32[]{:S(2)}) collective-permute-start(bf16[128,2048]{1,0:T(8,128)(2,1)S(1)} %add_convert_fusion.4), channel_id=1, source_target_pairs={{0,2},{1,3},{2,0},{3,1},{4,6},{5,7},{6,4},{7,5},{8,10},{9,11},{10,... | collective-permute-start | bytes 1572872 | tf_op jit(solution)/shard_map/ppermute | solution.py:892
  (83 other events, 1380.9 us)
Sparse Core Ops, SparseCore 0:
  238.4 89.7 all-gather.1

commit v3 on v2

v3 whole, which is shorter than its diff:
```python
import functools
import jax
import jax.numpy as jnp
from jax import lax
from jax.experimental import pallas as pl
from jax.experimental.pallas import tpu as pltpu
from jax.sharding import PartitionSpec as P

DK, DV, BLOCK, EPS = 128, 256, 64, 1e-6
BF = jnp.bfloat16
F32 = jnp.float32


def mm(a, b):
    return jnp.dot(a.astype(BF), b.astype(BF), preferred_element_type=F32)


def mm_nt(a, b):
    return lax.dot_general(a.astype(BF), b.astype(BF), (((1,), (1,)), ((), ())), preferred_element_type=F32)


def mm_tn(a, b):
    return lax.dot_general(a.astype(BF), b.astype(BF), (((0,), (0,)), ((), ())), preferred_element_type=F32)


def split(a):
    high = a.astype(BF)
    return high, (a - high.astype(F32)).astype(BF)


def mm_fine(a, b):
    ah, al = split(a)
    bh, bl = split(b)
    return mm(ah, bh) + (mm(ah, bl) + mm(al, bh))


def unit_lower_inverses(systems, rows, cols):
    gap = rows ^ cols
    below = rows > cols
    unit = jnp.where(rows == cols, 1.0, 0.0)
    found = [unit - jnp.where(below & (gap < 2), a, 0.0) for a in systems]
    size = 2
    while size < systems[0].shape[0]:
        mask = below & (gap >= size) & (gap < 2 * size)
        inner = [mm_fine(jnp.where(mask, a, 0.0), t) for a, t in zip(systems, found)]
        found = [t - mm_fine(t, m) for t, m in zip(found, inner)]
        size *= 2
    return found


def block_tables(g_col, g_row, rows, cols):
    lower = rows >= cols
    return jnp.where(lower, jnp.exp(jnp.where(lower, g_col - g_row, 0.0)), 0.0)


def shifted(rows, before, back):
    if back == 0:
        return rows
    return jnp.concatenate([before[8 - back:], rows[:rows.shape[0] - back]], axis=0)


def conv_rows(rows, before, taps):
    count = taps.shape[0]
    total = taps[count - 1:count] * rows
    for back in range(1, count):
        total = total + taps[count - 1 - back:count - back] * shifted(rows, before, back)
    return total


def head_slices(heads, h):
    key = heads * DK
    return slice(h * DK, (h + 1) * DK), slice(key + h * DK, key + (h + 1) * DK), slice(2 * key + h * DV, 2 * key + (h + 1) * DV)


def unit_factor(rows):
    return lax.rsqrt(jnp.sum(rows * rows, axis=1, keepdims=True) + EPS)


def exact_tn(a, b):
    return lax.dot_general(a, b, (((0,), (0,)), ((), ())), precision=lax.Precision.HIGHEST, preferred_element_type=F32)


def softplus(x):
    return jnp.maximum(x, 0.0) + jnp.log(1.0 + jnp.exp(-jnp.abs(x)))


def decay_tables(heads, small, a_log, dt_bias, live, rows, cols):
    speed = -jnp.exp(a_log)
    biased = small[:, :heads] + dt_bias
    log_decay = speed * softplus(biased)
    sig = jax.nn.sigmoid(small[:, heads:2 * heads])
    upto = jnp.where(rows <= cols, 1.0, 0.0)
    run = exact_tn(upto, log_decay)
    run_row = exact_tn(log_decay, upto)
    return speed, biased, log_decay, sig, sig * live, run, run_row


def forward_kernel(heads, flag_ref, x_ref, rim_ref, taps_ref, small_ref, live_ref, alog_ref, dt_ref,
                   o_ref, e_ref, t_ref, z_ref, end_ref, carry, before_ref):
    step = pl.program_id(0)
    rows = lax.broadcasted_iota(jnp.int32, (BLOCK, BLOCK), 0)
    cols = lax.broadcasted_iota(jnp.int32, (BLOCK, BLOCK), 1)
    flag = flag_ref[step]

    @pl.when(step == 0)
    def _():
        before_ref[...] = rim_ref[8:16, :].astype(F32)
        unit = jnp.where(lax.broadcasted_iota(jnp.int32, (DK, DK), 0) == lax.broadcasted_iota(jnp.int32, (DK, DK), 1), 1.0, 0.0)
        for h in range(heads):
            carry[h, :, :DV] = jnp.zeros((DK, DV), F32)
            carry[h, :, DV:] = unit

    _, _, _, _, betas, run, run_row = decay_tables(heads, small_ref[...], alog_ref[...], dt_ref[...], live_ref[...], rows, cols)
    openings = flag * jnp.exp(run)
    closings = jnp.exp(run[BLOCK - 1:BLOCK] - run)

    def active(columns):
        c = conv_rows(x_ref[:, columns].astype(F32), before_ref[:, columns] * flag, taps_ref[:, columns])
        return c * jax.nn.sigmoid(c)

    tables, systems, parts = [], [], []
    for h in range(heads):
        qs, ks, vs = head_slices(heads, h)
        q, k, v = active(qs), active(ks), active(vs).astype(BF)
        q = (q * unit_factor(q) * DK ** (-0.5)).astype(BF)
        k = (k * unit_factor(k)).astype(BF)
        parts.append((q, k, v))
        table = block_tables(run[:, h:h + 1], run_row[h:h + 1, :], rows, cols)
        tables.append(table)
        systems.append(jnp.where(rows > cols, betas[:, h:h + 1] * table * mm_nt(k, k), 0.0))
    before_ref[...] = x_ref[BLOCK - 8:, :].astype(F32)
    inverses = unit_lower_inverses(systems, rows, cols)
    for h in range(heads):
        q, k, v = parts[h]
        beta, opening, closing = betas[:, h:h + 1], openings[:, h:h + 1], closings[:, h:h + 1]
        low_t = inverses[h].astype(BF)
        t_ref[0, h] = low_t
        u = mm(low_t, beta * v.astype(F32))
        w = mm(low_t, (beta * opening) * k.astype(F32))
        scores = mm_nt(q, k) * tables[h]
        state = carry[h]
        low_state = state.astype(BF)
        z_ref[0, h] = low_state
        reach = mm(jnp.concatenate([w.astype(BF), (opening * q.astype(F32)).astype(BF)], axis=0), low_state)
        c = jnp.concatenate([u, jnp.zeros((BLOCK, DK), F32)], axis=1) - reach[:BLOCK]
        low_c = c.astype(BF)
        out = reach[BLOCK:] + mm(scores, low_c)
        o_ref[:, h * DV:(h + 1) * DV] = out[:, :DV]
        e_ref[:, h * DK:(h + 1) * DK] = out[:, DV:].astype(BF)
        new = opening[BLOCK - 1:BLOCK] * state + mm_tn(closing * k.astype(F32), low_c)
        carry[h] = new
        end_ref[h] = new


def unfinish_kernel(heads, o_ref, e_ref, s_ref, gate_ref, live_ref, gain_ref, gm_ref, go_ref, gg_ref, ggain_ref, direct_ref):
    @pl.when(pl.program_id(0) == 0)
    def _():
        ggain_ref[...] = jnp.zeros_like(ggain_ref)
        direct_ref[...] = jnp.zeros_like(direct_ref)

    live = live_ref[...]
    gain = gain_ref[...]
    total = jnp.zeros((1, DV), F32)
    for h in range(heads):
        vs = slice(h * DV, (h + 1) * DV)
        e = e_ref[:, h * DK:(h + 1) * DK]
        y = (o_ref[:, vs] + mm(e, s_ref[h])) * live
        r = lax.rsqrt(jnp.mean(y * y, axis=1, keepdims=True) + EPS)
        gate = gate_ref[:, vs]
        sig = jax.nn.sigmoid(gate)
        act = gate * sig
        gm = gm_ref[:, vs]
        unit = y * r
        gn = gm * act
        total = total + jnp.sum(gn * unit, axis=0, keepdims=True)
        gn = gn * gain
        gg_ref[:, vs] = (gm * unit * gain * (sig * (1.0 + gate * (1.0 - sig)))).astype(BF)
        go = (r * (gn - unit * jnp.mean(gn * unit, axis=1, keepdims=True)) * live).astype(BF)
        go_ref[:, vs] = go
        direct_ref[h] += mm_tn(e, go)
    ggain_ref[...] += total


def unfinish(o, e, entry, gate, live, gain, gm, heads, tile=256):
    rows = o.shape[0]
    row = lambda width: pl.BlockSpec((tile, width), lambda i: (i, 0))
    return pl.pallas_call(
        functools.partial(unfinish_kernel, heads),
        grid=(rows // tile,),
        in_specs=[row(heads * DV), row(heads * DK), pl.BlockSpec((heads, DK, DV), lambda i: (0, 0, 0)), row(heads * DV),
                  row(1), pl.BlockSpec((1, DV), lambda i: (0, 0)), row(heads * DV)],
        out_specs=[row(heads * DV), row(heads * DV), pl.BlockSpec((1, DV), lambda i: (0, 0)),
                   pl.BlockSpec((heads, DK, DV), lambda i: (0, 0, 0))],
        out_shape=[jax.ShapeDtypeStruct((rows, heads * DV), BF), jax.ShapeDtypeStruct((rows, heads * DV), BF),
                   jax.ShapeDtypeStruct((1, DV), F32), jax.ShapeDtypeStruct((heads, DK, DV), F32)],
        compiler_params=pltpu.CompilerParams(vmem_limit_bytes=48 * 2**20),
    )(o, e, entry, gate, live, gain, gm)


def silu_back(c, grad):
    sig = jax.nn.sigmoid(c)
    return grad * (sig * (1.0 + c * (1.0 - sig)))


def backward_kernel(heads, flag_ref, x_ref, prev_ref, rim_ref, taps_ref, small_ref, live_ref, alog_ref, dt_ref, t_ref, z_ref,
                    go_ref, s_ref, exit_ref, gx_ref, gsmall_ref, gtaps_ref, gscalar_ref, carry, after_ref):
    step = pl.program_id(0)
    nb = pl.num_programs(0)
    at = nb - 1 - step
    rows = lax.broadcasted_iota(jnp.int32, (BLOCK, BLOCK), 0)
    cols = lax.broadcasted_iota(jnp.int32, (BLOCK, BLOCK), 1)
    last = lax.broadcasted_iota(jnp.int32, (BLOCK, 1), 0) == BLOCK - 1
    flag = flag_ref[at]
    taps_count = taps_ref.shape[0]

    @pl.when(step == 0)
    def _():
        carry[...] = exit_ref[...].astype(F32)
        after_ref[...] = jnp.zeros_like(after_ref)
        gtaps_ref[...] = jnp.zeros_like(gtaps_ref)
        gscalar_ref[...] = jnp.zeros_like(gscalar_ref)

    live = live_ref[...]
    speed, biased, log_decay, sig, betas, run, run_row = decay_tables(
        heads, small_ref[...], alog_ref[...], dt_ref[...], live, rows, cols)
    openings = flag * jnp.exp(run)
    closings = jnp.exp(run[BLOCK - 1:BLOCK] - run)
    row_block = pl.ds(pl.multiple_of(at * BLOCK, BLOCK), BLOCK)

    def inputs(columns):
        x = x_ref[:, columns].astype(F32)
        before = jnp.where(at == 0, rim_ref[8:16, columns].astype(F32), prev_ref[8:16, columns].astype(F32)) * flag
        return x, before, conv_rows(x, before, taps_ref[:, columns])

    def conv_back(columns, x, before, grad):
        taps = taps_ref[:, columns]
        later = after_ref[:, columns]
        longer = jnp.concatenate([grad, later], axis=0)
        gx = taps[taps_count - 1:taps_count] * grad
        sums = [jnp.sum(grad * x, axis=0, keepdims=True)]
        for back in range(1, taps_count):
            gx = gx + taps[taps_count - 1 - back:taps_count - back] * longer[back:back + BLOCK]
            sums.append(jnp.sum(grad * shifted(x, before, back), axis=0, keepdims=True))
        gx_ref[row_block, columns] = gx.astype(BF)
        gtaps_ref[:, columns] += jnp.concatenate(sums[::-1], axis=0)
        after_ref[:, columns] = grad[:8] * flag

    grad_runs, grad_betas = [], []
    for h in range(heads):
        qs, ks, vs = head_slices(heads, h)
        xq, bq, cq = inputs(qs)
        xk, bk, ck = inputs(ks)
        xv, bv, cv = inputs(vs)
        aq, ak = cq * jax.nn.sigmoid(cq), ck * jax.nn.sigmoid(ck)
        rq, rk_unit = unit_factor(aq), unit_factor(ak)
        uq, uk = aq * rq, ak * rk_unit
        q, k = (uq * DK ** (-0.5)).astype(BF), uk.astype(BF)
        v = (cv * jax.nn.sigmoid(cv)).astype(BF)
        qf, kf, vf = q.astype(F32), k.astype(F32), v.astype(F32)
        beta, opening, closing = betas[:, h:h + 1], openings[:, h:h + 1], closings[:, h:h + 1]
        gamma = opening[BLOCK - 1:BLOCK]
        table = block_tables(run[:, h:h + 1], run_row[h:h + 1, :], rows, cols)
        kk = mm_nt(k, k)
        scores = mm_nt(q, k) * table
        low_t = t_ref[0, h]
        u = mm(low_t, beta * vf)
        w = mm(low_t, (beta * opening) * kf)
        low_w = w.astype(BF)
        state = z_ref[0, h, :, :DV].astype(F32) + mm(z_ref[0, h, :, DV:], s_ref[h])
        low_s = state.astype(BF)
        c = u - mm(low_w, low_s)
        low_c = c.astype(BF)
        go = go_ref[:, h * DV:(h + 1) * DV]
        g = carry[h]
        low_g = g.astype(BF)
        low_ck = (closing * kf).astype(BF)
        low_oq = (opening * qf).astype(BF)
        dc = mm_tn(scores, go) + mm(low_ck, low_g)
        low_dc = dc.astype(BF)
        both = jnp.concatenate([go, low_dc], axis=0)
        carry[h] = gamma * g + mm_tn(jnp.concatenate([low_oq, -low_w], axis=0), both)
        dkeyed = mm_nt(low_c, low_g)
        dgamma = jnp.sum(jnp.sum(state * g, axis=1, keepdims=True), axis=0, keepdims=True)
        dscore = jnp.where(rows >= cols, mm_nt(go, low_c), 0.0)
        back = mm_nt(both, low_s)
        doq, dw = back[:BLOCK], -back[BLOCK:]
        drv = mm_tn(low_t, low_dc)
        drw = mm_tn(low_t, dw)
        low_drv, low_drw = drv.astype(BF), drw.astype(BF)
        da = jnp.where(rows > cols, -(mm_nt(low_drv, u) + mm_nt(low_drw, low_w)), 0.0)
        dat = da * table
        dkk = (beta * dat).astype(BF)
        dqk = (dscore * table).astype(BF)
        gq = (opening * doq + mm(dqk, k)) * DK ** (-0.5)
        gk = mm_tn(dqk, q) + mm(dkk, k) + mm_tn(dkk, k) + closing * dkeyed + (beta * opening) * drw
        gq = rq * (gq - uq * jnp.sum(gq * uq, axis=1, keepdims=True))
        gk = rk_unit * (gk - uk * jnp.sum(gk * uk, axis=1, keepdims=True))
        conv_back(qs, xq, bq, silu_back(cq, gq))
        conv_back(ks, xk, bk, silu_back(ck, gk))
        conv_back(vs, xv, bv, silu_back(cv, beta * drv))
        rk = jnp.sum(drw * kf, axis=1, keepdims=True)
        atk = dat * kk
        grad_betas.append(jnp.sum(drv * vf, axis=1, keepdims=True) + opening * rk + jnp.sum(atk, axis=1, keepdims=True))
        dopen = opening * (jnp.sum(doq * qf, axis=1, keepdims=True) + beta * rk)
        dclose = closing * jnp.sum(dkeyed * kf, axis=1, keepdims=True)
        e = dscore * scores + beta * atk
        by_col = exact_tn(e, jnp.ones((BLOCK, 8), F32))[:, :1]
        dg = jnp.sum(e, axis=1, keepdims=True) - by_col + dopen - dclose
        grad_runs.append(dg + jnp.where(last, jnp.sum(dclose, axis=0, keepdims=True) + dgamma * gamma, 0.0))

    lane = lax.broadcasted_iota(jnp.int32, (BLOCK, heads), 1)
    grad_run = sum(jnp.where(lane == h, grad_runs[h], 0.0) for h in range(heads))
    grad_beta = sum(jnp.where(lane == h, grad_betas[h], 0.0) for h in range(heads))
    grad_log = exact_tn(jnp.where(cols <= rows, 1.0, 0.0), grad_run)
    grad_biased = grad_log * speed * jax.nn.sigmoid(biased)
    gsmall_ref[:, :heads] = grad_biased
    gsmall_ref[:, heads:] = grad_beta * live * sig * (1.0 - sig)
    gscalar_ref[0:1, :] += jnp.sum(grad_log * log_decay, axis=0, keepdims=True)
    gscalar_ref[1:2, :] += jnp.sum(grad_biased, axis=0, keepdims=True)

    @pl.when(step == nb - 1)
    def _():
        longer = jnp.concatenate([jnp.zeros((16, taps_ref.shape[1]), F32), after_ref[...]], axis=0)
        gx = jnp.zeros((16, taps_ref.shape[1]), F32)
        for back in range(1, taps_count):
            gx = gx + taps_ref[taps_count - 1 - back:taps_count - back, :] * longer[back:back + 16]
        gx_ref[pl.ds(nb * BLOCK, 16), :] = gx.astype(BF)


MESH = pl.DeviceIdType.MESH


def position():
    w = lax.axis_index("wide")
    return w, w // 2, w % 2, lax.axis_index("narrow")


def greet(line=0, pair=False, cube=False, bits=(), places=0, rim=False):
    w, place, side, n = position()
    barrier = pltpu.get_barrier_semaphore()

    def signal(*device):
        pl.semaphore_signal(barrier, inc=1, device_id=device, device_id_type=MESH)

    count = 0
    if pair:
        signal(w + 1 - 2 * side, n)
        count += 1
    if cube:
        signal(w, n ^ 1)
        signal(w, n ^ 2)
        count += 2
    for bit in bits:
        signal(w ^ bit, n)
        count += 1
    if line:
        @pl.when(place > 0)
        def _():
            signal(w - 2, n)

        @pl.when(place < line - 1)
        def _():
            signal(w + 2, n)

        count = count + jnp.where(place > 0, 1, 0) + jnp.where(place < line - 1, 1, 0)
    if rim:
        @pl.when((side == 0) & (place > 0))
        def _():
            signal(w - 1, n)

        @pl.when((side == 1) & (place < line - 1))
        def _():
            signal(w + 1, n)

        count = count + jnp.where(side == 0, jnp.where(place > 0, 1, 0), jnp.where(place < line - 1, 1, 0))
    for k in range(1, places):
        for there in (place + k, place - k):
            @pl.when((there >= 0) & (there < places))
            def _():
                signal(2 * there + side, n)

    pl.semaphore_wait(barrier, count + max(places - 1, 0))


def row_cuts(rows, chunks):
    units = rows // 16
    chunks = min(chunks, units)
    edges = [16 * (units * c // chunks) for c in range(chunks + 1)]
    return [(edges[c], edges[c + 1] - edges[c]) for c in range(chunks)]


class LineGather:
    def __init__(self, places, cuts, sources, others, targets, local_sems, send_sems, recv_sems):
        self.places, self.sources, self.others, self.targets = places, sources, others, targets
        self.local_sems, self.send_sems, self.recv_sems = local_sems, send_sems, recv_sems
        self.w, self.place, self.side, self.n = position()
        self.items = [(i,) + cut for i, found in enumerate(cuts) for cut in found]

    def both(self, item):
        return self.others[self.items[item][0]] is not None

    def copy(self, item, slot, way, own=False):
        i, start, size = self.items[item]
        rows = pl.ds(start, size)
        source = self.targets[i].at[slot, rows]
        if own:
            source = (self.others if way == 0 and self.both(item) else self.sources)[i].at[rows]
        device = [self.w + 1 - 2 * self.side, self.w + 2, self.w - 2][way]
        return pltpu.make_async_remote_copy(
            src_ref=source, dst_ref=self.targets[i].at[slot, rows], send_sem=self.send_sems.at[way, slot, item],
            recv_sem=self.recv_sems.at[slot, item], device_id=(device, self.n), device_id_type=MESH)

    def start(self):
        for i, source in enumerate(self.sources):
            pltpu.make_async_copy(source, self.targets[i].at[self.w], self.local_sems.at[i]).start()
        for item in range(len(self.items)):
            self.copy(item, self.w, 0, True).start()
            self.along(item, self.w, 1, True)
            self.along(item, self.w, 2, True)

    def along(self, item, slot, way, own=False):
        @pl.when(self.place < self.places - 1 if way == 1 else self.place > 0)
        def _():
            self.copy(item, slot, way, own).start()

    def events(self):
        items = range(len(self.items))
        found = [(item, 0, 1) for item in items if self.both(item)]
        return found + [(item, t, s) for t in range(1, self.places) for item in items
                        for s in ((0, 1) if self.both(item) else (0,))]

    def run(self, event):
        item, t, s = event
        if t == 0:
            slot = self.w + 1 - 2 * self.side
            self.copy(item, slot, 0).wait_recv()
            self.along(item, slot, 1)
            self.along(item, slot, 2)
            return

        for way, there in ((1, self.place - t), (2, self.place + t)):
            slot = 2 * there + (self.side if s == 0 else 1 - self.side)

            @pl.when((there >= 0) & (there < self.places))
            def _():
                self.copy(item, slot, way).wait_recv()
                self.along(item, slot, way)
                if not self.both(item):
                    self.copy(item, slot, 0).start()

    def finish(self):
        for item in range(len(self.items)):
            if not self.both(item):
                for t in range(self.places):
                    self.copy(item, 2 * t + 1 - self.side, 0).wait_recv()
        for i, source in enumerate(self.sources):
            pltpu.make_async_copy(source, self.targets[i].at[self.w], self.local_sems.at[i]).wait()
        for item in range(len(self.items)):
            both = self.both(item)
            if both:
                self.copy(item, self.w, 0, True).wait_send()
            for t in range(self.places):
                if not both:
                    self.copy(item, 2 * t + self.side, 0).wait_send()
                for s in ((0, 1) if both else (0,)):
                    slot = 2 * t + (self.side if s == 0 else 1 - self.side)

                    @pl.when((self.place < self.places - 1) & (t <= self.place))
                    def _():
                        self.copy(item, slot, 1).wait_send()

                    @pl.when((self.place > 0) & (t >= self.place))
                    def _():
                        self.copy(item, slot, 2).wait_send()

    @staticmethod
    def scratch(count, cuts):
        items = sum(len(found) for found in cuts)
        return [pltpu.SemaphoreType.DMA((len(cuts),)), pltpu.SemaphoreType.DMA((3, count, items)),
                pltpu.SemaphoreType.DMA((count, items))]


class PairRows:
    def __init__(self, places, source, target, rim, send_sems, recv_sems, rim_send, rim_recv):
        self.places, self.source, self.target, self.rim = places, source, target, rim
        self.send_sems, self.recv_sems, self.rim_sems = send_sems, recv_sems, (rim_send, rim_recv)
        self.w, self.place, self.side, self.n = position()

    def copy(self, number, part):
        size = self.target.shape[1]
        device = [(self.w + 1 - 2 * self.side, self.n), (self.w, self.n ^ 2), (self.w, self.n ^ 1), (self.w, self.n ^ 1)][number]
        source = self.source.at[pl.ds(part * size, size)] if number == 0 else self.target.at[part]
        return pltpu.make_async_remote_copy(
            src_ref=source, dst_ref=self.target.at[part], send_sem=self.send_sems.at[number],
            recv_sem=self.recv_sems.at[part], device_id=device, device_id_type=MESH)

    def rim_copy(self, side):
        size = self.rim.shape[0]
        return pltpu.make_async_remote_copy(
            src_ref=self.source.at[pl.ds(self.source.shape[0] - size, size)], dst_ref=self.rim,
            send_sem=self.rim_sems[0].at[side], recv_sem=self.rim_sems[1],
            device_id=(2 * self.place + 2 + side, self.n), device_id_type=MESH)

    def sends_rim(self):
        return (self.side == 1) & (self.place < self.places - 1)

    def start(self):
        self.copy(0, self.n).start()

        @pl.when(self.sends_rim())
        def _():
            self.rim_copy(0).start()
            self.rim_copy(1).start()

    def events(self):
        return [0, 1]

    def run(self, event):
        if event == 0:
            self.copy(0, self.n).wait_recv()
            self.copy(1, self.n).start()
            self.copy(2, self.n).start()
        else:
            self.copy(1, self.n ^ 2).wait_recv()
            self.copy(3, self.n ^ 2).start()

    def finish(self):
        self.copy(2, self.n ^ 1).wait_recv()
        self.copy(3, self.n ^ 3).wait_recv()
        for number in range(4):
            self.copy(number, self.n ^ 2 if number == 3 else self.n).wait_send()

        @pl.when(self.place > 0)
        def _():
            self.rim_copy(0).wait_recv()

        @pl.when(self.sends_rim())
        def _():
            self.rim_copy(0).wait_send()
            self.rim_copy(1).wait_send()


def gather_kernel(places, cuts, halved, rows, *refs):
    m = len(cuts)
    sources, refs = refs[:m], refs[m:]
    others, refs = iter(refs[:sum(halved)]), refs[sum(halved):]
    others = [next(others) if h else None for h in halved]
    rows_in, refs = refs[:rows], refs[rows:]
    targets, rows_out, refs = refs[:m], refs[m:m + 2 * rows], refs[m + 2 * rows:]
    groups = [LineGather(places, cuts, sources, others, targets, *refs[:3])]
    if rows:
        groups.append(PairRows(places, rows_in[0], *rows_out, *refs[3:]))
    greet(line=places, pair=True, cube=bool(rows), rim=bool(rows))
    for group in groups[::-1]:
        group.start()
    for group, event in merged(groups):
        group.run(event)
    for group in groups[::-1]:
        group.finish()


def flat_blocks(gathered):
    return [g.reshape((g.shape[0] * g.shape[1],) + g.shape[2:]) for g in gathered]


def line_gather(values, call_id, chunks=4, rows=None):
    count = lax.axis_size("wide")
    halved = [isinstance(value, tuple) for value in values]
    sources = [value[0] if h else value for value, h in zip(values, halved)]
    others = [value[1] for value, h in zip(values, halved) if h]
    cuts = [row_cuts(value.shape[0], chunks if value.shape[0] > 64 else 1) for value in sources]
    hbm = pl.BlockSpec(memory_space=pl.ANY)
    shapes = [jax.ShapeDtypeStruct((count,) + value.shape, value.dtype) for value in sources]
    scratch = LineGather.scratch(count, cuts)
    if rows is not None:
        narrow = lax.axis_size("narrow")
        others.append(rows)
        shapes.append(jax.ShapeDtypeStruct((narrow, rows.shape[0] // narrow, rows.shape[1]), rows.dtype))
        shapes.append(jax.ShapeDtypeStruct((16, rows.shape[1]), rows.dtype))
        scratch += [pltpu.SemaphoreType.DMA((4,)), pltpu.SemaphoreType.DMA((narrow,)), pltpu.SemaphoreType.DMA((2,)),
                    pltpu.SemaphoreType.DMA]
    found = pl.pallas_call(
        functools.partial(gather_kernel, count // 2, cuts, halved, 0 if rows is None else 1),
        out_shape=shapes,
        in_specs=[hbm] * (len(sources) + len(others)),
        out_specs=[hbm] * len(shapes),
        scratch_shapes=scratch,
        compiler_params=pltpu.CompilerParams(collective_id=call_id, has_side_effects=True),
    )(*sources, *others)
    return flat_blocks(found[:-1]) + [found[-1]] if rows is not None else flat_blocks(found)


class LineScatter:
    def __init__(self, places, cuts, paired, sources, owns, pairs, lines, load_sems, pair_send, pair_recv, right_send,
                 right_recv, left_send, left_recv):
        self.places, self.paired = places, paired
        self.sources, self.owns, self.pairs, self.lines = sources, owns, pairs, lines
        self.load_sems, self.pair_sems = load_sems, (pair_send, pair_recv)
        self.right_sems, self.left_sems = (right_send, right_recv), (left_send, left_recv)
        self.w, self.place, self.side, self.n = position()
        self.items = [(i,) + cut for i, found in enumerate(cuts) for cut in found]
        self.order = [(t, item) for j in range(places // 2) for item in range(len(self.items)) for t in (places - 1 - j, j)]

    def remote(self, source, target, sems, t, item, device):
        return pltpu.make_async_remote_copy(src_ref=source, dst_ref=target, send_sem=sems[0].at[t, item],
                                            recv_sem=sems[1].at[t, item], device_id=(device, self.n), device_id_type=MESH)

    def at(self, t, item):
        i, start, size = self.items[item]
        return (t, pl.ds(start, size)) if self.paired else (t, slice(None), pl.ds(start, size))

    def across(self, t, item):
        i = self.items[item][0]
        source = self.sources[i].at[2 * t + 1 - self.side, self.at(t, item)[1]]
        return self.remote(source, self.pairs[i].at[self.at(t, item)], self.pair_sems, t, item, self.w + 1 - 2 * self.side)

    def load(self, t, item):
        i = self.items[item][0]
        slot = 2 * t + self.side if self.paired else t
        return pltpu.make_async_copy(self.sources[i].at[self.at(slot, item)], self.owns[i].at[self.at(t, item)],
                                     self.load_sems.at[t, item])

    def right(self, t, item):
        i, at = self.items[item][0], self.at(t, item)
        return self.remote(self.owns[i].at[at], self.lines[i].at[at], self.right_sems, t, item, self.w + 2)

    def left(self, t, item, arriving=False):
        i, at = self.items[item][0], self.at(t, item)
        slot = jnp.where(t == self.place - (0 if arriving else 1), self.places, t)
        return self.remote(self.owns[i].at[at], self.lines[i].at[(slot,) + at[1:]], self.left_sems, t, item, self.w - 2)

    ahead = 4

    def start(self):
        if self.sources is not None:
            for t, item in self.order:
                self.load(t, item).start()
        if self.paired:
            for t, item in self.order[:self.ahead]:
                self.across(t, item).start()

    def events(self):
        return self.order

    def run(self, event):
        t, item = event
        i, at = self.items[item][0], self.at(t, item)
        own, place, places = self.owns[i], self.place, self.places

        def add(other):
            own[at] = (own[at].astype(F32) + other[at].astype(F32)).astype(own.dtype)

        if self.sources is not None:
            self.load(t, item).wait()
        if self.paired:
            following = self.order.index(event) + self.ahead
            if following < len(self.order):
                self.across(*self.order[following]).start()
            self.across(t, item).wait_recv()
            add(self.pairs[i])

        @pl.when(t > place)
        def _():
            @pl.when(place > 0)
            def _():
                self.right(t, item).wait_recv()
                add(self.lines[i])

            self.right(t, item).start()

        @pl.when(t < place)
        def _():
            @pl.when(place < places - 1)
            def _():
                self.left(t, item, True).wait_recv()
                add(self.lines[i])

            self.left(t, item).start()

    def finish(self, outs, theirs=None):
        place, copies = self.place, []
        for item in range(len(self.items)):
            i, start, size = self.items[item]
            own, line, at, rows = self.owns[i], self.lines[i], self.at(place, item), pl.ds(start, size)

            @pl.when(place > 0)
            def _():
                self.right(place, item).wait_recv()
                own[at] = (own[at].astype(F32) + line[at].astype(F32)).astype(own.dtype)

            @pl.when(place < self.places - 1)
            def _():
                self.left(place, item, True).wait_recv()
                own[at] = (own[at].astype(F32) + line[(self.places,) + at[1:]].astype(F32)).astype(own.dtype)

            if self.paired:
                outs[i][rows] = own[at].astype(F32)
            else:
                copy = self.remote(own.at[place, 1 - self.side, rows], self.pairs[i].at[rows], self.pair_sems, 0, item,
                                   self.w + 1 - 2 * self.side)
                copy.start()
                copies.append((i, rows, copy))
                outs[i][rows] = own[place, self.side, rows].astype(F32)
        for i, rows, copy in copies:
            copy.wait()
            theirs[i][rows] = self.pairs[i][rows].astype(F32)
        for t in range(self.places):
            for item in range(len(self.items)):
                if self.paired:
                    self.across(t, item).wait_send()

                @pl.when(t > place)
                def _():
                    self.right(t, item).wait_send()

                @pl.when(t < place)
                def _():
                    self.left(t, item).wait_send()

    @staticmethod
    def scratch(places, cuts, paired, values):
        owns = [pltpu.VMEM((places,) + value.shape[1:], value.dtype) for value in values]
        pairs = owns if paired else [pltpu.VMEM(value.shape[2:], value.dtype) for value in values]
        lines = [pltpu.VMEM((places + 1,) + value.shape[1:], value.dtype) for value in values]
        items = sum(len(found) for found in cuts)
        return owns + pairs + lines + [pltpu.SemaphoreType.DMA((places, items))] * 7

    @staticmethod
    def take(places, cuts, paired, sources, refs):
        m = len(cuts)
        amount = 3 * m + 7
        groups = [refs[m * g:m * (g + 1)] for g in range(3)]
        return LineScatter(places, cuts, paired, sources, *groups, *refs[3 * m:amount]), refs[amount:]


class CubeScatter:
    def __init__(self, source, own, near, second, third, load_sems, send_sems, recv_sems):
        self.source, self.own, self.near, self.second, self.third = source, own, near, second, third
        self.load_sems, self.send_sems, self.recv_sems = load_sems, send_sems, recv_sems
        self.w, self.place, self.side, self.n = position()
        self.half = own.shape[2] // 2
        self.order = (3, 1, 2, 0)

    def block(self, s, m):
        return (self.side ^ s) * 4 + (self.n ^ m)

    def remote(self, number, source, target, device):
        return pltpu.make_async_remote_copy(src_ref=source, dst_ref=target, send_sem=self.send_sems.at[number],
                                            recv_sem=self.recv_sems.at[number], device_id=device, device_id_type=MESH)

    def cut(self, part):
        return pl.ds(part * self.half, self.half)

    def first(self, j):
        return self.remote(j, self.source.at[self.block(j // 2, 1 + 2 * (j % 2))], self.near.at[j], (self.w, self.n ^ 1))

    def load(self, j):
        return pltpu.make_async_copy(self.source.at[self.block(j // 2, 2 * (j % 2))], self.own.at[j], self.load_sems.at[j])

    def device(self, part, stage):
        return (self.w, self.n ^ 2) if part == stage else (self.w + 1 - 2 * self.side, self.n)

    def middle(self, part, k):
        j = 2 * k + 1 if part == 0 else 2 + k
        return self.remote(4 + 2 * part + k, self.own.at[j, :, self.cut(part)], self.second.at[part, k], self.device(part, 0))

    def end(self, part):
        j = 2 if part == 0 else 1
        return self.remote(8 + part, self.own.at[j, :, self.cut(part)], self.third.at[part], self.device(part, 1))

    def start(self):
        for j in self.order:
            self.load(j).start()
        for j in self.order:
            self.first(j).start()

    def events(self):
        return [("near", j) for j in self.order] + [("middle", k) for k in (1, 0)]

    def run(self, event):
        kind, j = event
        if kind == "near":
            self.load(j).wait()
            self.first(j).wait_recv()
            self.own[j] = (self.own[j].astype(F32) + self.near[j].astype(F32)).astype(self.own.dtype)
            if j % 2 == 1:
                self.middle(0, j // 2).start()
            if j // 2 == 1:
                self.middle(1, j % 2).start()
            return
        for part in (0, 1):
            self.middle(part, j).wait_recv()
            target = (2 * j if part == 0 else j, slice(None), self.cut(part))
            self.own[target] = (self.own[target].astype(F32) + self.second[part, j].astype(F32)).astype(self.own.dtype)
            if j == 1:
                self.end(part).start()

    def finish(self, out):
        for part in (0, 1):
            self.end(part).wait_recv()
            out[:, self.cut(part)] = self.own[0, :, self.cut(part)].astype(F32) + self.third[part].astype(F32)
        for j in range(4):
            self.first(j).wait_send()
        for part in (0, 1):
            for k in (0, 1):
                self.middle(part, k).wait_send()
            self.end(part).wait_send()

    @staticmethod
    def scratch(value):
        rows, columns = value.shape[1:]
        block = pltpu.VMEM((4, rows, columns), value.dtype)
        return [block, block, pltpu.VMEM((2, 2, rows, columns // 2), value.dtype),
                pltpu.VMEM((2, rows, columns // 2), value.dtype), pltpu.SemaphoreType.DMA((4,)),
                pltpu.SemaphoreType.DMA((10,)), pltpu.SemaphoreType.DMA((10,))]


class NarrowScatter:
    def __init__(self, sources, owns, nears, fars, load_sems, send_sems, recv_sems):
        self.sources, self.owns, self.nears, self.fars = sources, owns, nears, fars
        self.load_sems, self.send_sems, self.recv_sems = load_sems, send_sems, recv_sems
        self.w, self.place, self.side, self.n = position()

    def cut(self, i, m):
        size = self.owns[i].shape[2]
        return self.sources[i].at[:, pl.ds(pl.multiple_of((self.n ^ m) * size, size), size)]

    def remote(self, i, number, source, target, bit):
        return pltpu.make_async_remote_copy(
            src_ref=source, dst_ref=target, send_sem=self.send_sems.at[i, number], recv_sem=self.recv_sems.at[i, number],
            device_id=(self.w, self.n ^ bit), device_id_type=MESH)

    def near(self, i, m):
        return self.remote(i, m, self.cut(i, 1 + 2 * m), self.nears[i].at[m], 1)

    def far(self, i):
        return self.remote(i, 2, self.owns[i].at[1], self.fars[i], 2)

    def load(self, i, m):
        return pltpu.make_async_copy(self.cut(i, 2 * m), self.owns[i].at[m], self.load_sems.at[i, m])

    def start(self):
        for i in range(len(self.owns)):
            for m in (1, 0):
                self.load(i, m).start()
        for i in range(len(self.owns)):
            for m in (1, 0):
                self.near(i, m).start()

    def events(self):
        return [(kind, i) for i in range(len(self.owns)) for kind in ("high", "low")]

    def run(self, event):
        kind, i = event
        m = 1 if kind == "high" else 0
        self.load(i, m).wait()
        self.near(i, m).wait_recv()
        self.owns[i][m] = (self.owns[i][m].astype(F32) + self.nears[i][m].astype(F32)).astype(self.owns[i].dtype)
        if m == 1:
            self.far(i).start()

    def finish(self, outs):
        for i, out in enumerate(outs):
            self.far(i).wait_recv()
            out[...] = self.owns[i][0].astype(F32) + self.fars[i][...].astype(F32)
            for m in (0, 1):
                self.near(i, m).wait_send()
            self.far(i).wait_send()

    @staticmethod
    def scratch(values, narrow):
        shapes = [(value.shape[0], value.shape[1] // narrow) for value in values]
        pairs = [pltpu.VMEM((2,) + shape, value.dtype) for shape, value in zip(shapes, values)]
        m = len(values)
        return (pairs * 2 + [pltpu.VMEM(shape, value.dtype) for shape, value in zip(shapes, values)]
                + [pltpu.SemaphoreType.DMA((m, 2)), pltpu.SemaphoreType.DMA((m, 3)), pltpu.SemaphoreType.DMA((m, 3))])

    @staticmethod
    def take(sources, refs):
        m = len(sources)
        amount = 3 * m + 3
        return NarrowScatter(sources, refs[:m], refs[m:2 * m], refs[2 * m:3 * m], *refs[3 * m:amount]), refs[amount:]


def cube_scatter_kernel(x_ref, o_ref, *refs):
    cube = CubeScatter(x_ref, *refs)
    greet(pair=True, cube=True)
    cube.start()
    for event in cube.events():
        cube.run(event)
    cube.finish(o_ref)


def cube_scatter(value, call_id):
    return pl.pallas_call(
        cube_scatter_kernel,
        out_shape=jax.ShapeDtypeStruct(value.shape[1:], F32),
        in_specs=[pl.BlockSpec(memory_space=pl.ANY)],
        out_specs=pl.BlockSpec(memory_space=pltpu.VMEM),
        scratch_shapes=CubeScatter.scratch(value),
        compiler_params=pltpu.CompilerParams(collective_id=call_id, has_side_effects=True, vmem_limit_bytes=32 * 2**20),
    )(value)


def cube_gather_kernel(x_ref, o_ref, local_sem, send_sems, recv_sems):
    w, place, side, n = position()
    half = x_ref.shape[1] // 2
    devices = [(w + 1 - 2 * side, n), (w, n ^ 2), (w, n ^ 1)]

    def copy(s, m, part, way, own=False):
        slot = (side ^ s) * 4 + (n ^ m)
        columns = pl.ds(part * half, half)
        source = x_ref.at[:, columns] if own else o_ref.at[slot, :, columns]
        return pltpu.make_async_remote_copy(
            src_ref=source, dst_ref=o_ref.at[slot, :, columns], send_sem=send_sems.at[way, slot, part],
            recv_sem=recv_sems.at[slot, part], device_id=devices[way], device_id_type=MESH)

    greet(pair=True, cube=True)
    local = pltpu.make_async_copy(x_ref, o_ref.at[side * 4 + n], local_sem)
    local.start()
    sent = []

    def send(s, m, part, way, own=False):
        found = copy(s, m, part, way, own)
        found.start()
        sent.append(found)

    for way in (0, 1, 2):
        for part in (0, 1):
            send(0, 0, part, way, True)
    copy(1, 0, 0, 0).wait_recv()
    send(1, 0, 0, 1)
    copy(0, 2, 1, 1).wait_recv()
    send(0, 2, 1, 0)
    send(1, 0, 0, 2)
    send(0, 2, 1, 2)
    copy(0, 2, 0, 1).wait_recv()
    send(0, 2, 0, 2)
    copy(1, 0, 1, 0).wait_recv()
    send(1, 0, 1, 2)
    copy(1, 2, 0, 1).wait_recv()
    send(1, 2, 0, 2)
    copy(1, 2, 1, 0).wait_recv()
    send(1, 2, 1, 2)
    for s in (0, 1):
        for m in (1, 3):
            for part in (0, 1):
                copy(s, m, part, 2).wait_recv()
    local.wait()
    for found in sent:
        found.wait_send()


def cube_gather(value, call_id):
    return pl.pallas_call(
        cube_gather_kernel,
        out_shape=jax.ShapeDtypeStruct((8,) + value.shape, value.dtype),
        in_specs=[pl.BlockSpec(memory_space=pltpu.VMEM)],
        out_specs=pl.BlockSpec(memory_space=pl.ANY),
        scratch_shapes=[pltpu.SemaphoreType.DMA, pltpu.SemaphoreType.DMA((3, 8, 2)), pltpu.SemaphoreType.DMA((8, 2))],
        compiler_params=pltpu.CompilerParams(collective_id=call_id, has_side_effects=True, vmem_limit_bytes=16 * 2**20),
    )(value).reshape(8 * value.shape[0], value.shape[1])


class SmallSums:
    def __init__(self, steps, value, stages, inbox, cube, place_send, place_recv, cube_send, cube_recv):
        self.steps, self.value, self.stages, self.inbox, self.cube = steps, value, stages, inbox, cube
        self.place_sems, self.cube_sems = (place_send, place_recv), (cube_send, cube_recv)
        self.w, self.place, self.side, self.n = position()

    def step(self, i):
        return pltpu.make_async_remote_copy(
            src_ref=self.stages.at[i], dst_ref=self.inbox.at[i], send_sem=self.place_sems[0].at[i],
            recv_sem=self.place_sems[1].at[i], device_id=(self.w ^ (2 << i), self.n), device_id_type=MESH)

    def spread(self, way, s, m):
        slot = (self.side ^ s) * 4 + (self.n ^ m)
        device = [(self.w + 1 - 2 * self.side, self.n), (self.w, self.n ^ 2), (self.w, self.n ^ 1)][way]
        return pltpu.make_async_remote_copy(
            src_ref=self.cube.at[slot], dst_ref=self.cube.at[slot], send_sem=self.cube_sems[0].at[way, slot],
            recv_sem=self.cube_sems[1].at[slot], device_id=device, device_id_type=MESH)

    sent = {0: [(0, 0)], 1: [(0, 0), (1, 0)], 2: [(0, 0), (1, 0), (0, 2), (1, 2)]}
    arriving = {0: [(1, 0)], 1: [(0, 2), (1, 2)], 2: [(0, 1), (1, 1), (0, 3), (1, 3)]}

    def send(self, way):
        for s, m in self.sent[way]:
            self.spread(way, s, m).start()

    def start(self):
        self.stages[0] = self.value[...]
        self.step(0).start()

    def events(self):
        return [("place", i) for i in range(self.steps)] + [("cube", way) for way in range(3)]

    def run(self, event):
        kind, i = event
        if kind == "place":
            self.step(i).wait_recv()
            self.stages[i + 1] = self.stages[i] + self.inbox[i]
            if i + 1 < self.steps:
                self.step(i + 1).start()
            else:
                self.cube[self.side * 4 + self.n] = self.stages[i + 1]
                self.send(0)
            return
        for s, m in self.arriving[i]:
            self.spread(i, s, m).wait_recv()
        if i < 2:
            self.send(i + 1)

    def finish(self, out):
        out[...] = self.cube[...]
        for i in range(self.steps):
            self.step(i).wait_send()
        for way in range(3):
            for s, m in self.sent[way]:
                self.spread(way, s, m).wait_send()

    @staticmethod
    def scratch(steps, value):
        rows = pltpu.VMEM((steps + 1,) + value.shape, value.dtype)
        return [rows, rows, pltpu.VMEM((8,) + value.shape, value.dtype), pltpu.SemaphoreType.DMA((steps,)),
                pltpu.SemaphoreType.DMA((steps,)), pltpu.SemaphoreType.DMA((3, 8)), pltpu.SemaphoreType.DMA((8,))]


def place_bits(places):
    return [2 << i for i in range(places.bit_length() - 1)]


def scatter_kernel(places, half_cuts, pair_cuts, cubes, small, narrow, *refs):
    hm, pm = len(half_cuts), len(pair_cuts)

    def take(count):
        nonlocal refs
        found, refs = refs[:count], refs[count:]
        return found

    halves, pairs, cube_in, small_in = take(hm), take(pm), take(cubes), take(small)
    half_outs, half_theirs, pair_outs, cube_outs, small_outs = take(hm), take(hm), take(pm), take(cubes), take(small)
    groups, ends = [], []
    if hm:
        half, refs = LineScatter.take(places, half_cuts, False, halves, refs)
        groups.append(half)
        ends.append(lambda: half.finish(half_outs, half_theirs))
    if pm:
        pair, refs = LineScatter.take(places, pair_cuts, True, pairs, refs)
        groups.append(pair)
        ends.append(lambda: pair.finish(pair_outs))
    for source, out in zip(cube_in, cube_outs):
        cube = CubeScatter(source, *take(7))
        groups.append(cube)
        ends.append(lambda cube=cube, out=out: cube.finish(out))
    if small:
        sums = SmallSums(len(place_bits(places)), small_in[0], *take(7))
        groups.append(sums)
        ends.append(lambda: sums.finish(small_outs[0]))
    greet(line=places, pair=True, cube=bool(cubes), bits=place_bits(places) if small else ())
    for group in groups[::-1]:
        group.start()
    for group, event in merged(groups):
        group.run(event)
    for end in ends[:0:-1]:
        end()
    if cubes == 2:
        w, place, side, n = position()
        rim_in, rim_send, rim_recv = take(3)
        rim = pltpu.make_async_remote_copy(src_ref=cube_outs[1], dst_ref=rim_in, send_sem=rim_send, recv_sem=rim_recv,
                                           device_id=(w - 2, n), device_id_type=MESH)
        last = (side == 1) & (n == narrow - 1)

        @pl.when(last & (place > 0))
        def _():
            rim.start()

        @pl.when(last & (place < places - 1))
        def _():
            rim.wait_recv()
            rows = pl.ds(cube_outs[0].shape[0] - rim_in.shape[0], rim_in.shape[0])
            cube_outs[0][rows] = cube_outs[0][rows] + rim_in[...]

        @pl.when(last & (place > 0))
        def _():
            rim.wait_send()
    ends[0]()


def merged(groups):
    found = []
    for order, group in enumerate(groups):
        events = group.events()
        found += [((i + 0.5) / len(events), order, i, group, event) for i, event in enumerate(events)]
    return [(group, event) for _, _, _, group, event in sorted(found, key=lambda e: e[:3])]


def place_blocks(term, places):
    return term.reshape(places, 2, term.shape[0] // (2 * places), term.shape[1])


def line_scatter(halves, pairs, cubes, small, call_id, chunks=4):
    places = lax.axis_size("wide") // 2
    halves = [place_blocks(term, places) for term in halves]
    half_cuts = [row_cuts(term.shape[2], chunks) for term in halves]
    pair_cuts = [row_cuts(term.shape[1], chunks if term.shape[1] > 64 else 1) for term in pairs]
    shapes = [term.shape[2:] for term in halves] * 2 + [term.shape[1:] for term in list(pairs) + list(cubes)]
    shapes += [(8,) + term.shape for term in small]
    scratch = []
    if halves:
        scratch += LineScatter.scratch(places, half_cuts, False, halves)
    if pairs:
        scratch += LineScatter.scratch(places, pair_cuts, True, pairs)
    for term in cubes:
        scratch += CubeScatter.scratch(term)
    for term in small:
        scratch += SmallSums.scratch(len(place_bits(places)), term)
    if cubes:
        scratch += [pltpu.VMEM(cubes[1].shape[1:], F32), pltpu.SemaphoreType.DMA, pltpu.SemaphoreType.DMA]
    vmem = pl.BlockSpec(memory_space=pltpu.VMEM)
    found = pl.pallas_call(
        functools.partial(scatter_kernel, places, half_cuts, pair_cuts, len(cubes), len(small), lax.axis_size("narrow")),
        out_shape=[jax.ShapeDtypeStruct(shape, F32) for shape in shapes],
        in_specs=[pl.BlockSpec(memory_space=pl.ANY)] * (len(halves) + len(pairs) + len(cubes)) + [vmem] * len(small),
        out_specs=[vmem] * len(shapes),
        scratch_shapes=scratch,
        compiler_params=pltpu.CompilerParams(collective_id=call_id, has_side_effects=True, vmem_limit_bytes=56 * 2**20),
    )(*halves, *pairs, *cubes, *small)
    h, p, c = len(halves), len(pairs), len(cubes)
    return list(zip(found[:h], found[h:2 * h])), found[2 * h:2 * h + p], found[2 * h + p:2 * h + p + c], found[2 * h + p + c:]


class PassStates:
    def __init__(self, places, forward, mine, turned, total, send_sems, recv_sems):
        self.places, self.forward, self.ahead = places, forward, 1 if forward else -1
        self.mine, self.turned, self.total = mine, turned, total
        self.send_sems, self.recv_sems = send_sems, recv_sems
        self.w, self.place, self.side, self.n = position()

    def copy(self, k):
        return pltpu.make_async_remote_copy(
            src_ref=self.mine, dst_ref=self.turned.at[k], send_sem=self.send_sems.at[k], recv_sem=self.recv_sems.at[k],
            device_id=(self.w + 2 * self.ahead * k, self.n), device_id_type=MESH)

    def inside(self, there):
        return (there >= 0) & (there < self.places)

    def start(self, state, maps):
        self.mine[:, :, :DV] = state.astype(BF)
        self.mine[:, :, DV:] = maps.astype(BF)
        for k in range(1, self.places):
            @pl.when(self.inside(self.place + self.ahead * k))
            def _():
                self.copy(k).start()

    def finish(self, out):
        total, turned = self.total, self.turned
        total[...] = jnp.zeros_like(total)
        for k in range(self.places - 1, 0, -1):
            @pl.when(self.inside(self.place - self.ahead * k))
            def _():
                self.copy(k).wait_recv()
                for h in range(total.shape[0]):
                    apply = mm if self.forward else mm_tn
                    total[h] = apply(turned[k, h, :, DV:], total[h]) + turned[k, h, :, :DV].astype(F32)

        out[...] = total[...].astype(out.dtype)
        for k in range(1, self.places):
            @pl.when(self.inside(self.place + self.ahead * k))
            def _():
                self.copy(k).wait_send()

    @staticmethod
    def scratch(places, heads):
        return [pltpu.VMEM((heads, DK, DV + DK), BF), pltpu.VMEM((places, heads, DK, DV + DK), BF),
                pltpu.VMEM((heads, DK, DV), F32), pltpu.SemaphoreType.DMA((places,)), pltpu.SemaphoreType.DMA((places,))]


def forward_gather_kernel(heads, nb, places, cuts, halved, *refs):
    m = len(cuts)
    inputs, sources, refs = refs[:8], refs[8:8 + m], refs[8 + m:]
    others, refs = iter(refs[:sum(halved)]), refs[sum(halved):]
    others = [next(others) if h else None for h in halved]
    outs, entry_ref, targets, refs = refs[:5], refs[5], refs[6:6 + m], refs[6 + m:]
    gather = LineGather(places, cuts, sources, others, targets, *refs[2:5])
    states = PassStates(places, True, *refs[5:])
    step = pl.program_id(0)

    @pl.when(step == 0)
    def _():
        greet(line=places, pair=True, places=places)
        gather.start()

    forward_kernel(heads, *inputs, *outs, *refs[:2])
    events = gather.events()
    early = min(len(events) // 2, nb)
    for i in range(nb):
        @pl.when(step == i)
        def _():
            for event in events[early * i // nb:early * (i + 1) // nb]:
                gather.run(event)

    @pl.when(step == nb - 1)
    def _():
        states.start(outs[4][:, :, :DV], outs[4][:, :, DV:])
        for event in events[early:(early + len(events)) // 2]:
            gather.run(event)
        states.finish(entry_ref)
        for event in events[(early + len(events)) // 2:]:
            gather.run(event)
        gather.finish()


def forward_gather(flags, mixed, taps, small, live, a_log, dt_bias, heads, blocks, call_id, chunks=2):
    rows, width = live.shape[0], mixed.shape[1]
    nb = rows // BLOCK
    count = lax.axis_size("wide")
    halved = [isinstance(block, tuple) for block in blocks]
    others = [b[1] for b, h in zip(blocks, halved) if h]
    blocks = [b[0] if h else b for b, h in zip(blocks, halved)]
    cuts = [row_cuts(block.shape[0], chunks) for block in blocks]
    row = lambda width: pl.BlockSpec((BLOCK, width), lambda i: (i, 0))
    same = lambda *shape: pl.BlockSpec(shape, lambda i: (0,) * len(shape))
    hbm = pl.BlockSpec(memory_space=pl.ANY)
    found = pl.pallas_call(
        functools.partial(forward_gather_kernel, heads, nb, count // 2, cuts, halved),
        grid=(nb,),
        in_specs=[pl.BlockSpec(memory_space=pltpu.SMEM), row(width), pl.BlockSpec((16, width), lambda i: (rows // 16, 0)),
                  same(*taps.shape), row(small.shape[1]), row(1), same(1, heads), same(1, heads)]
                 + [hbm] * (len(blocks) + len(others)),
        out_specs=[row(heads * DV), row(heads * DK),
                   pl.BlockSpec((1, heads, BLOCK, BLOCK), lambda i: (i, 0, 0, 0)),
                   pl.BlockSpec((1, heads, DK, DV + DK), lambda i: (i, 0, 0, 0)),
                   same(heads, DK, DV + DK), same(heads, DK, DV)] + [hbm] * len(blocks),
        out_shape=[jax.ShapeDtypeStruct((rows, heads * DV), F32), jax.ShapeDtypeStruct((rows, heads * DK), BF),
                   jax.ShapeDtypeStruct((nb, heads, BLOCK, BLOCK), BF),
                   jax.ShapeDtypeStruct((nb, heads, DK, DV + DK), BF),
                   jax.ShapeDtypeStruct((heads, DK, DV + DK), F32), jax.ShapeDtypeStruct((heads, DK, DV), BF)]
                  + [jax.ShapeDtypeStruct((count,) + block.shape, block.dtype) for block in blocks],
        scratch_shapes=[pltpu.VMEM((heads, DK, DV + DK), F32), pltpu.VMEM((8, width), F32)]
                       + LineGather.scratch(count, cuts) + PassStates.scratch(count // 2, heads),
        compiler_params=pltpu.CompilerParams(collective_id=call_id, has_side_effects=True, vmem_limit_bytes=48 * 2**20),
    )(flags, mixed, mixed, taps, small, live, a_log, dt_bias, *blocks, *others)
    return found[:6], flat_blocks(found[6:])


def backward_scatter_kernel(heads, nb, places, half_cuts, pair_cuts, shares, *refs):
    hm, pm = len(half_cuts), len(pair_cuts)

    def take(count):
        nonlocal refs
        found, refs = refs[:count], refs[count:]
        return found

    inputs, halves, pairs, share_in = tuple(take(15)), take(hm), take(pm), take(shares)
    outs, half_outs, half_theirs, pair_outs, share_outs = take(4), take(hm), take(hm), take(pm), take(shares)
    scratch = take(2)
    states, exit_ref = PassStates(places, False, *take(5)), take(1)[0]
    direct_ref, end_ref = inputs[-2:]
    inputs = inputs[:-2] + (exit_ref,)
    half, refs = LineScatter.take(places, half_cuts, False, halves, refs)
    groups = [half]
    if pm:
        pair, refs = LineScatter.take(places, pair_cuts, True, pairs, refs)
        groups.append(pair)
    share, refs = NarrowScatter.take(share_in, refs)
    groups.append(share)
    step = pl.program_id(0)

    @pl.when(step == 0)
    def _():
        greet(line=places, pair=True, cube=True, places=places)
        states.start(direct_ref[...], end_ref[:, :, DV:])
        for group in groups:
            group.start()
        states.finish(exit_ref)

    backward_kernel(heads, *inputs, *outs, *scratch)
    events = merged(groups)
    for i in range(nb):
        @pl.when(step == i)
        def _():
            for group, event in events[len(events) * i // nb:len(events) * (i + 1) // nb]:
                group.run(event)

    @pl.when(step == nb - 1)
    def _():
        share.finish(share_outs)
        if pm:
            pair.finish(pair_outs)
        half.finish(half_outs, half_theirs)


def backward_scatter(flags, mixed, taps, small, live, a_log, dt_bias, t, z, go, entry, direct, end, heads, halves, pairs, shares, call_id,
                     chunks=2):
    rows, width = live.shape[0], mixed.shape[1]
    nb = rows // BLOCK
    places = lax.axis_size("wide") // 2
    halves = [place_blocks(term, places) for term in halves]
    half_cuts = [row_cuts(term.shape[2], chunks) for term in halves]
    pair_cuts = [row_cuts(term.shape[1], chunks) for term in pairs]
    h = len(halves)
    narrow = lax.axis_size("narrow")
    sums = [term.shape[2:] for term in halves] * 2 + [term.shape[1:] for term in pairs]
    sums += [(term.shape[0], term.shape[1] // narrow) for term in shares]
    row = lambda width: pl.BlockSpec((BLOCK, width), lambda i: (nb - 1 - i, 0))
    same = lambda *shape: pl.BlockSpec(shape, lambda i: (0,) * len(shape))
    prev = pl.BlockSpec((16, width), lambda i: (jnp.maximum((nb - 1 - i) * (BLOCK // 16) - 1, 0), 0))
    found = pl.pallas_call(
        functools.partial(backward_scatter_kernel, heads, nb, places, half_cuts, pair_cuts, len(shares)),
        grid=(nb,),
        in_specs=[pl.BlockSpec(memory_space=pltpu.SMEM), row(width), prev,
                  pl.BlockSpec((16, width), lambda i: (rows // 16, 0)), same(*taps.shape), row(small.shape[1]), row(1),
                  same(1, heads), same(1, heads),
                  pl.BlockSpec((1, heads, BLOCK, BLOCK), lambda i: (nb - 1 - i, 0, 0, 0)),
                  pl.BlockSpec((1, heads, DK, DV + DK), lambda i: (nb - 1 - i, 0, 0, 0)),
                  row(heads * DV), same(heads, DK, DV), same(heads, DK, DV), same(heads, DK, DV + DK)]
                 + [pl.BlockSpec(memory_space=pl.ANY)] * (len(halves) + len(pairs) + len(shares)),
        out_specs=[same(rows + 16, width), row(2 * heads), same(*taps.shape), same(8, heads)]
                  + [pl.BlockSpec(shape, lambda i: (0, 0), pipeline_mode=pl.Buffered(1)) for shape in sums],
        out_shape=[jax.ShapeDtypeStruct((rows + 16, width), BF), jax.ShapeDtypeStruct((rows, 2 * heads), F32),
                   jax.ShapeDtypeStruct(taps.shape, F32), jax.ShapeDtypeStruct((8, heads), F32)]
                  + [jax.ShapeDtypeStruct(shape, F32) for shape in sums],
        scratch_shapes=[pltpu.VMEM((heads, DK, DV), F32), pltpu.VMEM((8, width), F32)]
                       + PassStates.scratch(places, heads) + [pltpu.VMEM((heads, DK, DV), F32)]
                       + LineScatter.scratch(places, half_cuts, False, halves)
                       + (LineScatter.scratch(places, pair_cuts, True, pairs) if pairs else [])
                       + NarrowScatter.scratch(shares, narrow),
        compiler_params=pltpu.CompilerParams(collective_id=call_id, has_side_effects=True, vmem_limit_bytes=58 * 2**20),
    )(flags, mixed, mixed, mixed, taps, small, live, a_log, dt_bias, t, z, go, entry, direct, end, *halves, *pairs, *shares)
    p = len(pairs)
    return (found[:4], list(zip(found[4:4 + h], found[4 + h:4 + 2 * h])), found[4 + 2 * h:4 + 2 * h + p],
            found[4 + 2 * h + p:])


TILE = 256


def place_rows(side_ref, own_ref, their_ref):
    return jnp.where(pl.program_id(0) // (pl.num_programs(0) // 2) == side_ref[0], own_ref[...], their_ref[...]).astype(F32)


def project_kernel(side_ref, own_ref, their_ref, rim_ref, gain_ref, w_ref, sw_ref, normed_ref, mixed_ref, small_ref):
    step = pl.program_id(0)

    def normal(x):
        return (x * lax.rsqrt(jnp.mean(x * x, axis=1, keepdims=True) + EPS) * gain_ref[...]).astype(BF)

    @pl.when(step < pl.num_programs(0) - 1)
    def _():
        normed = normal(place_rows(side_ref, own_ref, their_ref))
        normed_ref[...] = normed
        mixed_ref[...] = mm(normed, w_ref[...]).astype(BF)
        small_ref[...] = mm_nt(normed, sw_ref[...])

    @pl.when(step == pl.num_programs(0) - 1)
    def _():
        normed = normal(rim_ref[...].astype(F32))
        normed_ref[:16] = normed
        mixed_ref[:16] = mm(normed, w_ref[...]).astype(BF)


def row_specs(rows):
    tiles = 2 * rows // TILE
    held = lambda width: pl.BlockSpec((TILE, width), lambda i: (jnp.minimum(i, tiles - 1) % (tiles // 2), 0))
    tile = lambda width: pl.BlockSpec((TILE, width), lambda i: (jnp.minimum(i, tiles - 1), 0))
    every = lambda width: pl.BlockSpec((TILE, width), lambda i: (i, 0))
    same = lambda *shape: pl.BlockSpec(shape, lambda i: (0,) * len(shape))
    return tiles + 1, held, tile, every, same


def project(side, own, their, rim, gain, weight, small_weight):
    rows, width = own.shape
    steps, held, tile, every, same = row_specs(rows)
    columns = weight.shape[1]
    return pl.pallas_call(
        project_kernel,
        grid=(steps,),
        in_specs=[pl.BlockSpec(memory_space=pltpu.SMEM), held(width), held(width), same(16, width), same(1, width),
                  same(*weight.shape), same(*small_weight.shape)],
        out_specs=[every(width), every(columns), tile(small_weight.shape[0])],
        out_shape=[jax.ShapeDtypeStruct((2 * rows + 16, width), BF), jax.ShapeDtypeStruct((2 * rows + 16, columns), BF),
                   jax.ShapeDtypeStruct((2 * rows, small_weight.shape[0]), F32)],
        compiler_params=pltpu.CompilerParams(vmem_limit_bytes=48 * 2**20),
    )(side, own, their, rim, gain, weight, small_weight)


def unproject_kernel(side_ref, own_ref, their_ref, rim_ref, gain_ref, gm_ref, gg_ref, gs_ref, w_ref, gw_ref, sw_ref, back_ref,
                     rim_back_ref, grad_gain_ref):
    step = pl.program_id(0)

    @pl.when(step == 0)
    def _():
        grad_gain_ref[...] = jnp.zeros_like(grad_gain_ref)

    def norm_back(x, grad):
        factor = lax.rsqrt(jnp.mean(x * x, axis=1, keepdims=True) + EPS)
        unit = x * factor
        grad_gain_ref[...] += jnp.sum(grad * unit, axis=0, keepdims=True)
        scaled = grad * gain_ref[...]
        return (factor * (scaled - unit * jnp.mean(scaled * unit, axis=1, keepdims=True))).astype(BF)

    @pl.when(step < pl.num_programs(0) - 1)
    def _():
        grad = mm_nt(gm_ref[...], w_ref[...]) + mm_nt(gg_ref[...], gw_ref[...])
        for i in range(sw_ref.shape[0]):
            grad = grad + gs_ref[:, i:i + 1] * sw_ref[i:i + 1]
        back_ref[...] = norm_back(place_rows(side_ref, own_ref, their_ref), grad)

    @pl.when(step == pl.num_programs(0) - 1)
    def _():
        rim_back_ref[...] = norm_back(rim_ref[...].astype(F32), mm_nt(gm_ref[:16], w_ref[...]))


def unproject(side, own, their, rim, gain, grad_mixed, grad_gate, grad_small, weight, gate_weight, small_weight):
    rows, width = own.shape
    steps, held, tile, every, same = row_specs(rows)
    return pl.pallas_call(
        unproject_kernel,
        grid=(steps,),
        in_specs=[pl.BlockSpec(memory_space=pltpu.SMEM), held(width), held(width), same(16, width), same(1, width),
                  every(weight.shape[1]), tile(gate_weight.shape[1]), tile(grad_small.shape[1]), same(*weight.shape),
                  same(*gate_weight.shape), same(*small_weight.shape)],
        out_specs=[tile(width), same(16, width), same(1, width)],
        out_shape=[jax.ShapeDtypeStruct((2 * rows, width), BF), jax.ShapeDtypeStruct((16, width), BF),
                   jax.ShapeDtypeStruct((1, width), F32)],
        compiler_params=pltpu.CompilerParams(vmem_limit_bytes=56 * 2**20),
    )(side, own, their, rim, gain, grad_mixed, grad_gate, grad_small, weight, gate_weight, small_weight)


def mix_kernel(heads, x_ref, gw_ref, ow_ref, o_ref, e_ref, s_ref, live_ref, gain_ref, gate_ref, m_ref, out_ref):
    live = live_ref[...]
    gain = gain_ref[...]
    gates = mm(x_ref[...], gw_ref[...])
    gate_ref[...] = gates
    for h in range(heads):
        vs = slice(h * DV, (h + 1) * DV)
        y = (o_ref[:, vs] + mm(e_ref[:, h * DK:(h + 1) * DK], s_ref[h])) * live
        r = lax.rsqrt(jnp.mean(y * y, axis=1, keepdims=True) + EPS)
        gate = gates[:, vs]
        m_ref[:, vs] = (y * r * gain * (gate * jax.nn.sigmoid(gate))).astype(BF)
    out_ref[...] = mm_nt(m_ref[...], ow_ref[...]).astype(BF)


def mix(normed, gate_weight, out_weight, o, e, entry, live, gain, heads):
    rows, width = o.shape[0], normed.shape[1]
    row = lambda width: pl.BlockSpec((TILE, width), lambda i: (i, 0))
    same = lambda *shape: pl.BlockSpec(shape, lambda i: (0,) * len(shape))
    return pl.pallas_call(
        functools.partial(mix_kernel, heads),
        grid=(rows // TILE,),
        in_specs=[row(width), same(*gate_weight.shape), same(*out_weight.shape), row(heads * DV), row(heads * DK),
                  same(heads, DK, DV), row(1), same(1, DV)],
        out_specs=[row(heads * DV), row(heads * DV), row(width)],
        out_shape=[jax.ShapeDtypeStruct((rows, heads * DV), F32), jax.ShapeDtypeStruct((rows, heads * DV), BF),
                   jax.ShapeDtypeStruct((rows, width), BF)],
        compiler_params=pltpu.CompilerParams(vmem_limit_bytes=48 * 2**20),
    )(normed, gate_weight, out_weight, o, e, entry, live, gain)


def feed_kernel(places, chunks, own_ref, cot_hbm, wg_hbm, wu_hbm, wd_hbm, sum_ref, down_hbm, dwd_hbm, dwg_hbm, dwu_hbm,
                rows, cot, wg, wu, wd, hid, gg, gu, gr, pair, line, dn, dwd, dwg, dwu, load_sems, out_sems, own_sem,
                ag_send, ag_recv, pair_send, pair_recv, right_send, right_recv, left_send, left_recv):
    w, place, side, n = position()
    partner = w + 1 - 2 * side
    quarter, width = own_ref.shape
    size = quarter // chunks
    part = lambda c: pl.ds(c * size, size)
    devices = [(partner, n), (w + 2, n), (w - 2, n)]
    loads = [pltpu.make_async_copy(source, target, load_sems.at[i]) for i, (source, target) in enumerate(
        ((wg_hbm, wg), (wu_hbm, wu), (cot_hbm, cot), (wd_hbm, wd)))]

    def remote(source, target, send, recv, device):
        return pltpu.make_async_remote_copy(src_ref=source, dst_ref=target, send_sem=send, recv_sem=recv, device_id=device,
                                            device_id_type=MESH)

    def move(slot, way, c, own=False):
        source = own_ref.at[part(c)] if own else rows.at[slot, part(c)]
        return remote(source, rows.at[slot, part(c)], ag_send.at[way, slot, c], ag_recv.at[slot, c], devices[way])

    def along(slot, way, c, own=False):
        @pl.when(place < places - 1 if way == 1 else place > 0)
        def _():
            move(slot, way, c, own).start()

    def across(t, c):
        return remote(gr.at[2 * t + 1 - side, part(c)], pair.at[t, part(c)], pair_send.at[t, c], pair_recv.at[t, c], devices[0])

    def right(t, c):
        return remote(gr.at[2 * t + side, part(c)], line.at[t, part(c)], right_send.at[t, c], right_recv.at[t, c], devices[1])

    def left(t, c, arriving=False):
        slot = jnp.where(t == place - (0 if arriving else 1), places, t)
        return remote(gr.at[2 * t + side, part(c)], line.at[slot, part(c)], left_send.at[t, c], left_recv.at[t, c], devices[2])

    def inside(there):
        return (there >= 0) & (there < places)

    def arrive(s):
        for way, there in ((1, place - s), (2, place + s)):
            @pl.when(inside(there))
            def _():
                for c in range(chunks):
                    move(2 * there + side, way, c).wait_recv()
                    along(2 * there + side, way, c)
                    move(2 * there + side, 0, c).start()

    def work(there):
        for c in range(chunks):
            move(2 * there + 1 - side, 0, c).wait_recv()
        both = pl.ds(2 * there, 2)
        flat = lambda ref: ref[both].reshape(2 * quarter, ref.shape[2])
        x = flat(rows)
        gate = mm_nt(x, wg[...])
        up = mm_nt(x, wu[...])
        grad = mm_nt(flat(cot), wd[...])
        sig = jax.nn.sigmoid(gate)
        act = gate * sig
        hid[both] = (act * up).astype(BF).reshape(2, quarter, -1)
        low_gate = (grad * up * (sig + act * (1.0 - sig))).astype(BF)
        low_up = (grad * act).astype(BF)
        gg[both] = low_gate.reshape(2, quarter, -1)
        gu[both] = low_up.reshape(2, quarter, -1)
        gr[both] = (mm(low_gate, wg[...]) + mm(low_up, wu[...])).astype(BF).reshape(2, quarter, width)
        for c in range(chunks):
            across(there, c).start()

    def add(t, c, other, slot):
        at = (2 * t + side, part(c))
        gr[at] = (gr[at].astype(F32) + other[slot, part(c)].astype(F32)).astype(BF)

    def pass_on(s):
        t = s

        @pl.when(place < t)
        def _():
            for c in range(chunks):
                across(t, c).wait_recv()
                add(t, c, pair, t)

                @pl.when(place > 0)
                def _():
                    right(t, c).wait_recv()
                    add(t, c, line, t)

                right(t, c).start()

        t_left = places - 1 - s

        @pl.when(place > t_left)
        def _():
            for c in range(chunks):
                across(t_left, c).wait_recv()
                add(t_left, c, pair, t_left)

                @pl.when(place < places - 1)
                def _():
                    left(t_left, c, True).wait_recv()
                    add(t_left, c, line, t_left)

                left(t_left, c).start()

    greet(line=places, pair=True)
    for load in loads:
        load.start()
    for c in range(chunks):
        move(w, 0, c, True).start()
        along(w, 1, c, True)
        along(w, 2, c, True)
    own = pltpu.make_async_copy(own_ref, rows.at[w], own_sem)
    own.start()
    own.wait()
    for load in loads:
        load.wait()

    def rows_work(s, _):
        @pl.when(inside(place - s))
        def _():
            work(place - s)

        @pl.when(inside(place + s) & (s > 0))
        def _():
            work(place + s)
        return 0

    def advance(s, _):
        arrive(s)
        rows_work(s - 1, 0)

        @pl.when(s > 1)
        def _():
            pass_on(s - 1)
        return 0

    lax.fori_loop(1, places, advance, 0)
    rows_work(places - 1, 0)

    columns = width // 4

    def weights(i, _):
        cut = pl.ds(pl.multiple_of(i * columns, columns), columns)
        everything = lambda ref: ref[...].reshape(2 * places * quarter, ref.shape[2])
        slot = lax.rem(i, 2)

        @pl.when(i >= 2)
        def _():
            pltpu.make_async_copy(dn.at[slot], down_hbm.at[pl.ds(0, 2)], out_sems.at[3 + slot]).wait()

        dwd[:, cut] = mm_tn(everything(hid), cot[:, :, cut].reshape(2 * places * quarter, columns)).astype(BF)
        x = rows[:, :, cut].reshape(2 * places * quarter, columns)
        dwg[:, cut] = mm_tn(everything(gg), x).astype(BF)
        dwu[:, cut] = mm_tn(everything(gu), x).astype(BF)
        both = pl.ds(2 * i, 2)
        dn[slot] = jnp.dot(hid[both].reshape(2 * quarter, hid.shape[2]), wd[...],
                           preferred_element_type=F32).astype(BF).reshape(2, quarter, width)
        pltpu.make_async_copy(dn.at[slot], down_hbm.at[both], out_sems.at[3 + slot]).start()
        return 0

    before = jnp.where((place > 0) & (place < places - 1), 2, 0)
    lax.fori_loop(0, before, weights, 0)
    pass_on(places - 1)
    lax.fori_loop(before, 4, weights, 0)
    outs = [pltpu.make_async_copy(source, target, out_sems.at[i]) for i, (source, target) in enumerate(
        ((dwd, dwd_hbm), (dwg, dwg_hbm), (dwu, dwu_hbm)))]
    for out in outs:
        out.start()
    for c in range(chunks):
        across(place, c).wait_recv()
        add(place, c, pair, place)

        @pl.when(place > 0)
        def _():
            right(place, c).wait_recv()
            add(place, c, line, place)

        @pl.when(place < places - 1)
        def _():
            left(place, c, True).wait_recv()
            add(place, c, line, places)

        sum_ref[part(c)] = gr[2 * place + side, part(c)].astype(F32)
    for out in outs:
        out.wait()
    for slot in range(2):
        pltpu.make_async_copy(dn.at[slot], down_hbm.at[pl.ds(0, 2)], out_sems.at[3 + slot]).wait()

    def settle(t, _):
        for c in range(chunks):
            across(t, c).wait_send()
            move(2 * t + side, 0, c).wait_send()

            @pl.when((place < places - 1) & (t <= place))
            def _():
                move(2 * t + side, 1, c).wait_send()

            @pl.when((place > 0) & (t >= place))
            def _():
                move(2 * t + side, 2, c).wait_send()

            @pl.when(t > place)
            def _():
                right(t, c).wait_send()

            @pl.when(t < place)
            def _():
                left(t, c).wait_send()
        return 0

    lax.fori_loop(0, places, settle, 0)


def feed(own, cot, w_gate, w_up, w_down, call_id, chunks=2):
    count = lax.axis_size("wide")
    places = count // 2
    quarter, width = own.shape
    units = w_down.shape[0]
    hbm, vmem = pl.BlockSpec(memory_space=pl.ANY), pl.BlockSpec(memory_space=pltpu.VMEM)
    blocks = lambda columns: pltpu.VMEM((count, quarter, columns), BF)
    line = lambda amount: pltpu.VMEM((amount, quarter, width), BF)
    sems = pltpu.SemaphoreType.DMA((places, chunks))
    return pl.pallas_call(
        functools.partial(feed_kernel, places, chunks),
        in_specs=[vmem, hbm, hbm, hbm, hbm],
        out_specs=[vmem, hbm, hbm, hbm, hbm],
        out_shape=[jax.ShapeDtypeStruct((quarter, width), F32), jax.ShapeDtypeStruct((count, quarter, width), BF),
                   jax.ShapeDtypeStruct((units, width), BF), jax.ShapeDtypeStruct((units, width), BF),
                   jax.ShapeDtypeStruct((units, width), BF)],
        scratch_shapes=[blocks(width), blocks(width), pltpu.VMEM((units, width), BF), pltpu.VMEM((units, width), BF),
                        pltpu.VMEM((units, width), BF), blocks(units), blocks(units), blocks(units), blocks(width),
                        line(places), line(places + 1), pltpu.VMEM((2, 2, quarter, width), BF), pltpu.VMEM((units, width), BF),
                        pltpu.VMEM((units, width), BF), pltpu.VMEM((units, width), BF), pltpu.SemaphoreType.DMA((4,)),
                        pltpu.SemaphoreType.DMA((5,)), pltpu.SemaphoreType.DMA, pltpu.SemaphoreType.DMA((3, count, chunks)),
                        pltpu.SemaphoreType.DMA((count, chunks))] + [sems] * 6,
        compiler_params=pltpu.CompilerParams(collective_id=call_id, has_side_effects=True, vmem_limit_bytes=60 * 2**20),
    )(own, cot.reshape(count, quarter, width), w_gate, w_up, w_down)


CONV = 4


def rms_norm(value, gain):
    return value * lax.rsqrt(jnp.mean(value * value, axis=-1, keepdims=True) + EPS) * gain


def after(value, *others):
    return lax.optimization_barrier((value,) + others)[0]


def part(value, axis, index, count=2):
    size = value.shape[axis] // count
    return lax.dynamic_slice_in_dim(value, index * size, size, axis)


def ordered(mine, theirs, side, axis):
    return jnp.concatenate([jnp.where(side == 0, mine, theirs), jnp.where(side == 0, theirs, mine)], axis=axis)


def sequence_tables(doc_lengths, first_row, row_count, block_size):
    padded = (doc_lengths + block_size - 1) // block_size * block_size
    seq_ends = jnp.cumsum(padded)
    seq_starts = seq_ends - padded
    row_places = first_row + jnp.arange(row_count, dtype=jnp.int32)
    inside_mask = (row_places[:, None] >= seq_starts[None, :]) & (row_places[:, None] < seq_ends[None, :])
    live_mask = jnp.any(inside_mask & (row_places[:, None] < (seq_starts + doc_lengths)[None, :]), axis=1, keepdims=True)
    fresh_block = jnp.any(row_places[::block_size][:, None] == seq_starts[None, :], axis=1)
    return live_mask.astype(F32), jnp.where(fresh_block, 0.0, 1.0).astype(F32)


def contract_rows(left, right):
    return lax.dot_general(left, right, (((0,), (0,)), ((), ())), preferred_element_type=F32)


def contract_cols(left, right):
    return lax.dot_general(left, right, (((1,), (1,)), ((), ())), preferred_element_type=F32)


def feed_apart(own, cot, w_gate, w_up, w_down):
    quarter = own.shape[0]
    blocks = lambda a: a.astype(BF).reshape(-1, quarter, a.shape[1])
    gathered_rows = line_gather([own], 3)[0]
    gate_pre = contract_cols(gathered_rows, w_gate)
    up_pre = contract_cols(gathered_rows, w_up)
    gate_sig = jax.nn.sigmoid(gate_pre)
    gate_act = gate_pre * gate_sig
    hidden_low = (gate_act * up_pre).astype(BF)
    grad_hidden = contract_cols(cot, w_down)
    grad_gate_low = (grad_hidden * up_pre * gate_sig * (1.0 + gate_pre * (1.0 - gate_sig))).astype(BF)
    grad_up_low = (grad_hidden * gate_act).astype(BF)
    grad_rows = (jnp.dot(grad_gate_low, w_gate, preferred_element_type=F32)
                 + jnp.dot(grad_up_low, w_up, preferred_element_type=F32))
    grad_sum = line_scatter([], [blocks(grad_rows)], [], [], 4)[1][0]
    down_rows = blocks(jnp.dot(hidden_low, w_down, preferred_element_type=F32))
    grad_w_down = contract_rows(hidden_low, cot).astype(BF)
    grad_w_gate = contract_rows(grad_gate_low, gathered_rows).astype(BF)
    grad_w_up = contract_rows(grad_up_low, gathered_rows).astype(BF)
    return grad_sum, down_rows, grad_w_down, grad_w_gate, grad_w_up


def shards(block_input, gain_attn, w_query, w_key, w_value, w_gate_out, w_decay, w_beta, conv_query, conv_key,
           conv_value, a_log, dt_bias, out_gain, w_out, gain_mlp, w_gate, w_up, w_down, doc_lengths, cotangent):
    d_model = block_input.shape[1]
    row_count = 2 * block_input.shape[0]
    quarter = cotangent.shape[0]
    depth = w_query.shape[0]
    heads = a_log.shape[0] // 2
    narrow = lax.axis_size("narrow")
    wide = lax.axis_size("wide")
    wide_index = lax.axis_index("wide")
    place, side = wide_index // 2, wide_index % 2
    live, flags = sequence_tables(doc_lengths, place * row_count, row_count, BLOCK)
    gain_row, a_row, dt_row = out_gain[None, :], part(a_log, 0, side)[None, :], part(dt_bias, 0, side)[None, :]
    key_width, value_width = heads * DK, heads * DV
    columns = 2 * key_width + value_width
    row_blocks = lambda a: a.astype(BF).reshape(-1, quarter, a.shape[1])
    halves = lambda *arrays: tuple(
        jnp.concatenate([part(a, 1, s) for a in arrays], axis=1) for s in (side, 1 - side))
    padded = lambda a: jnp.pad(a, ((0, 16 - 4 * heads), (0, 0)))

    first, small_weight, their_input, rim_input = line_gather(
        [halves(w_query, w_key, w_value), padded(jnp.concatenate([w_decay.T, w_beta.T], axis=0))], 1, rows=block_input)
    rim_input = jnp.where(place > 0, rim_input, jnp.zeros_like(rim_input))
    small_weight = small_weight.reshape(wide, 16, depth).transpose(1, 0, 2).reshape(16, d_model)
    small_weight = jnp.concatenate([part(small_weight[:2 * heads], 0, side), part(small_weight[2 * heads:4 * heads], 0, side)],
                                   axis=0)
    taps = jnp.concatenate([part(conv_query, 1, side), part(conv_key, 1, side), part(conv_value, 1, side)], axis=1)
    side_word = side.astype(jnp.int32)[None]
    padded_small = jnp.pad(small_weight, ((0, 16 - 2 * heads), (0, 0)))
    normed_low, mixed, small = project(side_word, block_input, their_input, rim_input, gain_attn[None, :], first, padded_small)
    small = small[:, :2 * heads]

    (local_out, reach, inverses, states, end, entry), (gate_weight, gathered_cot, out_weight) = forward_gather(
        flags, mixed, taps, small, live, a_row, dt_row, heads, [halves(w_gate_out), cotangent, halves(w_out)], 7)
    gate_rows, mixer_low, head_part = mix(normed_low, gate_weight, out_weight, local_out, reach, entry, live,
                                          gain_row, heads)
    own_rows = cube_scatter(row_blocks(head_part), 9) + part(
        block_input, 0, lax.axis_index("narrow"), narrow).astype(F32)
    mlp_normed, mlp_norm_back = jax.vjp(rms_norm, own_rows, gain_mlp)
    feed_forward = feed_apart if wide > 8 else functools.partial(feed, call_id=3)
    grad_mlp_normed, down_rows, grad_w_down, grad_w_gate, grad_w_up = feed_forward(
        mlp_normed.astype(BF), gathered_cot, w_gate.T, w_up.T, w_down)
    grad_own_norm, grad_gain_mlp = mlp_norm_back(grad_mlp_normed)
    grad_own = cotangent.astype(F32) + grad_own_norm
    grad_attn = cube_gather(grad_own.astype(BF), 10)

    grad_mixer = jnp.dot(grad_attn, out_weight, preferred_element_type=F32)
    grad_outputs, grad_gate_rows, grad_out_gain, direct = unfinish(local_out, reach, entry, gate_rows, live, gain_row,
                                                                   grad_mixer, heads)
    grad_w_out = contract_rows(grad_attn, mixer_low).astype(BF)
    grad_w_gate_out = contract_rows(normed_low[:row_count], grad_gate_rows).astype(BF)
    (grad_mixed, grad_small, grad_taps, grad_scalars), (sum_w_out, sum_w_gate_out), (sum_down,), shares = backward_scatter(
        flags, mixed, taps, small, live, a_row, dt_row, inverses, states, grad_outputs, entry, direct, end, heads,
        [grad_w_out, grad_w_gate_out], [down_rows], [grad_w_gate, grad_w_up, grad_w_down], 8)
    output = (own_rows + sum_down).astype(BF)
    grad_small = grad_small.astype(BF)
    grad_first = contract_rows(normed_low, grad_mixed).astype(BF)
    grad_small_weight = contract_rows(grad_small, normed_low[:row_count]).astype(BF)
    both_sides = lambda a: ordered(a, jnp.zeros_like(a), side, 0)
    grad_small_weight = padded(jnp.concatenate([both_sides(grad_small_weight[:heads]), both_sides(grad_small_weight[heads:])],
                                               axis=0))
    small_blocks = grad_small_weight.reshape(16, wide, depth).transpose(1, 0, 2)
    grad_input_part, grad_rim, grad_gain_attn = unproject(
        side_word, block_input, their_input, rim_input, gain_attn[None, :], grad_mixed, grad_gate_rows, grad_small.astype(F32),
        first, gate_weight, small_weight.astype(F32))
    grad_rim = jnp.pad(grad_rim[None], ((7, 0), (0, 0), (0, 0)))

    lanes = lambda a: jnp.pad(a, (0, -a.shape[0] % 1024)).reshape(-1, 128)
    head_sums = lanes(jnp.concatenate([grad_taps.reshape(-1), grad_scalars[0], grad_scalars[1]]))
    whole_sums = lanes(jnp.concatenate([grad_gain_attn[0], grad_gain_mlp, grad_out_gain[0]]))
    (sum_first,), (sum_small,), (input_sum, _), (every,) = line_scatter(
        [grad_first], [small_blocks], [row_blocks(grad_input_part), grad_rim],
        [jnp.concatenate([head_sums, whole_sums], axis=0)], 6)
    grad_input = input_sum + grad_own
    whole_sums = jnp.sum(every[:, head_sums.shape[0]:], axis=0).reshape(-1)
    every = every[:, :head_sums.shape[0]].reshape(2, narrow, -1)
    conv_all = every[:, :, :4 * columns].reshape(2, narrow, 4, columns)
    conv_parts = [conv_all[:, :, :, lo:hi].transpose(2, 1, 0, 3).reshape(4, -1) for lo, hi in
                  ((0, key_width), (key_width, 2 * key_width), (2 * key_width, columns))]
    scalars = [every[:, :, lo:lo + heads].transpose(1, 0, 2).reshape(-1) for lo in (4 * columns, 4 * columns + heads)]
    joined = lambda found, lo, hi: ordered(found[0][:, lo:hi], found[1][:, lo:hi], side, 1)
    return (
        output, grad_input, whole_sums[:d_model],
        joined(sum_first, 0, key_width), joined(sum_first, key_width, 2 * key_width), joined(sum_first, 2 * key_width, columns),
        joined(sum_w_gate_out, 0, value_width),
        sum_small[:2 * heads].T, sum_small[2 * heads:4 * heads].T, conv_parts[0], conv_parts[1], conv_parts[2],
        scalars[0], scalars[1], whole_sums[2 * d_model:2 * d_model + DV], joined(sum_w_out, 0, value_width),
        whole_sums[d_model:2 * d_model], shares[0].T, shares[1].T, shares[2],
    )


def solution(mesh):
    both = P("wide", "narrow")
    rows = P(("wide", "narrow"), None)
    return jax.shard_map(
        shards,
        mesh=mesh,
        in_specs=(P("wide", None), P(), both, both, both, both, both, both, P(None, "narrow"), P(None, "narrow"),
                  P(None, "narrow"), P("narrow"), P("narrow"), P(), both, P(), P(None, "wide"), P(None, "wide"),
                  P("wide", None), P(), rows),
        out_specs=(rows, rows, P(), both, both, both, both, both, both, P(), P(), P(), P(), P(), P(), both, P(),
                   P("narrow", "wide"), P("narrow", "wide"), both),
        check_vma=False,
    )
```

time: 906 us -> 761 us (0.84)
  matrix products: 101 us -> 23.6 us
  waiting for transfers between devices: 59 us -> 0 us
  Pallas kernels: 628 us -> 675 us
  starting transfers between devices: 20.3 us -> 0 us
  other arithmetic: 37.2 us -> 19.9 us
  between operations: 15.6 us -> 1.9 us
    dot_general x13 -> x0, matrix products: 69.5 us -> none  [the longest x7 34.1 us: contract_cols(): lax.dot_general(left, right, (((1,), (1,)), ((), ())), preferred_element_...]
    ppermute x28 -> x0, waiting for transfers between devices: 59 us -> none  [the longest x26 59 us: across(): lax.ppermute(value, axis, [(i, i ^ bit) for i in range(lax.axis_size(axis...]
    pallas_call x8 -> x9, Pallas kernels: 531 us -> 561 us  [the longest x1 153 us: backward_scatter(): pl.pallas_call(functools.partial(backward_scatter_kernel, heads, nb, plac...]
    ppermute x28 -> x0, starting transfers between devices: 20.3 us -> none  [the longest x26 15 us: across(): lax.ppermute(value, axis, [(i, i ^ bit) for i in range(lax.axis_size(axis...]
    pallas_call x1, Pallas kernels: 92.1 us -> 108 us  [forward_gather(): pl.pallas_call(functools.partial(forward_gather_kernel, heads, nb, count...]
    add x10 -> x1, other arithmetic: 11.2 us -> 1.62 us  [shards(): grad_input = input_sum + grad_own]
    dot_general x7 -> x4, matrix products: 28.2 us -> 19.9 us  [contract_rows(): lax.dot_general(left, right, (((0,), (0,)), ((), ())), preferred_element_...]
    unnamed x182 -> x139, local copies, waits for them, and re-layouts: 13.5 us -> 19.2 us
  transfers between devices with their start and end apart: 29 -> 0, of which waited for: 8 -> 0; matrix products, arithmetic and copies ran while one was open for 10% -> 0% of each run, Pallas kernels for 34% -> 0%
where the time goes in v3:
time: 761 us; the launch traced here: 753 us
  Pallas kernels  675 us (89%)
  local copies, waits for them, and re-layouts  33.5 us (4%)
  matrix products  23.6 us (3%)
  other arithmetic  19.9 us (3%)
    pallas_call x1, Pallas kernels, backward_scatter(): pl.pallas_call(functools.partial(backward_scatter_kernel, heads, nb, plac...  153 us
    pallas_call x1, Pallas kernels, feed(): pl.pallas_call(functools.partial(feed_kernel, places, chunks), in_specs=[...  148 us
    pallas_call x1, Pallas kernels, forward_gather(): pl.pallas_call(functools.partial(forward_gather_kernel, heads, nb, count...  108 us
    pallas_call x1, Pallas kernels, line_scatter(): pl.pallas_call(functools.partial(scatter_kernel, places, half_cuts, pair_...  95.2 us
    pallas_call x1, Pallas kernels, line_gather(): pl.pallas_call(functools.partial(gather_kernel, count // 2, cuts, halved,...  77.7 us
    pallas_call x1, Pallas kernels, cube_scatter(): pl.pallas_call(cube_scatter_kernel, out_shape=jax.ShapeDtypeStruct(value....  22.9 us
    pallas_call x1, Pallas kernels, cube_gather(): pl.pallas_call(cube_gather_kernel, out_shape=jax.ShapeDtypeStruct((8,) +...  22.9 us
    dot_general x4, matrix products, contract_rows(): lax.dot_general(left, right, (((0,), (0,)), ((), ())), preferred_element_...  19.9 us

profile of v3, /device:TPU:10, one launch (start us, length us, event | category | flops | bytes accessed | tf_op | source)
XLA Modules:
  0.0 753.5 jit_solution(2379384361180862605)
XLA Ops:
  0.7 1.1 constant_dynamic-slice_fusion.9
  3.8 1.1 pad_maximum_fusion.3
  5.6 77.7 %shard_map.356 = (bf16[8,256,1024]{2,1,0:T(8,128)(2,1)}, bf16[8,16,256]{2,1,0:T(8,128)(2,1)}, bf16[4,128,2048]{2,1,0:T(8,128)(2,1)}, bf16[16,2048]{1,0:T(8,128)(2,1)}) custom-call(bf16[256,1024]{1,0:T(8,128)(2,1)} %get-tuple-element.166.refs_0_, bf16[16,256]{1,0:T(8,128)(2,1)} %fusion.22.refs_1_, bf16[256,1024]{1,0:T(8,128)(2,1)} %get-tuple-element.167.refs_2_, ...), custom_call_target="tpu_custom_call" | custom-call | tf_op jit(solution)/shard_map/pallas_call | solution.py:582
  85.7 1.6 copy-done.4
  87.4 11.3 %shard_map.357 = (bf16[1040,2048]{1,0:T(8,128)(2,1)}, bf16[1040,1024]{1,0:T(8,128)(2,1)}, f32[1024,16]{1,0:T(8,128)S(1)}) custom-call(s32[1]{0:T(128)} %bitcast.side_ref, bf16[512,2048]{1,0:T(8,128)(2,1)S(1)} %copy-done.2, bf16[512,2048]{1,0:T(8,128)(2,1)S(1)} %bitcast.88, bf16[16,2048]{1,0:T(8,128)(2,1)S(1)} %broadcast_select_fusion.4.rim_ref, ...), custom_call_target="tpu_custom_call" | custom-call | tf_op jit(solution)/shard_map/pallas_call | solution.py:1375
  107.1 108.5 %shard_map.358 = (f32[1024,512]{1,0:T(8,128)}, bf16[1024,256]{1,0:T(8,128)(2,1)S(1)}, bf16[16,2,64,64]{3,2,1,0:T(8,128)(2,1)S(1)}, bf16[16,2,128,384]{3,2,1,0:T(...) custom-call(f32[16]{0:T(128)S(1)} %broadcast_select_fusion.9.refs_0_, ...), custom_call_target="tpu_custom_call" | custom-call | tf_op jit(solution)/shard_map/pallas_call | solution.py:1224
  217.2 10.6 %shard_map.359 = (f32[1024,512]{1,0:T(8,128)S(1)}, bf16[1024,512]{1,0:T(8,128)(2,1)S(1)}, bf16[1024,2048]{1,0:T(8,128)(2,1)}) custom-call(bf16[1040,2048]{1,0:T(8,128)(2,1)} %get-tuple-element.72.x_ref, bf16[2048,512]{1,0:T(8,128)(2,1)} %bitcast.103, bf16[2048,512]{1,0:T(8,128)(2,1)} %bitcast.111, f32[1024,512]{1,0:T(8,128)} %get-tuple-element.77.o_ref, ...), custom_call_target="tpu_custom_call" | custom-call | tf_op jit(solution)/shard_map/pallas_call | solution.py:1448
  227.8 1.4 copy-done.11
  230.1 2.2 copy-done.8
  232.3 22.9 %shard_map.360 = f32[128,2048]{1,0:T(8,128)S(1)} custom-call(bf16[8,128,2048]{2,1,0:T(8,128)(2,1)S(1)} %bitcast.89), custom_call_target="tpu_custom_call" | custom-call | tf_op jit(solution)/shard_map/pallas_call | solution.py:895
  256.2 1.4 multiply_reduce_fusion.2
  259.6 148.0 %shard_map.361 = (f32[128,2048]{1,0:T(8,128)}, bf16[8,128,2048]{2,1,0:T(8,128)(2,1)}, bf16[688,2048]{1,0:T(8,128)(2,1)}, bf16[688,2048]{1,0:T(8,128)(2,1)}, bf16[688,2048]{1,0:T(8,128)(2,1)}) custom-call(bf16[128,2048]{1,0:T(8,128)(2,1)} %multiply_convert_fusion.own_ref, bf16[8,128,2048]{2,1,0:T(8,128)(2,1)} %get-tuple-element.84.cot_hbm, ...), custom_call_target="tpu_custom_call" | custom-call | tf_op jit(solution)/shard_map/pallas_call | solution.py:1680
  407.6 1.6 multiply_reduce_fusion
  409.5 22.9 %shard_map.362 = bf16[8,128,2048]{2,1,0:T(8,128)(2,1)S(1)} custom-call(bf16[128,2048]{1,0:T(8,128)(2,1)S(1)} %fusion.27.x_ref), custom_call_target="tpu_custom_call" | custom-call | tf_op jit(solution)/shard_map/pallas_call | solution.py:955
  432.5 3.7 fusion.33.gm_ref
  436.2 5.6 shard_map.363
  441.9 3.7 fusion.4
  445.6 3.8 convolution_convert_fusion.1
  449.4 153.3 %shard_map.364 = (bf16[1040,1024]{1,0:T(8,128)(2,1)}, f32[1024,4]{1,0:T(8,128)}, f32[4,1024]{1,0:T(4,128)}, f32[8,2]{1,0:T(8,128)}, f32[256,512]{1,0:T(8,128)}, ...) custom-call(f32[16]{0:T(128)} %copy-done.30, ...), custom_call_target="tpu_custom_call" | custom-call | tf_op jit(solution)/shard_map/pallas_call | solution.py:1308
  602.7 1.4 broadcast_select_fusion.1
  604.1 1.1 pad_maximum_fusion.2
  605.3 1.1 pad_maximum_fusion.1
  608.1 18.6 %shard_map.365 = (bf16[1024,2048]{1,0:T(8,128)(2,1)}, bf16[16,2048]{1,0:T(8,128)(2,1)}, f32[1,2048]{1,0:T(1,128)}) custom-call(s32[1]{0:T(128)} %bitcast.side_ref, bf16[512,2048]{1,0:T(8,128)(2,1)} %own_ref.3, bf16[512,2048]{1,0:T(8,128)(2,1)} %bitcast.87, bf16[16,2048]{1,0:T(8,128)(2,1)} %copy-done.20, f32[1,2048]{1,0:T(1,128)} %bitcast.94, ...), custom_call_target="tpu_custom_call" | custom-call | tf_op jit(solution)/shard_map/pallas_call | solution.py:1417
  628.0 1.8 pad.27.refs_3_
  629.9 2.9 fusion.7
  633.5 9.6 %convolution_convert_fusion = bf16[2048,1024]{1,0:T(8,128)(2,1)} fusion(bf16[1040,2048]{1,0:T(8,128)(2,1)} %get-tuple-element.72.x_ref, bf16[1040,1024]{1,0:T(8,128)(2,1)S(1)} %copy-done.38), kind=kOutput, calls=%fused_computation | convolution fusion | flops 4364173312 | bytes 10584064 | tf_op jit(solution)/shard_map/dot_general | solution.py:1729
  643.0 95.2 %shard_map.366 = (f32[256,1024]{1,0:T(8,128)}, f32[256,1024]{1,0:T(8,128)}, f32[16,256]{1,0:T(8,128)}, f32[128,2048]{1,0:T(8,128)}, f32[16,2048]{1,0:T(8,128)}, /*index=5*/f32[8,80,128]{2,1,0:T(8,128)}) custom-call(bf16[4,2,256,1024]{3,2,1,0:T(8,128)(2,1)} %bitcast.106, bf16[8,16,256]{2,1,0:T(8,128)(2,1)} %bitcast.115, bf16[8,128,2048]{2,1,0:T(8,128)(2,1)} %bitcast.105, ...), custom_call_target="tpu_custom_call" | custom-call | tf_op jit(solution)/shard_map/pallas_call | solution.py:1120
  738.3 1.4 slice_select_fusion.1
  742.7 1.6 fusion.26
  749.8 1.1 copy.90
  750.9 1.1 copy.91
  752.0 1.1 copy.92
  (191 shorter events, 31.4 us)
Async XLA Ops:
  0.7 99.7 %copy-start = (f32[4,1024]{1,0:T(4,128)S(1)}, f32[4,1024]{1,0:T(4,128)}, u32[]{:S(2)}) copy-start(f32[4,1024]{1,0:T(4,128)} %param.31) | copy-start | bytes 49156
  0.7 4.3 copy-start.59
  0.7 4.3 copy-start.58
  3.8 81.9 %copy-start.2 = (bf16[512,2048]{1,0:T(8,128)(2,1)S(1)}, bf16[512,2048]{1,0:T(8,128)(2,1)}, u32[]{:S(2)}) copy-start(bf16[512,2048]{1,0:T(8,128)(2,1)} %own_ref.3) | copy-start | bytes 6291460
  3.8 81.9 %copy-start.25 = (f32[2048]{0:T(1024)S(1)}, f32[2048]{0:T(1024)}, u32[]{:S(2)}) copy-start(f32[2048]{0:T(1024)} %param.22) | copy-start | bytes 24580
  85.7 13.0 %copy-start.20 = (bf16[16,2048]{1,0:T(8,128)(2,1)}, bf16[16,2048]{1,0:T(8,128)(2,1)S(1)}, u32[]{:S(2)}) copy-start(bf16[16,2048]{1,0:T(8,128)(2,1)S(1)} %broadcast_select_fusion.4.rim_ref) | copy-start | bytes 196612
  87.3 12.1 %copy-start.50 = (bf16[256,1024]{1,0:T(8,128)(2,1)S(1)}, bf16[256,1024]{1,0:T(8,128)(2,1)}, u32[]{:S(2)}) copy-start(bf16[256,1024]{1,0:T(8,128)(2,1)} %param.35) | copy-start | bytes 1572868
  87.3 12.1 %copy-start.51 = (bf16[256,1024]{1,0:T(8,128)(2,1)S(1)}, bf16[256,1024]{1,0:T(8,128)(2,1)}, u32[]{:S(2)}) copy-start(bf16[256,1024]{1,0:T(8,128)(2,1)} %param.26) | copy-start | bytes 1572868
  87.3 13.0 %copy-start.56 = (f32[4,512]{1,0:T(4,128)S(1)}, f32[4,512]{1,0:T(4,128)}, u32[]{:S(2)}) copy-start(f32[4,512]{1,0:T(4,128)} %param.30) | copy-start | bytes 24580
  87.3 13.0 %copy-start.57 = (f32[4,512]{1,0:T(4,128)S(1)}, f32[4,512]{1,0:T(4,128)}, u32[]{:S(2)}) copy-start(f32[4,512]{1,0:T(4,128)} %param.29) | copy-start | bytes 24580
  87.3 13.1 %copy-start.60 = (f32[4]{0:T(128)S(1)}, f32[4]{0:T(128)}, u32[]{:S(2)}) copy-start(f32[4]{0:T(128)} %param.33) | copy-start | bytes 52
  87.3 13.1 %copy-start.61 = (f32[4]{0:T(128)S(1)}, f32[4]{0:T(128)}, u32[]{:S(2)}) copy-start(f32[4]{0:T(128)} %param.32) | copy-start | bytes 52
  87.3 13.7 %copy-start.62 = (s32[9]{0:T(128)S(1)}, s32[9]{0:T(128)}, u32[]{:S(2)}) copy-start(s32[9]{0:T(128)} %param.40) | copy-start | bytes 112
  100.4 115.2 %copy-start.24 = (f32[4,1024]{1,0:T(4,128)}, f32[4,1024]{1,0:T(4,128)S(1)}, u32[]{:S(2)}) copy-start(f32[4,1024]{1,0:T(4,128)S(1)} %pad_maximum_fusion.9.refs_3_.refs_4_) | copy-start | bytes 49156
  101.6 334.6 %copy-start.3 = (f32[1024,1]{1,0:T(8,128)}, f32[1024,1]{1,0:T(8,128)S(1)}, u32[]{:S(2)}) copy-start(f32[1024,1]{1,0:T(8,128)S(1)} %copy.56.refs_5_.live_ref.refs_6_) | copy-start | bytes 12292
  107.1 108.5 %copy-start.30 = (f32[16]{0:T(128)}, f32[16]{0:T(128)S(1)}, u32[]{:S(2)}) copy-start(f32[16]{0:T(128)S(1)} %broadcast_select_fusion.9.refs_0_) | copy-start | bytes 196
  107.1 110.1 %copy-start.28 = (f32[256]{0:T(256)S(1)}, f32[256]{0:T(256)}, u32[]{:S(2)}) copy-start(f32[256]{0:T(256)} %param.34) | copy-start | bytes 3076
  217.2 10.6 %copy-start.9 = (bf16[1024,256]{1,0:T(8,128)(2,1)}, bf16[1024,256]{1,0:T(8,128)(2,1)S(1)}, u32[]{:S(2)}) copy-start(bf16[1024,256]{1,0:T(8,128)(2,1)S(1)} %get-tuple-element.78.e_ref) | copy-start | bytes 1572868
  217.2 219.0 %copy-start.14 = (bf16[2,128,256]{2,1,0:T(8,128)(2,1)}, bf16[2,128,256]{2,1,0:T(8,128)(2,1)S(1)}, u32[]{:S(2)}) copy-start(bf16[2,128,256]{2,1,0:T(8,128)(2,1)S(1)} %get-tuple-element.79.s_ref.refs_12_) | copy-start | bytes 393220
  232.3 26.3 %copy-start.53 = (f32[2048]{0:T(1024)S(1)}, f32[2048]{0:T(1024)}, u32[]{:S(2)}) copy-start(f32[2048]{0:T(1024)} %param.36) | copy-start | bytes 24580
  259.6 148.0 %copy-start.34 = (f32[128,2048]{1,0:T(8,128)S(1)}, f32[128,2048]{1,0:T(8,128)}, u32[]{:S(2)}) copy-start(f32[128,2048]{1,0:T(8,128)} %copy-done.33) | copy-start | bytes 3145732
  409.2 23.3 %copy-start.40 = (bf16[8,256,512]{2,1,0:T(8,128)(2,1)S(1)}, bf16[8,256,512]{2,1,0:T(8,128)(2,1)}, u32[]{:S(2)}) copy-start(bf16[8,256,512]{2,1,0:T(8,128)(2,1)} %get-tuple-element.76) | copy-start | bytes 6291460
  409.5 32.3 %slice-start = ((s8[4259840]{0:T(1024)(128)(4,1)}), s8[4194304]{0:T(1024)(128)(4,1)S(1)}, s32[]{:S(2)}) async-start(s8[4259840]{0:T(1024)(128)(4,1)} %bitcast.99), calls=%async_computation | async-start | bytes 8388608
  432.5 9.4 %slice-start.1 = ((s8[4259840]{0:T(1024)(128)(4,1)}), s8[65536]{0:T(1024)(128)(4,1)S(1)}, s32[]{:S(2)}) async-start(s8[4259840]{0:T(1024)(128)(4,1)} %bitcast.99), calls=%async_computation.1 | async-start | bytes 131072
  441.8 3.8 copy-start.18
  441.8 3.8 copy-start.19
  441.8 3.8 copy-start.23
  441.8 3.8 copy-start.32
  628.0 5.4 copy-start.38
  742.7 6.5 copy-start.55
  742.7 7.1 copy-start.43
  744.4 6.5 copy-start.42
  (33 other events, 65.2 us)

commit v4 on v3

--- a/solution.py
+++ b/solution.py
@@ -599,6 +599,7 @@
         self.right_sems, self.left_sems = (right_send, right_recv), (left_send, left_recv)
         self.w, self.place, self.side, self.n = position()
         self.items = [(i,) + cut for i, found in enumerate(cuts) for cut in found]
+        self.fill = None
         self.order = [(t, item) for j in range(places // 2) for item in range(len(self.items)) for t in (places - 1 - j, j)]
 
     def remote(self, source, target, sems, t, item, device):
@@ -650,6 +651,8 @@
         def add(other):
             own[at] = (own[at].astype(F32) + other[at].astype(F32)).astype(own.dtype)
 
+        if self.fill is not None and item == 0:
+            self.fill(t)
         if self.sources is not None:
             self.load(t, item).wait()
         if self.paired:
@@ -1025,6 +1028,38 @@
                 pltpu.SemaphoreType.DMA((steps,)), pltpu.SemaphoreType.DMA((3, 8)), pltpu.SemaphoreType.DMA((8,))]
 
 
+class Products:
+    def __init__(self, scatter, operands, buffers, sems):
+        self.scatter, self.buffers = scatter, buffers
+        self.loads = [pltpu.make_async_copy(source, target, sems.at[i])
+                      for i, (source, target) in enumerate(zip(operands, buffers))]
+        scatter.fill = self.fill
+
+    def start(self):
+        for load in self.loads:
+            load.start()
+
+    def wait(self):
+        for load in self.loads:
+            load.wait()
+
+    def fill(self, t):
+        for i, own in enumerate(self.scatter.owns):
+            left, right = self.buffers[2 * i], self.buffers[2 * i + 1]
+            depth = 2 * own.shape[2]
+            term = mm_tn(left[:right.shape[0], t * depth:(t + 1) * depth], right[...]).astype(own.dtype)
+            own[t] = term.reshape(own.shape[1:])
+
+    @staticmethod
+    def scratch(operands):
+        return [pltpu.VMEM(a.shape, a.dtype) for a in operands] + [pltpu.SemaphoreType.DMA((len(operands),))]
+
+
+def product_terms(products, places):
+    terms = [jax.ShapeDtypeStruct((places, 2, left.shape[1] // (2 * places), right.shape[1]), BF) for left, right in products]
+    return terms, [a for product in products for a in product]
+
+
 def place_bits(places):
     return [2 << i for i in range(places.bit_length() - 1)]
 
@@ -1037,11 +1072,14 @@
         found, refs = refs[:count], refs[count:]
         return found
 
-    halves, pairs, cube_in, small_in = take(hm), take(pm), take(cubes), take(small)
+    operands, pairs, cube_in, small_in = take(2 * hm), take(pm), take(cubes), take(small)
     half_outs, half_theirs, pair_outs, cube_outs, small_outs = take(hm), take(hm), take(pm), take(cubes), take(small)
     groups, ends = [], []
     if hm:
-        half, refs = LineScatter.take(places, half_cuts, False, halves, refs)
+        buffers, product_sems = take(2 * hm), take(1)[0]
+        half, refs = LineScatter.take(places, half_cuts, False, None, refs)
+        products = Products(half, operands, buffers, product_sems)
+        products.start()
         groups.append(half)
         ends.append(lambda: half.finish(half_outs, half_theirs))
     if pm:
@@ -1059,6 +1097,8 @@
     greet(line=places, pair=True, cube=bool(cubes), bits=place_bits(places) if small else ())
     for group in groups[::-1]:
         group.start()
+    if hm:
+        products.wait()
     for group, event in merged(groups):
         group.run(event)
     for end in ends[:0:-1]:
@@ -1094,20 +1134,16 @@
     return [(group, event) for _, _, _, group, event in sorted(found, key=lambda e: e[:3])]
 
 
-def place_blocks(term, places):
-    return term.reshape(places, 2, term.shape[0] // (2 * places), term.shape[1])
-
-
 def line_scatter(halves, pairs, cubes, small, call_id, chunks=4):
     places = lax.axis_size("wide") // 2
-    halves = [place_blocks(term, places) for term in halves]
+    halves, operands = product_terms(halves, places)
     half_cuts = [row_cuts(term.shape[2], chunks) for term in halves]
     pair_cuts = [row_cuts(term.shape[1], chunks if term.shape[1] > 64 else 1) for term in pairs]
     shapes = [term.shape[2:] for term in halves] * 2 + [term.shape[1:] for term in list(pairs) + list(cubes)]
     shapes += [(8,) + term.shape for term in small]
     scratch = []
     if halves:
-        scratch += LineScatter.scratch(places, half_cuts, False, halves)
+        scratch += Products.scratch(operands) + LineScatter.scratch(places, half_cuts, False, halves)
     if pairs:
         scratch += LineScatter.scratch(places, pair_cuts, True, pairs)
     for term in cubes:
@@ -1120,11 +1156,11 @@
     found = pl.pallas_call(
         functools.partial(scatter_kernel, places, half_cuts, pair_cuts, len(cubes), len(small), lax.axis_size("narrow")),
         out_shape=[jax.ShapeDtypeStruct(shape, F32) for shape in shapes],
-        in_specs=[pl.BlockSpec(memory_space=pl.ANY)] * (len(halves) + len(pairs) + len(cubes)) + [vmem] * len(small),
+        in_specs=[pl.BlockSpec(memory_space=pl.ANY)] * (len(operands) + len(pairs) + len(cubes)) + [vmem] * len(small),
         out_specs=[vmem] * len(shapes),
         scratch_shapes=scratch,
-        compiler_params=pltpu.CompilerParams(collective_id=call_id, has_side_effects=True, vmem_limit_bytes=56 * 2**20),
-    )(*halves, *pairs, *cubes, *small)
+        compiler_params=pltpu.CompilerParams(collective_id=call_id, has_side_effects=True, vmem_limit_bytes=60 * 2**20),
+    )(*operands, *pairs, *cubes, *small)
     h, p, c = len(halves), len(pairs), len(cubes)
     return list(zip(found[:h], found[h:2 * h])), found[2 * h:2 * h + p], found[2 * h + p:2 * h + p + c], found[2 * h + p + c:]
 
@@ -1251,13 +1287,15 @@
         found, refs = refs[:count], refs[count:]
         return found
 
-    inputs, halves, pairs, share_in = tuple(take(15)), take(hm), take(pm), take(shares)
+    inputs, operands, pairs, share_in = tuple(take(15)), take(2 * hm), take(pm), take(shares)
     outs, half_outs, half_theirs, pair_outs, share_outs = take(4), take(hm), take(hm), take(pm), take(shares)
     scratch = take(2)
     states, exit_ref = PassStates(places, False, *take(5)), take(1)[0]
     direct_ref, end_ref = inputs[-2:]
     inputs = inputs[:-2] + (exit_ref,)
-    half, refs = LineScatter.take(places, half_cuts, False, halves, refs)
+    buffers, product_sems = take(2 * hm), take(1)[0]
+    half, refs = LineScatter.take(places, half_cuts, False, None, refs)
+    products = Products(half, operands, buffers, product_sems)
     groups = [half]
     if pm:
         pair, refs = LineScatter.take(places, pair_cuts, True, pairs, refs)
@@ -1268,11 +1306,13 @@
 
     @pl.when(step == 0)
     def _():
+        products.start()
         greet(line=places, pair=True, cube=True, places=places)
         states.start(direct_ref[...], end_ref[:, :, DV:])
         for group in groups:
             group.start()
         states.finish(exit_ref)
+        products.wait()
 
     backward_kernel(heads, *inputs, *outs, *scratch)
     events = merged(groups)
@@ -1295,7 +1335,7 @@
     rows, width = live.shape[0], mixed.shape[1]
     nb = rows // BLOCK
     places = lax.axis_size("wide") // 2
-    halves = [place_blocks(term, places) for term in halves]
+    halves, operands = product_terms(halves, places)
     half_cuts = [row_cuts(term.shape[2], chunks) for term in halves]
     pair_cuts = [row_cuts(term.shape[1], chunks) for term in pairs]
     h = len(halves)
@@ -1314,7 +1354,7 @@
                   pl.BlockSpec((1, heads, BLOCK, BLOCK), lambda i: (nb - 1 - i, 0, 0, 0)),
                   pl.BlockSpec((1, heads, DK, DV + DK), lambda i: (nb - 1 - i, 0, 0, 0)),
                   row(heads * DV), same(heads, DK, DV), same(heads, DK, DV), same(heads, DK, DV + DK)]
-                 + [pl.BlockSpec(memory_space=pl.ANY)] * (len(halves) + len(pairs) + len(shares)),
+                 + [pl.BlockSpec(memory_space=pl.ANY)] * (len(operands) + len(pairs) + len(shares)),
         out_specs=[same(rows + 16, width), row(2 * heads), same(*taps.shape), same(8, heads)]
                   + [pl.BlockSpec(shape, lambda i: (0, 0), pipeline_mode=pl.Buffered(1)) for shape in sums],
         out_shape=[jax.ShapeDtypeStruct((rows + 16, width), BF), jax.ShapeDtypeStruct((rows, 2 * heads), F32),
@@ -1322,11 +1362,11 @@
                   + [jax.ShapeDtypeStruct(shape, F32) for shape in sums],
         scratch_shapes=[pltpu.VMEM((heads, DK, DV), F32), pltpu.VMEM((8, width), F32)]
                        + PassStates.scratch(places, heads) + [pltpu.VMEM((heads, DK, DV), F32)]
-                       + LineScatter.scratch(places, half_cuts, False, halves)
+                       + Products.scratch(operands) + LineScatter.scratch(places, half_cuts, False, halves)
                        + (LineScatter.scratch(places, pair_cuts, True, pairs) if pairs else [])
                        + NarrowScatter.scratch(shares, narrow),
-        compiler_params=pltpu.CompilerParams(collective_id=call_id, has_side_effects=True, vmem_limit_bytes=58 * 2**20),
-    )(flags, mixed, mixed, mixed, taps, small, live, a_log, dt_bias, t, z, go, entry, direct, end, *halves, *pairs, *shares)
+        compiler_params=pltpu.CompilerParams(collective_id=call_id, has_side_effects=True, vmem_limit_bytes=60 * 2**20),
+    )(flags, mixed, mixed, mixed, taps, small, live, a_log, dt_bias, t, z, go, entry, direct, end, *operands, *pairs, *shares)
     p = len(pairs)
     return (found[:4], list(zip(found[4:4 + h], found[4 + h:4 + 2 * h])), found[4 + 2 * h:4 + 2 * h + p],
             found[4 + 2 * h + p:])
@@ -1668,7 +1708,7 @@
     lax.fori_loop(0, places, settle, 0)
 
 
-def feed(own, cot, w_gate, w_up, w_down, call_id, chunks=2):
+def feed(own, cot, w_gate, w_up, w_down, call_id, chunks=4):
     count = lax.axis_size("wide")
     places = count // 2
     quarter, width = own.shape
@@ -1804,14 +1844,11 @@
     grad_mixer = jnp.dot(grad_attn, out_weight, preferred_element_type=F32)
     grad_outputs, grad_gate_rows, grad_out_gain, direct = unfinish(local_out, reach, entry, gate_rows, live, gain_row,
                                                                    grad_mixer, heads)
-    grad_w_out = contract_rows(grad_attn, mixer_low).astype(BF)
-    grad_w_gate_out = contract_rows(normed_low[:row_count], grad_gate_rows).astype(BF)
     (grad_mixed, grad_small, grad_taps, grad_scalars), (sum_w_out, sum_w_gate_out), (sum_down,), shares = backward_scatter(
         flags, mixed, taps, small, live, a_row, dt_row, inverses, states, grad_outputs, entry, direct, end, heads,
-        [grad_w_out, grad_w_gate_out], [down_rows], [grad_w_gate, grad_w_up, grad_w_down], 8)
+        [(grad_attn, mixer_low), (normed_low, grad_gate_rows)], [down_rows], [grad_w_gate, grad_w_up, grad_w_down], 8)
     output = (own_rows + sum_down).astype(BF)
     grad_small = grad_small.astype(BF)
-    grad_first = contract_rows(normed_low, grad_mixed).astype(BF)
     grad_small_weight = contract_rows(grad_small, normed_low[:row_count]).astype(BF)
     both_sides = lambda a: ordered(a, jnp.zeros_like(a), side, 0)
     grad_small_weight = padded(jnp.concatenate([both_sides(grad_small_weight[:heads]), both_sides(grad_small_weight[heads:])],
@@ -1826,7 +1863,7 @@
     head_sums = lanes(jnp.concatenate([grad_taps.reshape(-1), grad_scalars[0], grad_scalars[1]]))
     whole_sums = lanes(jnp.concatenate([grad_gain_attn[0], grad_gain_mlp, grad_out_gain[0]]))
     (sum_first,), (sum_small,), (input_sum, _), (every,) = line_scatter(
-        [grad_first], [small_blocks], [row_blocks(grad_input_part), grad_rim],
+        [(normed_low, grad_mixed)], [small_blocks], [row_blocks(grad_input_part), grad_rim],
         [jnp.concatenate([head_sums, whole_sums], axis=0)], 6)
     grad_input = input_sum + grad_own
     whole_sums = jnp.sum(every[:, head_sums.shape[0]:], axis=0).reshape(-1)

time: 761 us -> 746 us (0.980)
  matrix products: 23.6 us -> 6.53 us
    dot_general x4 -> x1, matrix products: 19.9 us -> 2.87 us  [contract_rows(): lax.dot_general(left, right, (((0,), (0,)), ((), ())), preferred_element_...]
    pallas_call x1, Pallas kernels: 148 us -> 138 us  [feed(): pl.pallas_call(functools.partial(feed_kernel, places, chunks), in_specs=[...]
    unnamed x139 -> x133, local copies, waits for them, and re-layouts: 19.2 us -> 21 us
where the time goes in v4:
time: 746 us; the launch traced here: 738 us
  Pallas kernels  675 us (90%)
  local copies, waits for them, and re-layouts  35.1 us (5%)
  other arithmetic  19.9 us (3%)
    pallas_call x1, Pallas kernels, backward_scatter(): pl.pallas_call(functools.partial(backward_scatter_kernel, heads, nb, plac...  157 us
    pallas_call x1, Pallas kernels, feed(): pl.pallas_call(functools.partial(feed_kernel, places, chunks), in_specs=[...  138 us
    pallas_call x1, Pallas kernels, forward_gather(): pl.pallas_call(functools.partial(forward_gather_kernel, heads, nb, count...  108 us
    pallas_call x1, Pallas kernels, line_scatter(): pl.pallas_call(functools.partial(scatter_kernel, places, half_cuts, pair_...  102 us
    pallas_call x1, Pallas kernels, line_gather(): pl.pallas_call(functools.partial(gather_kernel, count // 2, cuts, halved,...  77.7 us
    pallas_call x1, Pallas kernels, cube_scatter(): pl.pallas_call(cube_scatter_kernel, out_shape=jax.ShapeDtypeStruct(value....  22.9 us
    pallas_call x1, Pallas kernels, cube_gather(): pl.pallas_call(cube_gather_kernel, out_shape=jax.ShapeDtypeStruct((8,) +...  22.2 us
    unnamed x133, local copies, waits for them, and re-layouts  21 us

profile of v4, /device:TPU:10, one launch (start us, length us, event | category | flops | bytes accessed | tf_op | source)
XLA Modules:
  0.0 738.0 jit_solution(13511349927096783399)
XLA Ops:
  0.7 1.1 constant_dynamic-slice_fusion.9
  2.8 1.0 constant_dynamic-slice_fusion.10
  3.8 1.1 pad_maximum_fusion.3
  5.6 77.7 %shard_map.356 = (bf16[8,256,1024]{2,1,0:T(8,128)(2,1)}, bf16[8,16,256]{2,1,0:T(8,128)(2,1)}, bf16[4,128,2048]{2,1,0:T(8,128)(2,1)}, bf16[16,2048]{1,0:T(8,128)(2,1)}) custom-call(bf16[256,1024]{1,0:T(8,128)(2,1)} %get-tuple-element.166.refs_0_, bf16[16,256]{1,0:T(8,128)(2,1)} %fusion.17.refs_1_, bf16[256,1024]{1,0:T(8,128)(2,1)} %get-tuple-element.167.refs_2_, ...), custom_call_target="tpu_custom_call" | custom-call | tf_op jit(solution)/shard_map/pallas_call | solution.py:582
  85.7 1.6 copy-done.5
  87.4 11.3 %shard_map.357 = (bf16[1040,2048]{1,0:T(8,128)(2,1)}, bf16[1040,1024]{1,0:T(8,128)(2,1)}, f32[1024,16]{1,0:T(8,128)S(1)}) custom-call(s32[1]{0:T(128)} %bitcast.side_ref, bf16[512,2048]{1,0:T(8,128)(2,1)S(1)} %copy-done.2, bf16[512,2048]{1,0:T(8,128)(2,1)S(1)} %bitcast.82, bf16[16,2048]{1,0:T(8,128)(2,1)S(1)} %broadcast_select_fusion.4.rim_ref, ...), custom_call_target="tpu_custom_call" | custom-call | tf_op jit(solution)/shard_map/pallas_call | solution.py:1415
  101.9 1.0 copy-done.12
  107.1 108.5 %shard_map.358 = (f32[1024,512]{1,0:T(8,128)}, bf16[1024,256]{1,0:T(8,128)(2,1)S(1)}, bf16[16,2,64,64]{3,2,1,0:T(8,128)(2,1)S(1)}, bf16[16,2,128,384]{3,2,1,0:T(...) custom-call(f32[16]{0:T(128)S(1)} %broadcast_select_fusion.9.refs_0_, ...), custom_call_target="tpu_custom_call" | custom-call | tf_op jit(solution)/shard_map/pallas_call | solution.py:1260
  216.4 10.8 %shard_map.359 = (f32[1024,512]{1,0:T(8,128)S(1)}, bf16[1024,512]{1,0:T(8,128)(2,1)S(1)}, bf16[1024,2048]{1,0:T(8,128)(2,1)}) custom-call(bf16[1040,2048]{1,0:T(8,128)(2,1)} %get-tuple-element.72.x_ref.refs_17_.refs_0_, bf16[2048,512]{1,0:T(8,128)(2,1)} %bitcast.93, bf16[2048,512]{1,0:T(8,128)(2,1)} %bitcast.98, f32[1024,512]{1,0:T(8,128)} %get-tuple-element.77.o_ref, ...), custom_call_target="tpu_custom_call" | custom-call | tf_op jit(solution)/shard_map/pallas_call | solution.py:1488
  227.2 1.3 copy-done.15
  229.6 2.2 copy-done.9
  231.7 22.9 %shard_map.360 = f32[128,2048]{1,0:T(8,128)S(1)} custom-call(bf16[8,128,2048]{2,1,0:T(8,128)(2,1)S(1)} %bitcast.83), custom_call_target="tpu_custom_call" | custom-call | tf_op jit(solution)/shard_map/pallas_call | solution.py:898
  255.7 1.4 multiply_reduce_fusion.2
  259.0 138.2 %shard_map.361 = (f32[128,2048]{1,0:T(8,128)}, bf16[8,128,2048]{2,1,0:T(8,128)(2,1)}, bf16[688,2048]{1,0:T(8,128)(2,1)}, bf16[688,2048]{1,0:T(8,128)(2,1)}, bf16[688,2048]{1,0:T(8,128)(2,1)}) custom-call(bf16[128,2048]{1,0:T(8,128)(2,1)} %multiply_convert_fusion.own_ref, bf16[8,128,2048]{2,1,0:T(8,128)(2,1)} %get-tuple-element.84.cot_hbm, ...), custom_call_target="tpu_custom_call" | custom-call | tf_op jit(solution)/shard_map/pallas_call | solution.py:1720
  397.3 1.6 multiply_reduce_fusion
  399.2 22.2 %shard_map.362 = bf16[8,128,2048]{2,1,0:T(8,128)(2,1)S(1)} custom-call(bf16[128,2048]{1,0:T(8,128)(2,1)S(1)} %fusion.22.x_ref), custom_call_target="tpu_custom_call" | custom-call | tf_op jit(solution)/shard_map/pallas_call | solution.py:958
  421.5 3.7 fusion.28.gm_ref
  425.2 5.6 shard_map.363
  433.5 157.2 %shard_map.364 = (bf16[1040,1024]{1,0:T(8,128)(2,1)}, f32[1024,4]{1,0:T(8,128)}, f32[4,1024]{1,0:T(4,128)}, f32[8,2]{1,0:T(8,128)}, f32[256,512]{1,0:T(8,128)}, ...) custom-call(f32[16]{0:T(128)} %copy-done.32, ...), custom_call_target="tpu_custom_call" | custom-call | tf_op jit(solution)/shard_map/pallas_call | solution.py:1348
  590.7 1.4 broadcast_select_fusion.1
  592.1 1.1 pad_maximum_fusion.2
  593.3 1.1 pad_maximum_fusion.1
  596.0 18.5 %shard_map.365 = (bf16[1024,2048]{1,0:T(8,128)(2,1)}, bf16[16,2048]{1,0:T(8,128)(2,1)}, f32[1,2048]{1,0:T(1,128)}) custom-call(s32[1]{0:T(128)} %bitcast.side_ref, bf16[512,2048]{1,0:T(8,128)(2,1)} %own_ref.3, bf16[512,2048]{1,0:T(8,128)(2,1)} %bitcast.81, bf16[16,2048]{1,0:T(8,128)(2,1)} %copy-done.22, f32[1,2048]{1,0:T(1,128)} %bitcast.86, ...), custom_call_target="tpu_custom_call" | custom-call | tf_op jit(solution)/shard_map/pallas_call | solution.py:1457
  615.8 1.7 pad.27.refs_4_
  617.5 2.9 fusion.2
  621.1 101.7 %shard_map.366 = (f32[256,1024]{1,0:T(8,128)}, f32[256,1024]{1,0:T(8,128)}, f32[16,256]{1,0:T(8,128)}, f32[128,2048]{1,0:T(8,128)}, f32[16,2048]{1,0:T(8,128)}, /*index=5*/f32[8,80,128]{2,1,0:T(8,128)}) custom-call(bf16[1040,2048]{1,0:T(8,128)(2,1)} %get-tuple-element.72.x_ref.refs_17_.refs_0_, bf16[1040,1024]{1,0:T(8,128)(2,1)} %get-tuple-element.96.gm_ref.refs_1_, ...), custom_call_target="tpu_custom_call" | custom-call | tf_op jit(solution)/shard_map/pallas_call | solution.py:1156
  722.8 1.4 slice_select_fusion.1
  724.3 1.1 pad_maximum_fusion
  727.3 1.6 fusion.21
  734.3 1.1 copy.90
  735.4 1.1 copy.91
  736.5 1.1 copy.92
  (181 shorter events, 30.1 us)
Async XLA Ops:
  0.7 99.7 %copy-start = (f32[4,1024]{1,0:T(4,128)S(1)}, f32[4,1024]{1,0:T(4,128)}, u32[]{:S(2)}) copy-start(f32[4,1024]{1,0:T(4,128)} %param.31) | copy-start | bytes 49156
  0.7 4.3 copy-start.58
  0.7 4.3 copy-start.57
  3.8 81.9 %copy-start.2 = (bf16[512,2048]{1,0:T(8,128)(2,1)S(1)}, bf16[512,2048]{1,0:T(8,128)(2,1)}, u32[]{:S(2)}) copy-start(bf16[512,2048]{1,0:T(8,128)(2,1)} %own_ref.3) | copy-start | bytes 6291460
  3.8 81.9 %copy-start.27 = (f32[2048]{0:T(1024)S(1)}, f32[2048]{0:T(1024)}, u32[]{:S(2)}) copy-start(f32[2048]{0:T(1024)} %param.22) | copy-start | bytes 24580
  85.7 13.0 %copy-start.22 = (bf16[16,2048]{1,0:T(8,128)(2,1)}, bf16[16,2048]{1,0:T(8,128)(2,1)S(1)}, u32[]{:S(2)}) copy-start(bf16[16,2048]{1,0:T(8,128)(2,1)S(1)} %broadcast_select_fusion.4.rim_ref) | copy-start | bytes 196612
  87.3 12.1 %copy-start.49 = (bf16[256,1024]{1,0:T(8,128)(2,1)S(1)}, bf16[256,1024]{1,0:T(8,128)(2,1)}, u32[]{:S(2)}) copy-start(bf16[256,1024]{1,0:T(8,128)(2,1)} %param.35) | copy-start | bytes 1572868
  87.3 12.1 %copy-start.50 = (bf16[256,1024]{1,0:T(8,128)(2,1)S(1)}, bf16[256,1024]{1,0:T(8,128)(2,1)}, u32[]{:S(2)}) copy-start(bf16[256,1024]{1,0:T(8,128)(2,1)} %param.26) | copy-start | bytes 1572868
  87.3 13.0 %copy-start.55 = (f32[4,512]{1,0:T(4,128)S(1)}, f32[4,512]{1,0:T(4,128)}, u32[]{:S(2)}) copy-start(f32[4,512]{1,0:T(4,128)} %param.30) | copy-start | bytes 24580
  87.3 13.0 %copy-start.56 = (f32[4,512]{1,0:T(4,128)S(1)}, f32[4,512]{1,0:T(4,128)}, u32[]{:S(2)}) copy-start(f32[4,512]{1,0:T(4,128)} %param.29) | copy-start | bytes 24580
  87.3 13.1 %copy-start.59 = (f32[4]{0:T(128)S(1)}, f32[4]{0:T(128)}, u32[]{:S(2)}) copy-start(f32[4]{0:T(128)} %param.33) | copy-start | bytes 52
  87.3 13.1 %copy-start.60 = (f32[4]{0:T(128)S(1)}, f32[4]{0:T(128)}, u32[]{:S(2)}) copy-start(f32[4]{0:T(128)} %param.32) | copy-start | bytes 52
  87.3 13.7 %copy-start.61 = (s32[9]{0:T(128)S(1)}, s32[9]{0:T(128)}, u32[]{:S(2)}) copy-start(s32[9]{0:T(128)} %param.40) | copy-start | bytes 112
  100.4 115.2 %copy-start.26 = (f32[4,1024]{1,0:T(4,128)}, f32[4,1024]{1,0:T(4,128)S(1)}, u32[]{:S(2)}) copy-start(f32[4,1024]{1,0:T(4,128)S(1)} %pad_maximum_fusion.9.refs_3_.refs_4_) | copy-start | bytes 49156
  101.6 323.6 %copy-start.4 = (f32[1024,1]{1,0:T(8,128)}, f32[1024,1]{1,0:T(8,128)S(1)}, u32[]{:S(2)}) copy-start(f32[1024,1]{1,0:T(8,128)S(1)} %copy.56.refs_5_.live_ref.refs_6_) | copy-start | bytes 12292
  107.1 108.5 %copy-start.32 = (f32[16]{0:T(128)}, f32[16]{0:T(128)S(1)}, u32[]{:S(2)}) copy-start(f32[16]{0:T(128)S(1)} %broadcast_select_fusion.9.refs_0_) | copy-start | bytes 196
  107.1 109.3 %copy-start.30 = (f32[256]{0:T(256)S(1)}, f32[256]{0:T(256)}, u32[]{:S(2)}) copy-start(f32[256]{0:T(256)} %param.34) | copy-start | bytes 3076
  216.4 10.9 %copy-start.13 = (bf16[1024,256]{1,0:T(8,128)(2,1)}, bf16[1024,256]{1,0:T(8,128)(2,1)S(1)}, u32[]{:S(2)}) copy-start(bf16[1024,256]{1,0:T(8,128)(2,1)S(1)} %get-tuple-element.78.e_ref) | copy-start | bytes 1572868
  216.4 10.9 %copy-start.23 = (bf16[16,2,64,64]{3,2,1,0:T(8,128)(2,1)}, bf16[16,2,64,64]{3,2,1,0:T(8,128)(2,1)S(1)}, u32[]{:S(2)}) copy-start(bf16[16,2,64,64]{3,2,1,0:T(8,128)(2,1)S(1)} %get-tuple-element.81.refs_9_) | copy-start | bytes 786436
  216.4 208.8 %copy-start.16 = (bf16[2,128,256]{2,1,0:T(8,128)(2,1)}, bf16[2,128,256]{2,1,0:T(8,128)(2,1)S(1)}, u32[]{:S(2)}) copy-start(bf16[2,128,256]{2,1,0:T(8,128)(2,1)S(1)} %get-tuple-element.79.s_ref.refs_12_) | copy-start | bytes 393220
  231.7 26.3 %copy-start.52 = (f32[2048]{0:T(1024)S(1)}, f32[2048]{0:T(1024)}, u32[]{:S(2)}) copy-start(f32[2048]{0:T(1024)} %param.36) | copy-start | bytes 24580
  259.0 138.2 %copy-start.34 = (f32[128,2048]{1,0:T(8,128)S(1)}, f32[128,2048]{1,0:T(8,128)}, u32[]{:S(2)}) copy-start(f32[128,2048]{1,0:T(8,128)} %copy-done.33) | copy-start | bytes 3145732
  399.2 22.3 %copy-start.39 = (bf16[8,256,512]{2,1,0:T(8,128)(2,1)S(1)}, bf16[8,256,512]{2,1,0:T(8,128)(2,1)}, u32[]{:S(2)}) copy-start(bf16[8,256,512]{2,1,0:T(8,128)(2,1)} %get-tuple-element.76) | copy-start | bytes 6291460
  421.4 3.7 copy-start.3
  421.5 3.7 copy-start.6
  421.5 3.7 copy-start.14
  421.5 3.7 copy-start.31
  592.1 3.1 copy-start.38
  727.3 6.5 copy-start.54
  727.3 7.1 copy-start.42
  728.9 6.5 copy-start.41
  734.3 3.3 copy-start.1
  (30 other events, 49.5 us)

commit v5 on v4

--- a/solution.py
+++ b/solution.py
@@ -1134,7 +1134,7 @@
     return [(group, event) for _, _, _, group, event in sorted(found, key=lambda e: e[:3])]
 
 
-def line_scatter(halves, pairs, cubes, small, call_id, chunks=4):
+def line_scatter(halves, pairs, cubes, small, call_id, chunks=2):
     places = lax.axis_size("wide") // 2
     halves, operands = product_terms(halves, places)
     half_cuts = [row_cuts(term.shape[2], chunks) for term in halves]

time: 746 us -> 741 us (level)
  no operation moved by 1% of the time
where the time goes in v5:
time: 741 us; the launch traced here: 733 us
  Pallas kernels  669 us (90%)
  local copies, waits for them, and re-layouts  35.1 us (5%)
  other arithmetic  19.9 us (3%)
    pallas_call x1, Pallas kernels, backward_scatter(): pl.pallas_call(functools.partial(backward_scatter_kernel, heads, nb, plac...  157 us
    pallas_call x1, Pallas kernels, feed(): pl.pallas_call(functools.partial(feed_kernel, places, chunks), in_specs=[...  138 us
    pallas_call x1, Pallas kernels, forward_gather(): pl.pallas_call(functools.partial(forward_gather_kernel, heads, nb, count...  108 us
    pallas_call x1, Pallas kernels, line_scatter(): pl.pallas_call(functools.partial(scatter_kernel, places, half_cuts, pair_...  96.2 us
    pallas_call x1, Pallas kernels, line_gather(): pl.pallas_call(functools.partial(gather_kernel, count // 2, cuts, halved,...  77.7 us
    pallas_call x1, Pallas kernels, cube_scatter(): pl.pallas_call(cube_scatter_kernel, out_shape=jax.ShapeDtypeStruct(value....  22.9 us
    pallas_call x1, Pallas kernels, cube_gather(): pl.pallas_call(cube_gather_kernel, out_shape=jax.ShapeDtypeStruct((8,) +...  22.2 us
    unnamed x133, local copies, waits for them, and re-layouts  21 us

profile of v5, /device:TPU:10, one launch (start us, length us, event | category | flops | bytes accessed | tf_op | source)
XLA Modules:
  0.0 732.5 jit_solution(3614021941955328340)
XLA Ops:
  0.7 1.1 constant_dynamic-slice_fusion.9
  2.8 1.0 constant_dynamic-slice_fusion.10
  3.8 1.1 pad_maximum_fusion.3
  5.6 77.7 %shard_map.356 = (bf16[8,256,1024]{2,1,0:T(8,128)(2,1)}, bf16[8,16,256]{2,1,0:T(8,128)(2,1)}, bf16[4,128,2048]{2,1,0:T(8,128)(2,1)}, bf16[16,2048]{1,0:T(8,128)(2,1)}) custom-call(bf16[256,1024]{1,0:T(8,128)(2,1)} %get-tuple-element.166.refs_0_, bf16[16,256]{1,0:T(8,128)(2,1)} %fusion.17.refs_1_, bf16[256,1024]{1,0:T(8,128)(2,1)} %get-tuple-element.167.refs_2_, ...), custom_call_target="tpu_custom_call" | custom-call | tf_op jit(solution)/shard_map/pallas_call | solution.py:582
  85.7 1.6 copy-done.5
  87.4 11.3 %shard_map.357 = (bf16[1040,2048]{1,0:T(8,128)(2,1)}, bf16[1040,1024]{1,0:T(8,128)(2,1)}, f32[1024,16]{1,0:T(8,128)S(1)}) custom-call(s32[1]{0:T(128)} %bitcast.side_ref, bf16[512,2048]{1,0:T(8,128)(2,1)S(1)} %copy-done.2, bf16[512,2048]{1,0:T(8,128)(2,1)S(1)} %bitcast.82, bf16[16,2048]{1,0:T(8,128)(2,1)S(1)} %broadcast_select_fusion.4.rim_ref, ...), custom_call_target="tpu_custom_call" | custom-call | tf_op jit(solution)/shard_map/pallas_call | solution.py:1415
  101.9 1.0 copy-done.12
  107.1 108.5 %shard_map.358 = (f32[1024,512]{1,0:T(8,128)}, bf16[1024,256]{1,0:T(8,128)(2,1)S(1)}, bf16[16,2,64,64]{3,2,1,0:T(8,128)(2,1)S(1)}, bf16[16,2,128,384]{3,2,1,0:T(...) custom-call(f32[16]{0:T(128)S(1)} %broadcast_select_fusion.9.refs_0_, ...), custom_call_target="tpu_custom_call" | custom-call | tf_op jit(solution)/shard_map/pallas_call | solution.py:1260
  216.4 10.8 %shard_map.359 = (f32[1024,512]{1,0:T(8,128)S(1)}, bf16[1024,512]{1,0:T(8,128)(2,1)S(1)}, bf16[1024,2048]{1,0:T(8,128)(2,1)}) custom-call(bf16[1040,2048]{1,0:T(8,128)(2,1)} %get-tuple-element.72.x_ref.refs_17_.refs_0_, bf16[2048,512]{1,0:T(8,128)(2,1)} %bitcast.93, bf16[2048,512]{1,0:T(8,128)(2,1)} %bitcast.98, f32[1024,512]{1,0:T(8,128)} %get-tuple-element.77.o_ref, ...), custom_call_target="tpu_custom_call" | custom-call | tf_op jit(solution)/shard_map/pallas_call | solution.py:1488
  227.2 1.3 copy-done.15
  229.6 2.2 copy-done.9
  231.7 22.9 %shard_map.360 = f32[128,2048]{1,0:T(8,128)S(1)} custom-call(bf16[8,128,2048]{2,1,0:T(8,128)(2,1)S(1)} %bitcast.83), custom_call_target="tpu_custom_call" | custom-call | tf_op jit(solution)/shard_map/pallas_call | solution.py:898
  255.7 1.4 multiply_reduce_fusion.2
  259.0 138.2 %shard_map.361 = (f32[128,2048]{1,0:T(8,128)}, bf16[8,128,2048]{2,1,0:T(8,128)(2,1)}, bf16[688,2048]{1,0:T(8,128)(2,1)}, bf16[688,2048]{1,0:T(8,128)(2,1)}, bf16[688,2048]{1,0:T(8,128)(2,1)}) custom-call(bf16[128,2048]{1,0:T(8,128)(2,1)} %multiply_convert_fusion.own_ref, bf16[8,128,2048]{2,1,0:T(8,128)(2,1)} %get-tuple-element.84.cot_hbm, ...), custom_call_target="tpu_custom_call" | custom-call | tf_op jit(solution)/shard_map/pallas_call | solution.py:1720
  397.3 1.6 multiply_reduce_fusion
  399.2 22.2 %shard_map.362 = bf16[8,128,2048]{2,1,0:T(8,128)(2,1)S(1)} custom-call(bf16[128,2048]{1,0:T(8,128)(2,1)S(1)} %fusion.22.x_ref), custom_call_target="tpu_custom_call" | custom-call | tf_op jit(solution)/shard_map/pallas_call | solution.py:958
  421.5 3.7 fusion.28.gm_ref
  425.2 5.6 shard_map.363
  433.5 157.2 %shard_map.364 = (bf16[1040,1024]{1,0:T(8,128)(2,1)}, f32[1024,4]{1,0:T(8,128)}, f32[4,1024]{1,0:T(4,128)}, f32[8,2]{1,0:T(8,128)}, f32[256,512]{1,0:T(8,128)}, ...) custom-call(f32[16]{0:T(128)} %copy-done.32, ...), custom_call_target="tpu_custom_call" | custom-call | tf_op jit(solution)/shard_map/pallas_call | solution.py:1348
  590.7 1.4 broadcast_select_fusion.1
  592.1 1.1 pad_maximum_fusion.2
  593.3 1.1 pad_maximum_fusion.1
  596.0 18.5 %shard_map.365 = (bf16[1024,2048]{1,0:T(8,128)(2,1)}, bf16[16,2048]{1,0:T(8,128)(2,1)}, f32[1,2048]{1,0:T(1,128)}) custom-call(s32[1]{0:T(128)} %bitcast.side_ref, bf16[512,2048]{1,0:T(8,128)(2,1)} %own_ref.3, bf16[512,2048]{1,0:T(8,128)(2,1)} %bitcast.81, bf16[16,2048]{1,0:T(8,128)(2,1)} %copy-done.22, f32[1,2048]{1,0:T(1,128)} %bitcast.86, ...), custom_call_target="tpu_custom_call" | custom-call | tf_op jit(solution)/shard_map/pallas_call | solution.py:1457
  615.8 1.7 pad.27.refs_4_
  617.5 2.9 fusion.2
  621.1 96.2 %shard_map.366 = (f32[256,1024]{1,0:T(8,128)}, f32[256,1024]{1,0:T(8,128)}, f32[16,256]{1,0:T(8,128)}, f32[128,2048]{1,0:T(8,128)}, f32[16,2048]{1,0:T(8,128)}, /*index=5*/f32[8,80,128]{2,1,0:T(8,128)}) custom-call(bf16[1040,2048]{1,0:T(8,128)(2,1)} %get-tuple-element.72.x_ref.refs_17_.refs_0_, bf16[1040,1024]{1,0:T(8,128)(2,1)} %get-tuple-element.96.gm_ref.refs_1_, ...), custom_call_target="tpu_custom_call" | custom-call | tf_op jit(solution)/shard_map/pallas_call | solution.py:1156
  717.3 1.4 slice_select_fusion.1
  718.8 1.1 pad_maximum_fusion
  721.8 1.6 fusion.21
  728.8 1.1 copy.90
  729.9 1.1 copy.91
  731.0 1.1 copy.92
  (181 shorter events, 30.1 us)
Async XLA Ops:
  0.7 99.7 %copy-start = (f32[4,1024]{1,0:T(4,128)S(1)}, f32[4,1024]{1,0:T(4,128)}, u32[]{:S(2)}) copy-start(f32[4,1024]{1,0:T(4,128)} %param.31) | copy-start | bytes 49156
  0.7 4.3 copy-start.58
  0.7 4.3 copy-start.57
  3.8 81.9 %copy-start.2 = (bf16[512,2048]{1,0:T(8,128)(2,1)S(1)}, bf16[512,2048]{1,0:T(8,128)(2,1)}, u32[]{:S(2)}) copy-start(bf16[512,2048]{1,0:T(8,128)(2,1)} %own_ref.3) | copy-start | bytes 6291460
  3.8 81.9 %copy-start.27 = (f32[2048]{0:T(1024)S(1)}, f32[2048]{0:T(1024)}, u32[]{:S(2)}) copy-start(f32[2048]{0:T(1024)} %param.22) | copy-start | bytes 24580
  85.7 13.0 %copy-start.22 = (bf16[16,2048]{1,0:T(8,128)(2,1)}, bf16[16,2048]{1,0:T(8,128)(2,1)S(1)}, u32[]{:S(2)}) copy-start(bf16[16,2048]{1,0:T(8,128)(2,1)S(1)} %broadcast_select_fusion.4.rim_ref) | copy-start | bytes 196612
  87.3 12.1 %copy-start.49 = (bf16[256,1024]{1,0:T(8,128)(2,1)S(1)}, bf16[256,1024]{1,0:T(8,128)(2,1)}, u32[]{:S(2)}) copy-start(bf16[256,1024]{1,0:T(8,128)(2,1)} %param.35) | copy-start | bytes 1572868
  87.3 12.1 %copy-start.50 = (bf16[256,1024]{1,0:T(8,128)(2,1)S(1)}, bf16[256,1024]{1,0:T(8,128)(2,1)}, u32[]{:S(2)}) copy-start(bf16[256,1024]{1,0:T(8,128)(2,1)} %param.26) | copy-start | bytes 1572868
  87.3 13.0 %copy-start.55 = (f32[4,512]{1,0:T(4,128)S(1)}, f32[4,512]{1,0:T(4,128)}, u32[]{:S(2)}) copy-start(f32[4,512]{1,0:T(4,128)} %param.30) | copy-start | bytes 24580
  87.3 13.0 %copy-start.56 = (f32[4,512]{1,0:T(4,128)S(1)}, f32[4,512]{1,0:T(4,128)}, u32[]{:S(2)}) copy-start(f32[4,512]{1,0:T(4,128)} %param.29) | copy-start | bytes 24580
  87.3 13.1 %copy-start.59 = (f32[4]{0:T(128)S(1)}, f32[4]{0:T(128)}, u32[]{:S(2)}) copy-start(f32[4]{0:T(128)} %param.33) | copy-start | bytes 52
  87.3 13.1 %copy-start.60 = (f32[4]{0:T(128)S(1)}, f32[4]{0:T(128)}, u32[]{:S(2)}) copy-start(f32[4]{0:T(128)} %param.32) | copy-start | bytes 52
  87.3 13.7 %copy-start.61 = (s32[9]{0:T(128)S(1)}, s32[9]{0:T(128)}, u32[]{:S(2)}) copy-start(s32[9]{0:T(128)} %param.40) | copy-start | bytes 112
  100.4 115.2 %copy-start.26 = (f32[4,1024]{1,0:T(4,128)}, f32[4,1024]{1,0:T(4,128)S(1)}, u32[]{:S(2)}) copy-start(f32[4,1024]{1,0:T(4,128)S(1)} %pad_maximum_fusion.9.refs_3_.refs_4_) | copy-start | bytes 49156
  101.6 323.6 %copy-start.4 = (f32[1024,1]{1,0:T(8,128)}, f32[1024,1]{1,0:T(8,128)S(1)}, u32[]{:S(2)}) copy-start(f32[1024,1]{1,0:T(8,128)S(1)} %copy.56.refs_5_.live_ref.refs_6_) | copy-start | bytes 12292
  107.1 108.5 %copy-start.32 = (f32[16]{0:T(128)}, f32[16]{0:T(128)S(1)}, u32[]{:S(2)}) copy-start(f32[16]{0:T(128)S(1)} %broadcast_select_fusion.9.refs_0_) | copy-start | bytes 196
  107.1 109.3 %copy-start.30 = (f32[256]{0:T(256)S(1)}, f32[256]{0:T(256)}, u32[]{:S(2)}) copy-start(f32[256]{0:T(256)} %param.34) | copy-start | bytes 3076
  216.4 10.9 %copy-start.13 = (bf16[1024,256]{1,0:T(8,128)(2,1)}, bf16[1024,256]{1,0:T(8,128)(2,1)S(1)}, u32[]{:S(2)}) copy-start(bf16[1024,256]{1,0:T(8,128)(2,1)S(1)} %get-tuple-element.78.e_ref) | copy-start | bytes 1572868
  216.4 10.9 %copy-start.23 = (bf16[16,2,64,64]{3,2,1,0:T(8,128)(2,1)}, bf16[16,2,64,64]{3,2,1,0:T(8,128)(2,1)S(1)}, u32[]{:S(2)}) copy-start(bf16[16,2,64,64]{3,2,1,0:T(8,128)(2,1)S(1)} %get-tuple-element.81.refs_9_) | copy-start | bytes 786436
  216.4 208.8 %copy-start.16 = (bf16[2,128,256]{2,1,0:T(8,128)(2,1)}, bf16[2,128,256]{2,1,0:T(8,128)(2,1)S(1)}, u32[]{:S(2)}) copy-start(bf16[2,128,256]{2,1,0:T(8,128)(2,1)S(1)} %get-tuple-element.79.s_ref.refs_12_) | copy-start | bytes 393220
  231.7 26.3 %copy-start.52 = (f32[2048]{0:T(1024)S(1)}, f32[2048]{0:T(1024)}, u32[]{:S(2)}) copy-start(f32[2048]{0:T(1024)} %param.36) | copy-start | bytes 24580
  259.0 138.2 %copy-start.34 = (f32[128,2048]{1,0:T(8,128)S(1)}, f32[128,2048]{1,0:T(8,128)}, u32[]{:S(2)}) copy-start(f32[128,2048]{1,0:T(8,128)} %copy-done.33) | copy-start | bytes 3145732
  399.2 22.3 %copy-start.39 = (bf16[8,256,512]{2,1,0:T(8,128)(2,1)S(1)}, bf16[8,256,512]{2,1,0:T(8,128)(2,1)}, u32[]{:S(2)}) copy-start(bf16[8,256,512]{2,1,0:T(8,128)(2,1)} %get-tuple-element.76) | copy-start | bytes 6291460
  421.4 3.7 copy-start.3
  421.5 3.7 copy-start.6
  421.5 3.7 copy-start.14
  421.5 3.7 copy-start.31
  592.1 3.1 copy-start.38
  721.8 6.5 copy-start.54
  721.8 7.1 copy-start.42
  723.4 6.5 copy-start.41
  728.8 3.3 copy-start.1
  (30 other events, 49.5 us)
